TPU v7x, 256 devices: a whole 4x4x8 slice. The times are simulated.
256 devices in a mesh: seq: 64 (over z, y_lo, x), head: 4 (over y_hi, core).
Axes of the slice: x: 4, y: 4 (y_hi: 2, y_lo: 2; y = y_hi * 2 + y_lo), z: 8, core: 2. Of those that a mesh axis runs over, the one named last changes fastest.
Arguments:
- features: bfloat16 [8192, 4096], P('seq', 'head'), may hold values from -6 to 6
- queries: bfloat16 [8192, 1536], P('seq', 'head'), may hold values from -200 to 200
- keys: bfloat16 [8192, 1536], P('seq', 'head'), may hold values from -6 to 6
- router: bfloat16 [192, 4096], P('head'), may hold values from -0.09375 to 0.09375
- value_experts: bfloat16 [24, 8, 2048, 128], P('head', None, 'seq'), may hold values from -0.09375 to 0.09375
- output_experts: bfloat16 [24, 8, 2048, 128], P('head', None, 'seq'), may hold values from -3 to 3
- expert_ids: int32 [64, 24, 2], P(None, 'head'), may hold values from 0 to 7, all different within a row
Outputs:
- mixed: bfloat16 [8192, 4096], P('seq', 'head')
All inputs are finite; a program needn't handle non-finite values.
Results may differ from a plain program's by a relative error of at most 0.022.
Values may be sent and summed in bfloat16 or wider, within the bound.
No kernel may reach another device: no remote copies, remote signals or barrier semaphores. Data moves between devices by JAX's collectives and lax.ppermute only.
A program may use at most 128 MiB of HBM per device.

v0:
```python
import math

import jax
import jax.numpy as jnp
from jax import lax
from jax.sharding import PartitionSpec as P

TOP = 2
BLK = 128


masked_score = -1e30


def gated_output(gate_blocks, attended_blocks, out_weights):
    scaled = gate_blocks[..., None] * jnp.transpose(attended_blocks, (1, 2, 0, 3))[
        :, :, :, None, :
    ].astype(jnp.float32)
    upper = scaled.astype(jnp.bfloat16)
    lower = (scaled - upper.astype(jnp.float32)).astype(jnp.bfloat16)
    first = jnp.einsum("bthjk,hbjck->btc", upper, out_weights, preferred_element_type=jnp.float32)
    second = jnp.einsum("bthjk,hbjck->btc", lower, out_weights, preferred_element_type=jnp.float32)
    return first + second


def body(features, queries, keys, router, value_experts, output_experts, expert_ids):
    seq_count = lax.axis_size("seq")
    seq_index = lax.axis_index("seq")
    tok_rows = features.shape[0]
    heads_dev = value_experts.shape[0]
    experts = value_experts.shape[1]
    head_size = value_experts.shape[3] // 2
    blocks_dev = tok_rows // BLK
    score_scale = 1.0 / math.sqrt(head_size)
    full_x = lax.all_gather(features, "head", axis=1, tiled=True)
    model_width = full_x.shape[1]
    my_ids = lax.dynamic_slice_in_dim(expert_ids, seq_index * blocks_dev, blocks_dev, 0)
    token_ids = jnp.repeat(my_ids, BLK, axis=0)
    logits = jnp.einsum("td,ed->te", full_x, router, preferred_element_type=jnp.float32).reshape(
        tok_rows, heads_dev, experts
    )
    gates = jax.nn.sigmoid(jnp.take_along_axis(logits, token_ids, axis=2)).astype(jnp.bfloat16)
    gate_blocks = gates.astype(jnp.float32).reshape(blocks_dev, BLK, heads_dev, TOP)
    x_blocks = full_x.reshape(blocks_dev, BLK, model_width)
    slot_order = expert_ids.reshape(seq_count, blocks_dev, heads_dev, TOP).transpose(2, 1, 3, 0)
    slot_order = slot_order.reshape(heads_dev, blocks_dev * TOP * seq_count)

    def select_rows(expert_table):
        picked = jnp.take_along_axis(expert_table, slot_order[:, :, None, None], axis=1)
        return picked.reshape(
            heads_dev, blocks_dev * TOP, seq_count * expert_table.shape[2], expert_table.shape[3]
        )

    weights = lax.all_to_all(
        select_rows(value_experts), "seq", split_axis=2, concat_axis=2, tiled=True
    )
    shaped = weights.reshape(weights.shape[0], blocks_dev, TOP, model_width, head_size)
    raw_values = jnp.einsum(
        "btd,hbjdk->hbjtk", x_blocks, shaped, preferred_element_type=jnp.float32
    )
    out_rows = lax.all_to_all(
        select_rows(output_experts), "seq", split_axis=2, concat_axis=2, tiled=True
    )
    values = jnp.einsum("bthj,hbjtk->bthk", gate_blocks, raw_values)
    values = values.reshape(tok_rows, heads_dev * head_size).astype(jnp.bfloat16)
    own_position = seq_index * tok_rows + jnp.arange(tok_rows, dtype=jnp.int32)
    query_rows = queries.reshape(tok_rows, heads_dev, head_size)

    def attend(carried, query_part, query_pos, key_part, value_part, key_pos):
        top_score, denominator, weighted = carried
        scores = (
            jnp.einsum("thk,uhk->htu", query_part, key_part, preferred_element_type=jnp.float32)
            * score_scale
        )
        allowed = key_pos[None, None, :] <= query_pos[None, :, None]
        scores = jnp.where(allowed, scores, masked_score)
        new_top = jnp.maximum(top_score, jnp.max(scores, axis=-1))
        weights = jnp.where(allowed, jnp.exp(scores - new_top[..., None]), 0.0)
        denominator = jnp.sum(weights, axis=-1)
        update = jnp.einsum(
            "htu,uhk->htk",
            weights.astype(jnp.bfloat16),
            value_part,
            preferred_element_type=jnp.float32,
        )
        weighted = update
        return (new_top, denominator, weighted)

    initial = (
        jnp.full((heads_dev, tok_rows), masked_score, jnp.float32),
        jnp.zeros((heads_dev, tok_rows), jnp.float32),
        jnp.zeros((heads_dev, tok_rows, head_size), jnp.float32),
    )
    key_part = lax.all_gather(keys, "seq", axis=0, tiled=True).reshape(-1, heads_dev, head_size)
    value_part = lax.all_gather(values, "seq", axis=0, tiled=True).reshape(-1, heads_dev, head_size)
    key_pos = jnp.arange(key_part.shape[0], dtype=jnp.int32)
    carried = (initial[0], initial[1], initial[2])
    query_part = query_rows
    query_pos = own_position
    carried = lax.cond(
        jnp.int32(0) <= query_pos[-1],
        lambda state_in: attend(state_in, query_part, query_pos, key_part, value_part, key_pos),
        lambda state_in: state_in,
        carried,
    )
    pieces_out = [carried]
    top_score, denominator, weighted = tuple(
        (jnp.concatenate([member[which] for member in pieces_out], axis=1) for which in range(3))
    )
    attended = (weighted / denominator[..., None]).astype(jnp.bfloat16)
    attended_blocks = attended.reshape(heads_dev, blocks_dev, BLK, head_size)
    out_weights = out_rows.reshape(heads_dev, blocks_dev, TOP, model_width, head_size)
    terms = gated_output(gate_blocks, attended_blocks, out_weights).reshape(tok_rows, model_width)
    return lax.psum_scatter(terms.astype(jnp.bfloat16), "head", scatter_dimension=1, tiled=True)


def solution(mesh):
    return jax.shard_map(
        body,
        mesh=mesh,
        in_specs=(
            P("seq", "head"),
            P("seq", "head"),
            P("seq", "head"),
            P("head", None),
            P("head", None, "seq", None),
            P("head", None, "seq", None),
            P(None, "head", None),
        ),
        out_specs=P("seq", "head"),
        check_vma=False,
    )
```

profile of v0, /device:TPU:1, one launch (start us, length us, event | category | flops | bytes accessed | tf_op | source)
XLA Modules:
  0.0 834.3 jit_solution(7211121408797184545)
XLA Ops:
  6.5 0.0 copy-start
  6.5 0.0 all-gather.4.cloned.1.call-start
  6.5 0.7 all-gather.4.cloned.1.call-update
  7.3 0.8 broadcast_in_dim_reshape.2
  8.1 0.0 copy-done
  8.1 6.8 gather_fusion.1
  14.9 0.0 copy-done.2
  14.9 6.8 gather_fusion.2
  21.7 8.6 %broadcast_select_fusion.1 = (bf16[6,128,32,128]{3,2,1,0:T(8,128)(2,1)S(1)}, bf16[6,128,32,128]{3,2,1,0:T(8,128)(2,1)}) fusion(bf16[6,128,32,128]{3,2,1,0:T(8,128)(2,1)} %bitcast.81, pred[6,128]{1,0:T(8,128)(4,1)S(1)} %bitcast.89, bf16[6,128,32,128]{3,2,1,0:T(8,128)(2,1)} %bitcast.82), kind=kLoop, calls=%fused_computation.16 | loop fusion | flops 6291456 | bytes 25166592 | tf_op jit(solution)/shard_map/jit(take_along_axis)/select_n | solution.py:49
  30.3 46.5 %copy.86 = bf16[6,2,2048,128]{3,1,0,2:T(2,128)(2,1)} copy(bf16[6,2,2048,128]{3,2,1,0:T(8,128)(2,1)S(1)} %bitcast.83) | data formatting | bytes 12582912 | tf_op jit(solution)/shard_map/reshape | solution.py:50
  76.8 13.9 %all-to-all-start = ((bf16[6,2,2048,128]{3,1,0,2:T(2,128)(2,1)}), bf16[6,2,2048,128]{3,1,0,2:T(2,128)(2,1)}, u32[]{:S(2)}, u32[]{:S(2)}) async-start(bf16[6,2,2048,128]{3,1,0,2:T(2,128)(2,1)} %copy.86), calls=%async_computation | async-start | bytes 12582912 | tf_op jit(solution)/shard_map/all_to_all | solution.py:54
  90.7 0.0 all-gather.6.cloned.1.call-start
  90.8 0.0 copy-done.5
  90.8 0.8 copy.85
  91.5 0.0 all-gather.6.cloned.1.call-update
  91.6 0.0 copy-done.11
  91.6 0.1 constant_dynamic-slice_fusion
  91.6 0.1 copy.76
  91.7 0.1 copy.78
  91.8 0.1 copy.79
  91.9 0.1 copy.77
  92.1 0.1 shift-left_or_fusion
  92.2 0.3 copy-done.7
  92.4 0.1 copy-done.9
  92.5 0.3 copy.83
  92.8 0.2 reshape.201
  93.0 12.8 %copy.90 = bf16[6,2,2048,128]{3,1,0,2:T(2,128)(2,1)} copy(bf16[6,2,2048,128]{3,2,1,0:T(8,128)(2,1)} %bitcast.80) | data formatting | bytes 12582912 | tf_op jit(solution)/shard_map/reshape | solution.py:50
  105.7 0.0 copy-done.12
  105.8 0.0 copy-done.4
  105.8 1.7 convolution_bitcast_fusion.3
  107.5 0.0 copy-start.8
  107.5 0.0 copy-start.10
  107.5 0.0 copy-start.13
  107.5 8.9 %gather_fusion = f32[1536]{0:T(1024)S(1)} fusion(f32[128,6,8]{0,2,1:T(8,128)S(1)} %convolution_bitcast_fusion.3, s32[1536]{0:T(1024)S(1)} %reshape.201), kind=kCustom, calls=%fused_computation.2 | custom fusion | bytes 30720 | tf_op jit(solution)/shard_map/jit(take_along_axis)/gather | solution.py:42
  116.4 0.2 reshape.204
  116.6 0.2 copy.84
  116.8 0.0 copy-done.13
  116.8 0.1 fusion.23
  116.9 123.3 %all-to-all-done = bf16[6,2,2048,128]{3,1,0,2:T(2,128)(2,1)} async-done(((bf16[6,2,2048,128]{3,1,0,2:T(2,128)(2,1)}), bf16[6,2,2048,128]{3,1,0,2:T(2,128)(2,1)}, u32[]{:S(2)}, u32[]{:S(2)}) %all-to-all-start) | async-done | bytes 6291488 | tf_op jit(solution)/shard_map/all_to_all | solution.py:54
  240.2 23.4 %all-to-all-start.1 = ((bf16[6,2,2048,128]{3,1,0,2:T(2,128)(2,1)}), bf16[6,2,2048,128]{3,1,0,2:T(2,128)(2,1)}, u32[]{:S(2)}, u32[]{:S(2)}) async-start(bf16[6,2,2048,128]{3,1,0,2:T(2,128)(2,1)} %copy.90), calls=%async_computation.1 | async-start | bytes 12582912 | tf_op jit(solution)/shard_map/all_to_all | solution.py:61
  263.6 0.2 all-gather.8.cloned.1.call-start
  263.8 6.5 copy.87
  270.4 16.2 %reshape.181 = bf16[6,2,4096,64]{3,2,1,0:T(8,128)(2,1)} reshape(bf16[6,2,2048,128]{3,2,1,0:T(8,128)(2,1)} %copy.87) | data formatting | bytes 12582912 | tf_op jit(solution)/shard_map/reshape.9
  286.5 8.7 %fusion.12 = bf16[128,6,64]{0,2,1:T(8,128)(2,1)} fusion(bf16[6,2,4096,64]{3,2,1,0:T(8,128)(2,1)} %reshape.181, bf16[128,4096]{1,0:T(8,128)(2,1)S(1)} %copy-done.3, f32[128,6,2]{0,2,1:T(2,128)S(1)} %fusion.23), kind=kOutput, calls=%fused_computation.23 | convolution fusion | flops 805453824 | bytes 7444480 | tf_op jit(solution)/shard_map/btd,hbjdk->hbjtk/dot_general | solution.py:58
  295.2 0.0 all-gather.8.cloned.1.call-update
  295.3 0.0 reduce-scatter.2.cloned.1.call-start
  295.3 0.7 slice.3
  296.7 124.3 %all-to-all-done.1 = bf16[6,2,2048,128]{3,1,0,2:T(2,128)(2,1)} async-done(((bf16[6,2,2048,128]{3,1,0,2:T(2,128)(2,1)}), bf16[6,2,2048,128]{3,1,0,2:T(2,128)(2,1)}, u32[]{:S(2)}, u32[]{:S(2)}) %all-to-all-start.1) | async-done | bytes 6291488 | tf_op jit(solution)/shard_map/all_to_all | solution.py:61
  421.0 6.5 copy.91
  427.4 16.1 %reshape.184 = bf16[6,2,4096,64]{3,2,1,0:T(8,128)(2,1)} reshape(bf16[6,2,2048,128]{3,2,1,0:T(8,128)(2,1)} %copy.91) | data formatting | bytes 12582912 | tf_op jit(solution)/shard_map/reshape.18
  443.6 13.3 %all-gather.6.cloned.1.call-done = bf16[8192,384]{0,1:T(8,128)(2,1)} async-done(((bf16[128,384]{0,1:T(8,128)(2,1)}), bf16[8192,384]{0,1:T(8,128)(2,1)}) %all-gather.6.cloned.1.call-update) | async-done | bytes 6291472 | tf_op jit(solution)/shard_map/all_gather | solution.py:94
  456.9 240.5 %all-gather.8.cloned.1.call-done = bf16[8192,384]{0,1:T(8,128)(2,1)} async-done(((bf16[128,384]{0,1:T(8,128)(2,1)}), bf16[8192,384]{0,1:T(8,128)(2,1)}) %all-gather.8.cloned.1.call-update) | async-done | bytes 6291472 | tf_op jit(solution)/shard_map/all_gather | solution.py:95
  697.4 39.6 %conditional.1 = (f32[6,128]{1,0:T(8,128)S(1)}, f32[6,128,64]{1,2,0:T(8,128)S(1)}) conditional(s32[]{:T(128)} %bitcast.6, () %tuple.14, (s32[8192]{0:T(1024)S(1)}, s32[128]{0:T(128)S(1)}, bf16[128,384]{1,0:T(8,128)(2,1)S(1)}, bf16[8192,384]{0,1:T(8,128)(2,1)}, bf16[8192,384]{0,1:T(8,128)(2,1)}) %tuple.34), branch_computations={%region_0.2_spmd, %region_1.5_spmd} | conditional | flops 1693449472 | bytes 92817936 | solution.py:100
  697.4 0.6 broadcast_compare_fusion
  698.1 0.1 copy.89
  698.2 12.5 %fusion = (f32[6,128]{1,0:T(8,128)S(1)}, f32[6,128,8192]{2,1,0:T(8,128)}) fusion(pred[128,8192]{1,0:T(8,128)(4,1)S(1)} %broadcast_compare_fusion, bf16[128,6,64]{0,2,1:T(8,128)(2,1)S(1)} %bitcast.86, bf16[8192,6,64]{0,2,1:T(8,128)(2,1)} %bitcast.84), kind=kOutput, calls=%fused_computation.5 | convolution fusion | flops 824179968 | bytes 32607232 | tf_op jit(solution)/shard_map/cond/branch_1_fun/thk,uhk->htu/dot_general | solution.py:72
  710.7 13.6 %fusion.3 = f32[6,128,64]{1,2,0:T(8,128)S(1)} fusion(bf16[8192,6,64]{0,2,1:T(8,128)(2,1)} %bitcast.90, f32[6,128,8192]{2,1,0:T(8,128)} %get-tuple-element.61, f32[6,128]{1,0:T(8,128)S(1)} %broadcast_maximum_fusion, pred[128,8192]{1,0:T(8,128)(4,1)S(1)} %broadcast_compare_fusion), kind=kOutput, calls=%fused_computation.8 | convolution fusion | flops 836763648 | bytes 32705536 | tf_op jit(solution)/shard_map/cond/branch_1_fun/htu,uhk->htk/dot_general | solution.py:80
  724.3 12.4 %fusion.2 = f32[6,128]{1,0:T(8,128)S(1)} fusion(f32[6,128,8192]{2,1,0:T(8,128)} %get-tuple-element.61, f32[6,128]{1,0:T(8,128)S(1)} %broadcast_maximum_fusion, pred[128,8192]{1,0:T(8,128)(4,1)S(1)} %broadcast_compare_fusion), kind=kLoop, calls=%fused_computation.7 | loop fusion | flops 31456512 | bytes 26220544 | tf_op jit(solution)/shard_map/cond/branch_1_fun/reduce_sum | solution.py:79
  737.1 0.0 copy-start.1
  737.1 8.8 %convolution_bitcast_fusion = f32[128,4096]{1,0:T(8,128)S(1)} fusion(bf16[6,2,4096,64]{3,2,1,0:T(8,128)(2,1)} %reshape.184, f32[128,6,64]{0,2,1:T(8,128)S(1)} %convert_bitcast_fusion, f32[128,6,2]{0,2,1:T(2,128)S(1)} %fusion.23), kind=kOutput, calls=%fused_computation.17 | convolution fusion | flops 805797888 | bytes 8591360 | tf_op jit(solution)/shard_map/bthjk,hbjck->btc/dot_general | solution.py:22
  745.9 9.8 %fusion.10 = bf16[128,4096]{1,0:T(8,128)(2,1)} fusion(f32[128,4096]{1,0:T(8,128)S(1)} %convolution_bitcast_fusion, bf16[6,2,4096,64]{3,2,1,0:T(8,128)(2,1)} %reshape.184, f32[128,6,64]{0,2,1:T(8,128)S(1)} %convert_bitcast_fusion, f32[128,6,2]{0,2,1:T(2,128)S(1)} %fusion.23), kind=kOutput, calls=%fused_computation.20 | convolution fusion | flops 806551552 | bytes 9639936 | tf_op jit(solution)/shard_map/bthjk,hbjck->btc/dot_general | solution.py:21
  755.7 0.0 reduce-scatter.2.cloned.1.call-update
  755.7 72.1 %reduce-scatter.2.cloned.1.call-done = bf16[128,1024]{1,0:T(8,128)(2,1)} async-done(((bf16[128,4096]{1,0:T(8,128)(2,1)}), bf16[128,1024]{1,0:T(8,128)(2,1)}) %reduce-scatter.2.cloned.1.call-update) | async-done | bytes 262160 | tf_op jit(solution)/shard_map/reduce_scatter | solution.py:114
  827.8 0.0 copy-done.1
  (23 shorter events, 0.1 us)
Async XLA Ops:
  6.5 1.6 copy-start
  6.5 8.3 copy-start.2
  6.5 99.2 %all-gather.4.cloned.1.call-start = ((), (), s32[]{:S(2)}) async-start(), calls=%async_computation.3 | async-start | bytes 1310720 | tf_op jit(solution)/shard_map/all_gather | solution.py:35
  30.3 60.4 %copy-start.5 = (bf16[128,384]{1,0:T(8,128)(2,1)S(1)}, bf16[128,384]{1,0:T(8,128)(2,1)}, u32[]{:S(2)}) copy-start(bf16[128,384]{1,0:T(8,128)(2,1)} %param.13) | copy-start | bytes 294916
  30.3 61.2 %copy-start.11 = (s32[64,6,2]{0,2,1:T(2,128)S(1)}, s32[64,6,2]{0,2,1:T(2,128)}, u32[]{:S(2)}) copy-start(s32[64,6,2]{0,2,1:T(2,128)} %param.17) | copy-start | bytes 9220
  76.8 29.0 %copy-start.4 = (bf16[48,4096]{1,0:T(8,128)(2,1)S(1)}, bf16[48,4096]{1,0:T(8,128)(2,1)}, u32[]{:S(2)}) copy-start(bf16[48,4096]{1,0:T(8,128)(2,1)} %param.14) | copy-start | bytes 1179652
  76.8 163.4 %all-to-all-start = ((bf16[6,2,2048,128]{3,1,0,2:T(2,128)(2,1)}), bf16[6,2,2048,128]{3,1,0,2:T(2,128)(2,1)}, u32[]{:S(2)}, u32[]{:S(2)}) async-start(bf16[6,2,2048,128]{3,1,0,2:T(2,128)(2,1)} %copy.86), calls=%async_computation | async-start | bytes 12582912 | tf_op jit(solution)/shard_map/all_to_all | solution.py:54
  90.7 366.2 %all-gather.6.cloned.1.call-start = ((), (), s32[]{:S(2)}) async-start(), calls=%async_computation.4 | async-start | bytes 6389760 | tf_op jit(solution)/shard_map/all_gather | solution.py:94
  91.8 0.6 copy-start.7
  91.9 0.6 copy-start.9
  92.1 13.7 %copy-start.12 = (pred[6,2]{1,0:T(8,128)(4,1)}, pred[6,2]{1,0:T(8,128)(4,1)S(1)}, u32[]{:S(2)}) copy-start(pred[6,2]{1,0:T(8,128)(4,1)S(1)} %copy.77) | copy-start | bytes 40
  107.5 9.3 %copy-start.8 = (s32[6,2]{1,0:T(8,128)S(1)}, s32[6,2]{1,0:T(8,128)}, u32[]{:S(2)}) copy-start(s32[6,2]{1,0:T(8,128)} %copy-done.7) | copy-start | bytes 148
  107.5 9.3 %copy-start.10 = (s32[6,2]{1,0:T(8,128)S(1)}, s32[6,2]{1,0:T(8,128)}, u32[]{:S(2)}) copy-start(s32[6,2]{1,0:T(8,128)} %copy-done.9) | copy-start | bytes 148
  107.5 9.3 %copy-start.13 = (pred[6,2]{1,0:T(8,128)(4,1)S(1)}, pred[6,2]{1,0:T(8,128)(4,1)}, u32[]{:S(2)}) copy-start(pred[6,2]{1,0:T(8,128)(4,1)} %copy-done.12) | copy-start | bytes 40
  240.2 180.8 %all-to-all-start.1 = ((bf16[6,2,2048,128]{3,1,0,2:T(2,128)(2,1)}), bf16[6,2,2048,128]{3,1,0,2:T(2,128)(2,1)}, u32[]{:S(2)}, u32[]{:S(2)}) async-start(bf16[6,2,2048,128]{3,1,0,2:T(2,128)(2,1)} %copy.90), calls=%async_computation.1 | async-start | bytes 12582912 | tf_op jit(solution)/shard_map/all_to_all | solution.py:61
  263.6 433.8 %all-gather.8.cloned.1.call-start = ((), (), s32[]{:S(2)}) async-start(), calls=%async_computation.5 | async-start | bytes 6389760 | tf_op jit(solution)/shard_map/all_gather | solution.py:95
  270.4 16.2 %copy-start.3 = (bf16[128,4096]{1,0:T(8,128)(2,1)S(1)}, bf16[128,4096]{1,0:T(8,128)(2,1)}, u32[]{:S(2)}) copy-start(bf16[128,4096]{1,0:T(8,128)(2,1)} %all-gather.4.cloned.1.call-done) | copy-start | bytes 3145732
  295.3 532.6 %reduce-scatter.2.cloned.1.call-start = ((), (), s32[]{:S(2)}) async-start(), calls=%async_computation.6 | async-start | bytes 1310720 | tf_op jit(solution)/shard_map/reduce_scatter | solution.py:114
  427.4 270.0 %copy-start.6 = (bf16[128,384]{1,0:T(8,128)(2,1)S(1)}, bf16[128,384]{1,0:T(8,128)(2,1)}, u32[]{:S(2)}) copy-start(bf16[128,384]{1,0:T(8,128)(2,1)} %param.12) | copy-start | bytes 294916
  737.1 90.8 %copy-start.1 = (bf16[6,8,32,128]{3,2,1,0:T(8,128)(2,1)S(1)}, bf16[6,8,32,128]{3,2,1,0:T(8,128)(2,1)}, u32[]{:S(2)}) copy-start(bf16[6,8,32,128]{3,2,1,0:T(8,128)(2,1)} %param.15) | copy-start | bytes 1179652
Sparse Core Ops, SparseCore 0:
  9.2 27.5 all-gather.3
  93.3 363.5 all-gather.5
  458.6 238.7 all-gather.7
  755.8 71.9 reduce-scatter.1
where the time goes:
time: 836 us; the launch traced here: 834 us
  waiting for transfers between devices  574 us (69%)
  local copies, waits for them, and re-layouts  131 us (16%)
  matrix products  55.2 us (7%)
  starting transfers between devices  37.6 us (4%)
  other arithmetic  21.9 us (3%)
  between operations  14 us (2%)
    all_gather x1, waiting for transfers between devices, body(): lax.all_gather(values, 'seq', axis=0, tiled=True)  241 us
    all_to_all x1, waiting for transfers between devices, body(): lax.all_to_all(select_rows(output_experts), 'seq', split_axis=2, concat_a...  124 us
    all_to_all x1, waiting for transfers between devices, body(): lax.all_to_all(select_rows(value_experts), 'seq', split_axis=2, concat_ax...  123 us
    reduce_scatter x1, waiting for transfers between devices, body(): lax.psum_scatter(terms.astype(jnp.bfloat16), 'head', scatter_dimension=1,...  72.1 us
    reshape x2, local copies, waits for them, and re-layouts, select_rows(): picked.reshape(heads_dev, blocks_dev * TOP, seq_count * expert_table.shap...  59.2 us
    another operation x3, local copies, waits for them, and re-layouts  32.4 us
    all_to_all x1, starting transfers between devices, body(): lax.all_to_all(select_rows(output_experts), 'seq', split_axis=2, concat_a...  23.4 us
  transfers between devices with their start and end apart: 6, of which 5 were waited for; matrix products, arithmetic and copies ran while one was open for 18% of the time, Pallas kernels for 0%

commit v1 on v0

v1 whole, which is shorter than its diff:
```python
import math

import jax
import jax.numpy as jnp
from jax import lax
from jax.experimental import pallas as pl
from jax.experimental.pallas import tpu as pltpu
from jax.sharding import Mesh, PartitionSpec as P

TOP = 2
BLK = 128
SLABS = 8
PLANE = 8
HALF = 64
LANES = 128
AXES = ("z", "yl", "x", "yh", "c")
SEQ_AXES = ("z", "yl", "x")
HEAD_AXES = ("yh", "c")
PLANE_AXES = ("yl", "x")
bf16 = jnp.bfloat16
f32 = jnp.float32
i32 = jnp.int32
masked_score = -1e30
VMEM_BYTES = 56 * 1024 * 1024

smem = pl.BlockSpec(memory_space=pltpu.SMEM)
vmem = pl.BlockSpec(memory_space=pltpu.VMEM)
params = pltpu.CompilerParams(vmem_limit_bytes=VMEM_BYTES)


def cost(flops, nbytes, trans=0):
    return pl.CostEstimate(flops=flops, bytes_accessed=nbytes, transcendentals=trans)


def iota(shape, dim):
    return lax.broadcasted_iota(i32, shape, dim)


def one_hot(mask):
    return jnp.where(mask, 1.0, 0.0).astype(bf16)


def nt_dot(a, b):
    return lax.dot_general(a, b, (((1,), (1,)), ((), ())), preferred_element_type=f32)


def dot(a, b):
    return jnp.dot(a, b, preferred_element_type=f32)


def message_kernel(ids, place, f0, f1, f2, f3, router, out):
    slots = router.shape[0] // 8 * TOP
    quarter = f0.shape[1]
    seq, group = place[0], place[1]
    row, col = iota((LANES, router.shape[0]), 0), iota((LANES, router.shape[0]), 1)
    target = jnp.full(row.shape, -1, i32)
    for k in range(slots):
        target = jnp.where(row == k, (k // TOP) * 8 + ids[seq * slots + k], target)
    chosen = one_hot(col == target)
    logits = jnp.zeros((BLK, LANES), f32)
    for rel, part in enumerate((f0, f1, f2, f3)):
        first = pl.multiple_of((group ^ rel) * quarter, quarter)
        rows = dot(chosen, router[:, pl.ds(first, quarter)]).astype(bf16)
        logits = logits + nt_dot(part[...], rows)
        for pi in range(PLANE):
            low = part[:, pi * HALF : (pi + 1) * HALF]
            high = part[:, quarter // 2 + pi * HALF : quarter // 2 + (pi + 1) * HALF]
            out[pi, :, rel * LANES : (rel + 1) * LANES] = jnp.concatenate([low, high], axis=1)
    gates = jax.nn.sigmoid(logits).astype(bf16)
    for pi in range(PLANE):
        out[pi, :, 4 * LANES :] = gates


def pair_kernel(scale, queries, keys, out):
    for i in range(PLANE):
        if i * HALF < queries.shape[1]:
            own = slice(i * HALF, (i + 1) * HALF)
            out[i] = jnp.concatenate([queries[:, own] * bf16(scale), keys[:, own]], axis=1)
        else:
            out[i] = jnp.zeros((BLK, LANES), bf16)


def key_kernel(pairs, out):
    for q in range(PLANE // 2):
        out[q] = jnp.concatenate([pairs[2 * q][:, HALF:], pairs[2 * q + 1][:, HALF:]], axis=1)


def value_kernel(ids, place, message, table, out):
    heads = table.shape[1]
    z, group = place[2], place[1]
    src, dst = iota((512, 512), 0), iota((512, 512), 1)
    within = src & 63
    source_z = ((src >> 7) ^ group) * 2 + ((src >> 6) & 1)
    split = one_hot(dst == (within & 1) * 256 + source_z * 32 + (within >> 1))
    left = iota((BLK, LANES), 1) < HALF

    def two_blocks(q, carry):
        done = []
        for bb in range(2):
            b = 2 * q + bb
            x = dot(message[b, :, 0:512], split).astype(bf16)
            x = jnp.concatenate([x[:, :256], x[:, 256:]], axis=0)
            gates = message[b, :, 512:].astype(f32)
            sums = []
            for h in range(heads):
                total = 0.0
                picked = [
                    table[:, h, ids[((z * PLANE + b) * heads + h) * TOP + j]].reshape(256, LANES)
                    for j in range(TOP)
                ]
                r = dot(x, jnp.concatenate(picked, axis=1))
                for j in range(TOP):
                    cols = slice(j * LANES, (j + 1) * LANES)
                    k = h * TOP + j
                    total = total + gates[:, k : k + 1] * jnp.where(left, r[:BLK, cols], r[BLK:, cols])
                sums.append(total + pltpu.roll(total, HALF, 1))
            done.append(sums)
        for h in range(heads):
            out[h, q] = jnp.where(left, done[0][h], done[1][h]).astype(bf16)
        for h in range(heads, PLANE):
            out[h, q] = jnp.zeros((BLK, LANES), bf16)
        return carry

    lax.fori_loop(0, PLANE // 2, two_blocks, 0)


def weight_kernel(place, pairs, k0, k1, k2, k3, k4, k5, k6, k7, probs, sums, scores, tops, totals):
    block, z = pl.program_id(0), place[2]
    left = iota((BLK, LANES), 1) < HALF
    zero = jnp.zeros((BLK, HALF), bf16)
    own = pairs[0][:, :HALF]
    q = jnp.concatenate(
        [jnp.concatenate([own, zero], axis=1), jnp.concatenate([zero, own], axis=1)], axis=0
    )
    tops[...] = jnp.full(tops.shape, masked_score, f32)
    totals[...] = jnp.zeros(totals.shape, f32)

    for s, keys in enumerate((k0, k1, k2, k3, k4, k5, k6, k7)):

        @pl.when(s <= z)
        def _():
            got = nt_dot(q, keys[...])
            if s == 0:
                row, col = iota(got.shape, 0), iota(got.shape, 1)
                key_pos = (2 * (col >> 7) + (row >> 7)) * BLK + (col & 127)
                got = jnp.where(key_pos <= block * BLK + (row & 127), got, masked_score)
            scores[s] = got
            best = tops[...]
            for part in range(4):
                cols = slice(part * LANES, (part + 1) * LANES)
                best = jnp.maximum(best, jnp.maximum(got[:BLK, cols], got[BLK:, cols]))
            tops[...] = best

    top = jnp.max(tops[...], axis=1, keepdims=True)

    for s in range(SLABS):

        @pl.when(s <= z)
        def _():
            total = totals[...]
            for bb in range(2):
                p = jnp.exp(scores[s, bb * BLK : (bb + 1) * BLK, :] - top)
                for part in range(4):
                    total = total + p[:, part * LANES : (part + 1) * LANES]
                probs[s, bb] = p.astype(bf16)
            totals[...] = total

    sums[...] = jnp.broadcast_to(jnp.sum(totals[...], axis=1, keepdims=True), (BLK, LANES))


def attend_kernel(place, probs, sums, v0, v1, v2, v3, v4, v5, v6, v7, out, acc):
    step, z = pl.program_id(0), place[2]

    @pl.when(step == 0)
    def _():
        acc[...] = jnp.zeros(acc.shape, f32)

    for s, values in enumerate((v0, v1, v2, v3, v4, v5, v6, v7)):

        @pl.when((step == s) & (s <= z))
        def _():
            for bb in range(2):
                acc[bb] += dot(probs[0, bb], values[...])

    @pl.when(step == SLABS - 1)
    def _():
        left = iota((BLK, LANES), 1) < HALF
        for q in range(PLANE // 2):
            pair = []
            for bb in range(2):
                rows = slice((2 * q + bb) * BLK, (2 * q + bb + 1) * BLK)
                o = jnp.where(left, acc[0, rows], acc[1, rows])
                pair.append((o + pltpu.roll(o, HALF, 1)) / sums[rows])
            packed = jnp.where(left, pair[0], pair[1]).astype(bf16)
            for pi in range(PLANE):
                out[pi, q] = packed


def mix_kernel(ids, place, attended, gates_in, table, near, far, lhs, rhs, natural):
    heads = table.shape[1]
    z, group = place[2], place[1]
    src, dst = iota((512, 512), 0), iota((512, 512), 1)
    order = one_hot(dst == ((src & 255) >> 5) * 64 + 2 * (src & 31) + (src >> 8))
    left = iota((BLK, LANES), 1) < HALF

    def two_blocks(q, carry):
        for bb in range(2):
            b = 2 * q + bb
            gates = gates_in[b].astype(f32)
            for h in range(heads):
                half = attended[h, q][:, bb * HALF : (bb + 1) * HALF]
                both = jnp.concatenate([half, half], axis=1).astype(f32)
                for j in range(TOP):
                    k = h * TOP + j
                    cols = slice(k * LANES, (k + 1) * LANES)
                    gated = both * gates[:, k : k + 1]
                    lhs[0:BLK, cols] = jnp.where(left, gated, 0.0).astype(bf16)
                    lhs[BLK:, cols] = jnp.where(left, 0.0, gated).astype(bf16)
                    rhs[:, cols] = table[
                        :, h, ids[((z * PLANE + b) * heads + h) * TOP + j]
                    ].reshape(256, LANES)
            r = nt_dot(lhs[...], rhs[...])
            flat = jnp.concatenate([r[:BLK], r[BLK:]], axis=1).astype(bf16)
            flat = dot(flat, order).astype(bf16)
            for g in range(4):
                natural[g] = flat[:, g * LANES : (g + 1) * LANES]
            near[0, b] = natural[group]
            far[0, b] = natural[group ^ 1]
            near[1, b] = natural[group ^ 2]
            far[1, b] = natural[group ^ 3]
        return carry

    lax.fori_loop(0, PLANE // 2, two_blocks, 0)


def place_kernel(pieces, out):
    width = out.shape[1] // 2
    for low in range(2):
        own = slice(low * HALF, (low + 1) * HALF)
        for m in range(PLANE // 2):
            out[:, low * width + m * LANES : low * width + (m + 1) * LANES] = jnp.concatenate(
                [pieces[2 * m][:, own], pieces[2 * m + 1][:, own]], axis=1
            )


def swap(x, axis):
    return lax.ppermute(x, axis, [(0, 1), (1, 0)])


def plane_exchange(x):
    return lax.all_to_all(x, PLANE_AXES, split_axis=0, concat_axis=0, tiled=True)


def later_slabs(x):
    return [x] + [
        lax.ppermute(x, "z", [(i, i + s) for i in range(SLABS - s)]) for s in range(1, SLABS)
    ]


def add(a, b):
    return (a.astype(f32) + b.astype(f32)).astype(bf16)


def body(features, queries, keys, router, value_experts, output_experts, expert_ids):
    z = lax.axis_index("z")
    group = lax.axis_index(HEAD_AXES)
    seq = lax.axis_index(SEQ_AXES)
    place = jnp.stack([seq, group, z]).astype(i32)
    ids = expert_ids.reshape(-1)
    heads = value_experts.shape[0]
    scale = 1.0 / math.sqrt(HALF)

    value_table = lax.all_gather(value_experts, "z", axis=0, tiled=False)
    pairs = pl.pallas_call(
        lambda *refs: pair_kernel(scale, *refs),
        out_shape=jax.ShapeDtypeStruct((PLANE, BLK, LANES), bf16),
        in_specs=[vmem, vmem],
        out_specs=vmem,
        cost_estimate=cost(0, 500_000),
    )(queries, keys)
    pairs = plane_exchange(pairs)

    over_y = swap(features, "yh")
    over_c = swap(features, "c")
    over_yc = swap(over_y, "c")
    message = pl.pallas_call(
        message_kernel,
        out_shape=jax.ShapeDtypeStruct((PLANE, BLK, 5 * LANES), bf16),
        in_specs=[smem, smem] + [vmem] * 5,
        out_specs=vmem,
        compiler_params=params,
        cost_estimate=cost(2 * BLK * LANES * 4096 * 2, 3_000_000),
    )(ids, place, features, over_c, over_y, over_yc, router)
    message = plane_exchange(message)

    own_keys = pl.pallas_call(
        key_kernel,
        out_shape=jax.ShapeDtypeStruct((PLANE // 2, BLK, LANES), bf16),
        in_specs=[vmem],
        out_specs=vmem,
        cost_estimate=cost(0, 400_000),
    )(pairs).reshape(PLANE // 2 * BLK, LANES)
    key_parts = later_slabs(own_keys)

    slab = PLANE * BLK
    probs, sums = pl.pallas_call(
        weight_kernel,
        grid=(PLANE,),
        out_shape=(
            jax.ShapeDtypeStruct((SLABS, 2, slab, slab // 2), bf16),
            jax.ShapeDtypeStruct((slab, LANES), f32),
        ),
        in_specs=[smem, pl.BlockSpec((1, BLK, LANES), lambda i: (i, 0, 0))] + [vmem] * SLABS,
        out_specs=(
            pl.BlockSpec((SLABS, 2, BLK, slab // 2), lambda i: (0, 0, i, 0)),
            pl.BlockSpec((BLK, LANES), lambda i: (i, 0)),
        ),
        scratch_shapes=[
            pltpu.VMEM((SLABS, 2 * BLK, slab // 2), f32),
            pltpu.VMEM((BLK, LANES), f32),
            pltpu.VMEM((BLK, LANES), f32),
        ],
        compiler_params=params,
        cost_estimate=cost(2 * slab * SLABS * slab * 128, 18_000_000, slab * slab * SLABS),
    )(place, pairs, *key_parts)

    partial = pl.pallas_call(
        value_kernel,
        out_shape=jax.ShapeDtypeStruct((PLANE, PLANE // 2, BLK, LANES), bf16),
        in_specs=[smem, smem, vmem, vmem],
        out_specs=vmem,
        compiler_params=params,
        cost_estimate=cost(2 * 48 * 256 * 256 * 256, 6_000_000),
    )(ids, place, message, value_table)
    partial = plane_exchange(partial)
    own_values = jnp.sum(partial.astype(f32), axis=0).astype(bf16).reshape(slab // 2, LANES)
    value_parts = later_slabs(own_values)
    output_table = lax.all_gather(output_experts, "z", axis=0, tiled=False)

    attended = pl.pallas_call(
        attend_kernel,
        grid_spec=pltpu.PrefetchScalarGridSpec(
            num_scalar_prefetch=1,
            grid=(SLABS,),
            in_specs=[
                pl.BlockSpec((1, 2, slab, slab // 2), lambda s, at: (jnp.minimum(s, at[2]), 0, 0, 0)),
                pl.BlockSpec((slab, LANES), lambda s, at: (0, 0)),
            ]
            + [pl.BlockSpec((slab // 2, LANES), lambda s, at: (0, 0))] * SLABS,
            out_specs=pl.BlockSpec((PLANE, PLANE // 2, BLK, LANES), lambda s, at: (0, 0, 0, 0)),
            scratch_shapes=[pltpu.VMEM((2, slab, LANES), f32)],
        ),
        out_shape=jax.ShapeDtypeStruct((PLANE, PLANE // 2, BLK, LANES), bf16),
        compiler_params=params,
        cost_estimate=cost(2 * slab * SLABS * slab * 128, 18_000_000),
    )(place, probs, sums, *value_parts)
    attended = plane_exchange(attended)

    half_out = jax.ShapeDtypeStruct((2, PLANE, BLK, LANES), bf16)
    near, far = pl.pallas_call(
        mix_kernel,
        out_shape=(half_out, half_out),
        in_specs=[smem, smem, vmem, vmem, vmem],
        out_specs=(vmem, vmem),
        scratch_shapes=[
            pltpu.VMEM((2 * BLK, heads * TOP * LANES), bf16),
            pltpu.VMEM((256, heads * TOP * LANES), bf16),
            pltpu.VMEM((4, BLK, LANES), bf16),
        ],
        compiler_params=params,
        cost_estimate=cost(2 * 48 * 256 * 256 * 256, 6_000_000),
    )(ids, place, attended, message[:, :, 4 * LANES :], output_table)
    near = add(near, swap(far, "c"))
    mixed = add(near[0], swap(near[1], "yh"))
    mixed = plane_exchange(mixed)
    return pl.pallas_call(
        place_kernel,
        out_shape=jax.ShapeDtypeStruct(features.shape, bf16),
        in_specs=[vmem],
        out_specs=vmem,
        cost_estimate=cost(0, 600_000),
    )(mixed)


def solution(mesh):
    fine = Mesh(mesh.devices.reshape(SLABS, 2, 4, 2, 2), AXES)
    return jax.shard_map(
        body,
        mesh=fine,
        in_specs=(
            P(SEQ_AXES, HEAD_AXES),
            P(SEQ_AXES, HEAD_AXES),
            P(SEQ_AXES, HEAD_AXES),
            P(HEAD_AXES, None),
            P(HEAD_AXES, None, SEQ_AXES, None),
            P(HEAD_AXES, None, SEQ_AXES, None),
            P(None, HEAD_AXES, None),
        ),
        out_specs=P(SEQ_AXES, HEAD_AXES),
        check_vma=False,
    )
```

time: 836 us -> 225 us (0.27)
  the two profiles are of different devices: /device:TPU:1 before, /device:TPU:192 now
where the time goes in v1:
time: 225 us; the launch traced here: 224 us
  waiting for transfers between devices  83.9 us (37%)
  Pallas kernels  61.6 us (27%)
  starting transfers between devices  45.5 us (20%)
  between operations  13.8 us (6%)
  blocking collectives  10.4 us (5%)
  local copies, waits for them, and re-layouts  6.44 us (3%)
    all_to_all x4, waiting for transfers between devices, plane_exchange(): lax.all_to_all(x, PLANE_AXES, split_axis=0, concat_axis=0, tiled=True)  34.4 us
    ppermute x14, waiting for transfers between devices, later_slabs(): lax.ppermute(x, 'z', [(i, i + s) for i in range(SLABS - s)])  32.3 us
    pallas_call x1, Pallas kernels, body(): pl.pallas_call(weight_kernel, grid=(PLANE,), out_shape=(jax.ShapeDtypeStr...  22.9 us
    all_to_all x4, starting transfers between devices, plane_exchange(): lax.all_to_all(x, PLANE_AXES, split_axis=0, concat_axis=0, tiled=True)  20.2 us
    ppermute x14, starting transfers between devices, later_slabs(): lax.ppermute(x, 'z', [(i, i + s) for i in range(SLABS - s)])  19.2 us
    ppermute x5, waiting for transfers between devices, swap(): return lax.ppermute(x, axis, [(0, 1), (1, 0)])  15.9 us
    pallas_call x1, Pallas kernels, body(): pl.pallas_call(attend_kernel, grid_spec=pltpu.PrefetchScalarGridSpec(num_...  11.9 us
    all_to_all x1, blocking collectives, plane_exchange(): lax.all_to_all(x, PLANE_AXES, split_axis=0, concat_axis=0, tiled=True)  10.4 us
  transfers between devices with their start and end apart: 25, of which 10 were waited for; matrix products, arithmetic and copies ran while one was open for 2% of the time, Pallas kernels for 22%

profile of v1, /device:TPU:192, one launch (start us, length us, event | category | flops | bytes accessed | tf_op | source)
XLA Modules:
  0.0 223.7 jit_solution(10275113861823855712)
XLA Ops:
  6.5 0.7 all-gather.5.cloned.1.call-update
  7.3 0.0 all-gather.7.cloned.1.call-start
  7.3 0.7 all-gather.7.cloned.1.call-update
  8.0 3.3 %collective-permute-start.8 = (bf16[128,1024]{1,0:T(8,128)(2,1)}, bf16[128,1024]{1,0:T(8,128)(2,1)S(1)}, u32[]{:S(2)}, u32[]{:S(2)}) collective-permute-start(bf16[128,1024]{1,0:T(8,128)(2,1)} %f0.1), channel_id=1, source_target_pairs={{0,2},{2,0},{1,3},{3,1},{4,6},{6,4},{5,7},{7,5},{8,10},{10,8},{9,1... | collective-permute-start | bytes 786440 | tf_op jit(solution)/shard_map/ppermute | solution.py:247
  11.3 6.6 %collective-permute-done.8.f2 = bf16[128,1024]{1,0:T(8,128)(2,1)S(1)} collective-permute-done((bf16[128,1024]{1,0:T(8,128)(2,1)}, bf16[128,1024]{1,0:T(8,128)(2,1)S(1)}, u32[]{:S(2)}, u32[]{:S(2)}) %collective-permute-start.8) | collective-permute-done | bytes 262176 | tf_op jit(solution)/shard_map/ppermute | solution.py:247
  17.9 0.0 collective-permute-start.9
  17.9 0.9 copy.9
  18.7 0.7 reshape.11.ids
  19.4 0.6 pad_add_fusion.place
  20.1 0.7 copy-done.5
  20.8 0.7 copy-done.6
  21.5 3.4 %shard_map.76 = bf16[8,128,640]{2,1,0:T(8,128)(2,1)} custom-call(s32[768]{0:T(1024)} %reshape.11.ids, s32[3]{0:T(128)} %pad_add_fusion.place, bf16[128,1024]{1,0:T(8,128)(2,1)} %f0.1, bf16[128,1024]{1,0:T(8,128)(2,1)} %copy-done.5, bf16[128,1024]{1,0:T(8,128)(2,1)} %copy-done.4, bf16[128,1024]{1,0:T(8,128)(2,1)} %copy-done.6, bf16[48,4096]{1,0:T(8,128)(2,1)} %router.1), custom_call_target="tpu_custom_call" | custom-call | flops 268435456 | bytes 3000000 | tf_op jit(solution)/shard_map/pallas_call | solution.py:286
  24.9 5.3 %all-to-all-start.1 = ((bf16[8,128,640]{2,1,0:T(8,128)(2,1)}), bf16[8,128,640]{2,1,0:T(8,128)(2,1)S(1)}, u32[]{:S(2)}, u32[]{:S(2)}) async-start(bf16[8,128,640]{2,1,0:T(8,128)(2,1)} %shard_map.76), calls=%async_computation.1 | async-start | bytes 2621440 | tf_op jit(solution)/shard_map/all_to_all | solution.py:251
  30.2 1.8 shard_map.73
  32.0 17.4 %all-to-all-done.1.message = bf16[8,128,640]{2,1,0:T(8,128)(2,1)S(1)} async-done(((bf16[8,128,640]{2,1,0:T(8,128)(2,1)}), bf16[8,128,640]{2,1,0:T(8,128)(2,1)S(1)}, u32[]{:S(2)}, u32[]{:S(2)}) %all-to-all-start.1) | async-done | bytes 1310752 | tf_op jit(solution)/shard_map/all_to_all | solution.py:251
  49.4 3.6 %all-to-all-start = ((bf16[8,128,128]{2,1,0:T(8,128)(2,1)}), bf16[8,128,128]{2,1,0:T(8,128)(2,1)S(1)}, u32[]{:S(2)}, u32[]{:S(2)}) async-start(bf16[8,128,128]{2,1,0:T(8,128)(2,1)} %shard_map.73), calls=%async_computation | async-start | bytes 524288 | tf_op jit(solution)/shard_map/all_to_all | solution.py:251
  53.0 0.0 all-gather.5.cloned.1.call-done
  53.0 7.9 %shard_map.77 = bf16[8,4,128,128]{3,2,1,0:T(8,128)(2,1)} custom-call(s32[768]{0:T(1024)} %reshape.11.ids, s32[3]{0:T(128)} %pad_add_fusion.place, bf16[8,128,640]{2,1,0:T(8,128)(2,1)} %copy-done, bf16[8,6,8,32,128]{4,3,2,1,0:T(8,128)(2,1)} %bitcast.31), custom_call_target="tpu_custom_call" | custom-call | flops 1610612736 | bytes 6000000 | tf_op jit(solution)/shard_map/pallas_call | solution.py:327
  60.9 0.0 all-to-all-done.pairs
  60.9 5.7 %all-to-all-start.2 = ((bf16[8,4,128,128]{3,2,1,0:T(8,128)(2,1)}), bf16[8,4,128,128]{3,2,1,0:T(8,128)(2,1)S(1)}, u32[]{:S(2)}, u32[]{:S(2)}) async-start(bf16[8,4,128,128]{3,2,1,0:T(8,128)(2,1)} %shard_map.77), calls=%async_computation.2 | async-start | bytes 2097152 | tf_op jit(solution)/shard_map/all_to_all | solution.py:251
  66.6 1.7 shard_map.74
  68.3 2.9 %collective-permute-start = (bf16[512,128]{1,0:T(8,128)(2,1)}, bf16[512,128]{1,0:T(8,128)(2,1)S(1)}, u32[]{:S(2)}, u32[]{:S(2)}) collective-permute-start(bf16[512,128]{1,0:T(8,128)(2,1)} %bitcast.22), channel_id=1, source_target_pairs={{0,32},{32,64},{64,96},{96,128},{128,160},{160,192},{192,224},{1,3... | collective-permute-start | bytes 393224 | tf_op jit(solution)/shard_map/ppermute | solution.py:256
  71.2 1.3 collective-permute-start.1
  72.5 1.3 collective-permute-start.2
  73.8 1.3 collective-permute-start.3
  75.1 1.3 collective-permute-start.4
  76.4 5.3 %all-to-all-done.2 = bf16[8,4,128,128]{3,2,1,0:T(8,128)(2,1)S(1)} async-done(((bf16[8,4,128,128]{3,2,1,0:T(8,128)(2,1)}), bf16[8,4,128,128]{3,2,1,0:T(8,128)(2,1)S(1)}, u32[]{:S(2)}, u32[]{:S(2)}) %all-to-all-start.2) | async-done | bytes 1048608 | tf_op jit(solution)/shard_map/all_to_all | solution.py:251
  81.7 0.1 reduce_sum.12
  81.8 0.0 collective-permute-done.k1
  81.9 1.3 collective-permute-start.5
  83.2 5.8 %collective-permute-done.1.k2 = bf16[512,128]{1,0:T(8,128)(2,1)S(1)} collective-permute-done((bf16[512,128]{1,0:T(8,128)(2,1)}, bf16[512,128]{1,0:T(8,128)(2,1)S(1)}, u32[]{:S(2)}, u32[]{:S(2)}) %collective-permute-start.1) | collective-permute-done | bytes 131104 | tf_op jit(solution)/shard_map/ppermute | solution.py:256
  88.9 0.7 collective-permute-start.6
  89.6 13.2 %collective-permute-done.2.k3 = bf16[512,128]{1,0:T(8,128)(2,1)S(1)} collective-permute-done((bf16[512,128]{1,0:T(8,128)(2,1)}, bf16[512,128]{1,0:T(8,128)(2,1)S(1)}, u32[]{:S(2)}, u32[]{:S(2)}) %collective-permute-start.2) | collective-permute-done | bytes 131104 | tf_op jit(solution)/shard_map/ppermute | solution.py:256
  102.8 1.9 collective-permute-start.10
  104.7 5.3 %collective-permute-done.3.k4 = bf16[512,128]{1,0:T(8,128)(2,1)S(1)} collective-permute-done((bf16[512,128]{1,0:T(8,128)(2,1)}, bf16[512,128]{1,0:T(8,128)(2,1)S(1)}, u32[]{:S(2)}, u32[]{:S(2)}) %collective-permute-start.3) | collective-permute-done | bytes 131104 | tf_op jit(solution)/shard_map/ppermute | solution.py:256
  110.0 1.3 collective-permute-start.11
  111.3 0.0 collective-permute-done.4.k5
  111.3 1.3 collective-permute-start.12
  112.6 0.0 collective-permute-done.5.k6
  112.6 1.3 collective-permute-start.13
  113.9 1.3 collective-permute-start.14
  115.2 1.3 collective-permute-start.15
  116.5 8.0 %collective-permute-done.11.v2 = bf16[512,128]{1,0:T(8,128)(2,1)S(1)} collective-permute-done((bf16[512,128]{1,0:T(8,128)(2,1)S(1)}, bf16[512,128]{1,0:T(8,128)(2,1)S(1)}, u32[]{:S(2)}, u32[]{:S(2)}) %collective-permute-start.11) | collective-permute-done | bytes 131104 | tf_op jit(solution)/shard_map/ppermute | solution.py:256
  124.6 0.8 collective-permute-start.16
  125.5 22.9 %shard_map.75 = (bf16[8,2,1024,512]{3,2,1,0:T(8,128)(2,1)}, f32[1024,128]{1,0:T(8,128)}) custom-call(s32[3]{0:T(128)} %pad_add_fusion.place, bf16[8,128,128]{2,1,0:T(8,128)(2,1)} %copy-done.2, bf16[512,128]{1,0:T(8,128)(2,1)} %bitcast.29, bf16[512,128]{1,0:T(8,128)(2,1)} %copy-done.14, bf16[512,128]{1,0:T(8,128)(2,1)} %copy-done.15, ...), custom_call_target="tpu_custom_call" | custom-call | flops 2147483648 | bytes 18000000 | tf_op jit(solution)/shard_map/pallas_call | solution.py:306
  148.4 0.0 copy-start.9
  148.5 0.6 copy-done.9
  149.1 0.0 copy-done.10
  149.1 0.0 copy-done.11
  149.1 0.1 copy-done.12
  149.2 0.0 copy-done.13
  149.2 11.9 %shard_map.78 = bf16[8,4,128,128]{3,2,1,0:T(8,128)(2,1)} custom-call(s32[3]{0:T(128)} %pad_add_fusion.place, bf16[8,2,1024,512]{3,2,1,0:T(8,128)(2,1)} %get-tuple-element.9.probs, f32[1024,128]{1,0:T(8,128)} %get-tuple-element.10.sums, bf16[512,128]{1,0:T(8,128)(2,1)} %bitcast.21, bf16[512,128]{1,0:T(8,128)(2,1)} %copy-done.7, bf16[512,128]{1,0:T(8,128)(2,1)} %copy-done.8, ...), custom_call_target="tpu_custom_call" | custom-call | flops 2147483648 | bytes 18000000 | tf_op jit(solution)/shard_map/pallas_call | solution.py:340
  161.1 5.6 %all-to-all-start.3 = ((bf16[8,4,128,128]{3,2,1,0:T(8,128)(2,1)}), bf16[8,4,128,128]{3,2,1,0:T(8,128)(2,1)S(1)}, u32[]{:S(2)}, u32[]{:S(2)}) async-start(bf16[8,4,128,128]{3,2,1,0:T(8,128)(2,1)} %shard_map.78), calls=%async_computation.3 | async-start | bytes 2097152 | tf_op jit(solution)/shard_map/all_to_all | solution.py:251
  166.7 1.7 slice.12.gates_in
  168.4 11.7 %all-to-all-done.3.attended = bf16[8,4,128,128]{3,2,1,0:T(8,128)(2,1)S(1)} async-done(((bf16[8,4,128,128]{3,2,1,0:T(8,128)(2,1)}), bf16[8,4,128,128]{3,2,1,0:T(8,128)(2,1)S(1)}, u32[]{:S(2)}, u32[]{:S(2)}) %all-to-all-start.3) | async-done | bytes 1048608 | tf_op jit(solution)/shard_map/all_to_all | solution.py:251
  180.1 1.0 copy-done.1
  181.1 10.3 %shard_map.79 = (bf16[2,8,128,128]{3,2,1,0:T(8,128)(2,1)}, bf16[2,8,128,128]{3,2,1,0:T(8,128)(2,1)}) custom-call(s32[768]{0:T(1024)} %reshape.11.ids, s32[3]{0:T(128)} %pad_add_fusion.place, bf16[8,4,128,128]{3,2,1,0:T(8,128)(2,1)} %copy-done.1, bf16[8,128,128]{2,1,0:T(8,128)(2,1)} %slice.12.gates_in, bf16[8,6,8,32,128]{4,3,2,1,0:T(8,128)(2,1)} %bitcast.30), custom_call_target="tpu_custom_call" | custom-call | flops 1610612736 | bytes 6000000 | tf_op jit(solution)/shard_map/pallas_call | solution.py:360
  191.3 2.1 collective-permute-done.17
  193.4 1.2 add_convert_fusion
  194.7 2.7 %collective-permute-start.18 = (bf16[8,128,128]{2,1,0:T(8,128)(2,1)S(1)}, bf16[8,128,128]{2,1,0:T(8,128)(2,1)S(1)}, u32[]{:S(2)}, u32[]{:S(2)}) collective-permute-start(bf16[8,128,128]{2,1,0:T(8,128)(2,1)S(1)} %slice_bitcast_fusion), channel_id=1, source_target_pairs={{0,2},{2,0},{1,3},{3,1},{4,6},{6,4},{5,7},{7,5},{8,10},{10,8},{9,1... | collective-permute-start | bytes 786440 | tf_op jit(solution)/shard_map/ppermute | solution.py:247
  197.4 7.2 %collective-permute-done.18 = bf16[8,128,128]{2,1,0:T(8,128)(2,1)S(1)} collective-permute-done((bf16[8,128,128]{2,1,0:T(8,128)(2,1)S(1)}, bf16[8,128,128]{2,1,0:T(8,128)(2,1)S(1)}, u32[]{:S(2)}, u32[]{:S(2)}) %collective-permute-start.18) | collective-permute-done | bytes 262176 | tf_op jit(solution)/shard_map/ppermute | solution.py:247
  204.6 0.1 fusion
  204.7 10.4 %all_to_all.25.pieces = bf16[8,128,128]{2,1,0:T(8,128)(2,1)} all-to-all(bf16[8,128,128]{2,1,0:T(8,128)(2,1)S(1)} %fusion), channel_id=1, replica_groups=mesh['z'=8,'yl'=2,'x'=4,'yh'=2,'c'=2] {'yl','x'}, dimensions={0} | all-to-all | bytes 524288 | tf_op jit(solution)/shard_map/all_to_all | solution.py:251
  215.0 1.8 shard_map.80
  (47 shorter events, 0.1 us)
Async XLA Ops:
  6.5 46.5 %all-gather.5.cloned.1.call-start = ((), (), s32[]{:S(2)}) async-start(), calls=%async_computation.5 | async-start | bytes 3538944 | tf_op jit(solution)/shard_map/all_gather | solution.py:273
  7.3 161.2 %all-gather.7.cloned.1.call-start = ((), (), s32[]{:S(2)}) async-start(), calls=%async_computation.6 | async-start | bytes 3538944 | tf_op jit(solution)/shard_map/all_gather | solution.py:338
  8.0 9.8 %collective-permute-start.8 = (bf16[128,1024]{1,0:T(8,128)(2,1)}, bf16[128,1024]{1,0:T(8,128)(2,1)S(1)}, u32[]{:S(2)}, u32[]{:S(2)}) collective-permute-start(bf16[128,1024]{1,0:T(8,128)(2,1)} %f0.1), channel_id=1, source_target_pairs={{0,2},{2,0},{1,3},{3,1},{4,6},{6,4},{5,7},{7,5},{8,10},{10,8},{9,1... | collective-permute-start | bytes 786440 | tf_op jit(solution)/shard_map/ppermute | solution.py:247
  11.3 8.8 %collective-permute-start.7 = (bf16[128,1024]{1,0:T(8,128)(2,1)}, bf16[128,1024]{1,0:T(8,128)(2,1)S(1)}, u32[]{:S(2)}, u32[]{:S(2)}) collective-permute-start(bf16[128,1024]{1,0:T(8,128)(2,1)} %f0.1), channel_id=1, source_target_pairs={{0,1},{1,0},{2,3},{3,2},{4,5},{5,4},{6,7},{7,6},{8,9},{9,8},{10,11... | collective-permute-start | bytes 786440 | tf_op jit(solution)/shard_map/ppermute | solution.py:247
  17.9 2.2 copy-start.4
  17.9 2.2 collective-permute-start.9
  20.1 0.7 copy-start.5
  20.8 0.7 copy-start.6
  24.9 24.5 %all-to-all-start.1 = ((bf16[8,128,640]{2,1,0:T(8,128)(2,1)}), bf16[8,128,640]{2,1,0:T(8,128)(2,1)S(1)}, u32[]{:S(2)}, u32[]{:S(2)}) async-start(bf16[8,128,640]{2,1,0:T(8,128)(2,1)} %shard_map.76), calls=%async_computation.1 | async-start | bytes 2621440 | tf_op jit(solution)/shard_map/all_to_all | solution.py:251
  49.4 3.6 %copy-start = (bf16[8,128,640]{2,1,0:T(8,128)(2,1)}, bf16[8,128,640]{2,1,0:T(8,128)(2,1)S(1)}, u32[]{:S(2)}) copy-start(bf16[8,128,640]{2,1,0:T(8,128)(2,1)S(1)} %all-to-all-done.1.message) | copy-start | bytes 3932164
  49.4 11.5 %all-to-all-start = ((bf16[8,128,128]{2,1,0:T(8,128)(2,1)}), bf16[8,128,128]{2,1,0:T(8,128)(2,1)S(1)}, u32[]{:S(2)}, u32[]{:S(2)}) async-start(bf16[8,128,128]{2,1,0:T(8,128)(2,1)} %shard_map.73), calls=%async_computation | async-start | bytes 524288 | tf_op jit(solution)/shard_map/all_to_all | solution.py:251
  60.9 5.7 %copy-start.2 = (bf16[8,128,128]{2,1,0:T(8,128)(2,1)}, bf16[8,128,128]{2,1,0:T(8,128)(2,1)S(1)}, u32[]{:S(2)}) copy-start(bf16[8,128,128]{2,1,0:T(8,128)(2,1)S(1)} %all-to-all-done.pairs) | copy-start | bytes 786436
  60.9 20.8 %all-to-all-start.2 = ((bf16[8,4,128,128]{3,2,1,0:T(8,128)(2,1)}), bf16[8,4,128,128]{3,2,1,0:T(8,128)(2,1)S(1)}, u32[]{:S(2)}, u32[]{:S(2)}) async-start(bf16[8,4,128,128]{3,2,1,0:T(8,128)(2,1)} %shard_map.77), calls=%async_computation.2 | async-start | bytes 2097152 | tf_op jit(solution)/shard_map/all_to_all | solution.py:251
  68.3 13.6 %collective-permute-start = (bf16[512,128]{1,0:T(8,128)(2,1)}, bf16[512,128]{1,0:T(8,128)(2,1)S(1)}, u32[]{:S(2)}, u32[]{:S(2)}) collective-permute-start(bf16[512,128]{1,0:T(8,128)(2,1)} %bitcast.22), channel_id=1, source_target_pairs={{0,32},{32,64},{64,96},{96,128},{128,160},{160,192},{192,224},{1,3... | collective-permute-start | bytes 393224 | tf_op jit(solution)/shard_map/ppermute | solution.py:256
  71.2 17.7 %collective-permute-start.1 = (bf16[512,128]{1,0:T(8,128)(2,1)}, bf16[512,128]{1,0:T(8,128)(2,1)S(1)}, u32[]{:S(2)}, u32[]{:S(2)}) collective-permute-start(bf16[512,128]{1,0:T(8,128)(2,1)} %bitcast.23), channel_id=1, source_target_pairs={{0,64},{32,96},{64,128},{96,160},{128,192},{160,224},{1,65},{33,97... | collective-permute-start | bytes 393224 | tf_op jit(solution)/shard_map/ppermute | solution.py:256
  72.5 30.3 %collective-permute-start.2 = (bf16[512,128]{1,0:T(8,128)(2,1)}, bf16[512,128]{1,0:T(8,128)(2,1)S(1)}, u32[]{:S(2)}, u32[]{:S(2)}) collective-permute-start(bf16[512,128]{1,0:T(8,128)(2,1)} %bitcast.24), channel_id=1, source_target_pairs={{0,96},{32,128},{64,160},{96,192},{128,224},{1,97},{33,129},{65,16... | collective-permute-start | bytes 393224 | tf_op jit(solution)/shard_map/ppermute | solution.py:256
  73.8 36.2 %collective-permute-start.3 = (bf16[512,128]{1,0:T(8,128)(2,1)}, bf16[512,128]{1,0:T(8,128)(2,1)S(1)}, u32[]{:S(2)}, u32[]{:S(2)}) collective-permute-start(bf16[512,128]{1,0:T(8,128)(2,1)} %bitcast.25), channel_id=1, source_target_pairs={{0,128},{32,160},{64,192},{96,224},{1,129},{33,161},{65,193},{97,2... | collective-permute-start | bytes 393224 | tf_op jit(solution)/shard_map/ppermute | solution.py:256
  75.1 36.2 %collective-permute-start.4 = (bf16[512,128]{1,0:T(8,128)(2,1)}, bf16[512,128]{1,0:T(8,128)(2,1)S(1)}, u32[]{:S(2)}, u32[]{:S(2)}) collective-permute-start(bf16[512,128]{1,0:T(8,128)(2,1)} %bitcast.26), channel_id=1, source_target_pairs={{0,160},{32,192},{64,224},{1,161},{33,193},{65,225},{2,162},{34,19... | collective-permute-start | bytes 393224 | tf_op jit(solution)/shard_map/ppermute | solution.py:256
  81.8 66.6 %copy-start.3 = (bf16[4,128,128]{2,1,0:T(8,128)(2,1)}, bf16[4,128,128]{2,1,0:T(8,128)(2,1)S(1)}, u32[]{:S(2)}) copy-start(bf16[4,128,128]{2,1,0:T(8,128)(2,1)S(1)} %reduce_sum.12) | copy-start | bytes 393220
  81.9 43.6 %copy-start.14 = (bf16[512,128]{1,0:T(8,128)(2,1)}, bf16[512,128]{1,0:T(8,128)(2,1)S(1)}, u32[]{:S(2)}) copy-start(bf16[512,128]{1,0:T(8,128)(2,1)S(1)} %collective-permute-done.k1) | copy-start | bytes 393220
  81.9 30.7 %collective-permute-start.5 = (bf16[512,128]{1,0:T(8,128)(2,1)}, bf16[512,128]{1,0:T(8,128)(2,1)S(1)}, u32[]{:S(2)}, u32[]{:S(2)}) collective-permute-start(bf16[512,128]{1,0:T(8,128)(2,1)} %bitcast.27), channel_id=1, source_target_pairs={{0,192},{32,224},{1,193},{33,225},{2,194},{34,226},{3,195},{35,227... | collective-permute-start | bytes 393224 | tf_op jit(solution)/shard_map/ppermute | solution.py:256
  88.9 36.5 %copy-start.15 = (bf16[512,128]{1,0:T(8,128)(2,1)}, bf16[512,128]{1,0:T(8,128)(2,1)S(1)}, u32[]{:S(2)}) copy-start(bf16[512,128]{1,0:T(8,128)(2,1)S(1)} %collective-permute-done.1.k2) | copy-start | bytes 393220
  88.9 25.0 %collective-permute-start.6 = (bf16[512,128]{1,0:T(8,128)(2,1)}, bf16[512,128]{1,0:T(8,128)(2,1)S(1)}, u32[]{:S(2)}, u32[]{:S(2)}) collective-permute-start(bf16[512,128]{1,0:T(8,128)(2,1)} %bitcast.28), channel_id=1, source_target_pairs={{0,224},{1,225},{2,226},{3,227},{4,228},{5,229},{6,230},{7,231},{8... | collective-permute-start | bytes 393224 | tf_op jit(solution)/shard_map/ppermute | solution.py:256
  102.8 22.7 %copy-start.16 = (bf16[512,128]{1,0:T(8,128)(2,1)}, bf16[512,128]{1,0:T(8,128)(2,1)S(1)}, u32[]{:S(2)}) copy-start(bf16[512,128]{1,0:T(8,128)(2,1)S(1)} %collective-permute-done.2.k3) | copy-start | bytes 393220
  102.8 12.4 %collective-permute-start.10 = (bf16[512,128]{1,0:T(8,128)(2,1)S(1)}, bf16[512,128]{1,0:T(8,128)(2,1)S(1)}, u32[]{:S(2)}, u32[]{:S(2)}) collective-permute-start(bf16[512,128]{1,0:T(8,128)(2,1)S(1)} %bitcast.14), channel_id=1, source_target_pairs={{0,32},{32,64},{64,96},{96,128},{128,160},{160,192},{192,224},{1,3... | collective-permute-start | bytes 393224 | tf_op jit(solution)/shard_map/ppermute | solution.py:256
  110.0 15.5 %copy-start.17 = (bf16[512,128]{1,0:T(8,128)(2,1)}, bf16[512,128]{1,0:T(8,128)(2,1)S(1)}, u32[]{:S(2)}) copy-start(bf16[512,128]{1,0:T(8,128)(2,1)S(1)} %collective-permute-done.3.k4) | copy-start | bytes 393220
  110.0 14.6 %collective-permute-start.11 = (bf16[512,128]{1,0:T(8,128)(2,1)S(1)}, bf16[512,128]{1,0:T(8,128)(2,1)S(1)}, u32[]{:S(2)}, u32[]{:S(2)}) collective-permute-start(bf16[512,128]{1,0:T(8,128)(2,1)S(1)} %bitcast.15), channel_id=1, source_target_pairs={{0,64},{32,96},{64,128},{96,160},{128,192},{160,224},{1,65},{33,97... | collective-permute-start | bytes 393224 | tf_op jit(solution)/shard_map/ppermute | solution.py:256
  111.3 14.2 %copy-start.18 = (bf16[512,128]{1,0:T(8,128)(2,1)}, bf16[512,128]{1,0:T(8,128)(2,1)S(1)}, u32[]{:S(2)}) copy-start(bf16[512,128]{1,0:T(8,128)(2,1)S(1)} %collective-permute-done.4.k5) | copy-start | bytes 393220
  111.3 37.1 %collective-permute-start.12 = (bf16[512,128]{1,0:T(8,128)(2,1)S(1)}, bf16[512,128]{1,0:T(8,128)(2,1)S(1)}, u32[]{:S(2)}, u32[]{:S(2)}) collective-permute-start(bf16[512,128]{1,0:T(8,128)(2,1)S(1)} %bitcast.16), channel_id=1, source_target_pairs={{0,96},{32,128},{64,160},{96,192},{128,224},{1,97},{33,129},{65,16... | collective-permute-start | bytes 393224 | tf_op jit(solution)/shard_map/ppermute | solution.py:256
  112.6 12.9 %copy-start.19 = (bf16[512,128]{1,0:T(8,128)(2,1)}, bf16[512,128]{1,0:T(8,128)(2,1)S(1)}, u32[]{:S(2)}) copy-start(bf16[512,128]{1,0:T(8,128)(2,1)S(1)} %collective-permute-done.5.k6) | copy-start | bytes 393220
  112.6 35.8 %collective-permute-start.13 = (bf16[512,128]{1,0:T(8,128)(2,1)S(1)}, bf16[512,128]{1,0:T(8,128)(2,1)S(1)}, u32[]{:S(2)}, u32[]{:S(2)}) collective-permute-start(bf16[512,128]{1,0:T(8,128)(2,1)S(1)} %bitcast.17), channel_id=1, source_target_pairs={{0,128},{32,160},{64,192},{96,224},{1,129},{33,161},{65,193},{97,2... | collective-permute-start | bytes 393224 | tf_op jit(solution)/shard_map/ppermute | solution.py:256
  113.9 11.6 %copy-start.20 = (bf16[512,128]{1,0:T(8,128)(2,1)}, bf16[512,128]{1,0:T(8,128)(2,1)S(1)}, u32[]{:S(2)}) copy-start(bf16[512,128]{1,0:T(8,128)(2,1)S(1)} %collective-permute-done.6.k7) | copy-start | bytes 393220
  113.9 34.5 %collective-permute-start.14 = (bf16[512,128]{1,0:T(8,128)(2,1)S(1)}, bf16[512,128]{1,0:T(8,128)(2,1)S(1)}, u32[]{:S(2)}, u32[]{:S(2)}) collective-permute-start(bf16[512,128]{1,0:T(8,128)(2,1)S(1)} %bitcast.18), channel_id=1, source_target_pairs={{0,160},{32,192},{64,224},{1,161},{33,193},{65,225},{2,162},{34,19... | collective-permute-start | bytes 393224 | tf_op jit(solution)/shard_map/ppermute | solution.py:256
  115.2 33.2 %copy-start.7 = (bf16[512,128]{1,0:T(8,128)(2,1)}, bf16[512,128]{1,0:T(8,128)(2,1)S(1)}, u32[]{:S(2)}) copy-start(bf16[512,128]{1,0:T(8,128)(2,1)S(1)} %collective-permute-done.10.v1) | copy-start | bytes 393220
  115.2 33.2 %collective-permute-start.15 = (bf16[512,128]{1,0:T(8,128)(2,1)S(1)}, bf16[512,128]{1,0:T(8,128)(2,1)S(1)}, u32[]{:S(2)}, u32[]{:S(2)}) collective-permute-start(bf16[512,128]{1,0:T(8,128)(2,1)S(1)} %bitcast.19), channel_id=1, source_target_pairs={{0,192},{32,224},{1,193},{33,225},{2,194},{34,226},{3,195},{35,227... | collective-permute-start | bytes 393224 | tf_op jit(solution)/shard_map/ppermute | solution.py:256
  124.6 23.8 %copy-start.8 = (bf16[512,128]{1,0:T(8,128)(2,1)}, bf16[512,128]{1,0:T(8,128)(2,1)S(1)}, u32[]{:S(2)}) copy-start(bf16[512,128]{1,0:T(8,128)(2,1)S(1)} %collective-permute-done.11.v2) | copy-start | bytes 393220
  124.6 23.9 %collective-permute-start.16 = (bf16[512,128]{1,0:T(8,128)(2,1)S(1)}, bf16[512,128]{1,0:T(8,128)(2,1)S(1)}, u32[]{:S(2)}, u32[]{:S(2)}) collective-permute-start(bf16[512,128]{1,0:T(8,128)(2,1)S(1)} %bitcast.20), channel_id=1, source_target_pairs={{0,224},{1,225},{2,226},{3,227},{4,228},{5,229},{6,230},{7,231},{8... | collective-permute-start | bytes 393224 | tf_op jit(solution)/shard_map/ppermute | solution.py:256
  148.4 0.7 copy-start.9
  148.4 0.7 copy-start.10
  148.5 0.7 copy-start.11
  148.5 0.7 copy-start.12
  148.5 0.7 copy-start.13
  161.1 18.9 %all-to-all-start.3 = ((bf16[8,4,128,128]{3,2,1,0:T(8,128)(2,1)}), bf16[8,4,128,128]{3,2,1,0:T(8,128)(2,1)S(1)}, u32[]{:S(2)}, u32[]{:S(2)}) async-start(bf16[8,4,128,128]{3,2,1,0:T(8,128)(2,1)} %shard_map.78), calls=%async_computation.3 | async-start | bytes 2097152 | tf_op jit(solution)/shard_map/all_to_all | solution.py:251
  180.1 1.0 copy-start.1
  191.3 2.1 collective-permute-start.17
  194.7 9.9 %collective-permute-start.18 = (bf16[8,128,128]{2,1,0:T(8,128)(2,1)S(1)}, bf16[8,128,128]{2,1,0:T(8,128)(2,1)S(1)}, u32[]{:S(2)}, u32[]{:S(2)}) collective-permute-start(bf16[8,128,128]{2,1,0:T(8,128)(2,1)S(1)} %slice_bitcast_fusion), channel_id=1, source_target_pairs={{0,2},{2,0},{1,3},{3,1},{4,6},{6,4},{5,7},{7,5},{8,10},{10,8},{9,1... | collective-permute-start | bytes 786440 | tf_op jit(solution)/shard_map/ppermute | solution.py:247
Sparse Core Ops, SparseCore 0:
  9.1 43.8 all-gather.4
  54.8 75.9 all-gather.6

commit v2 on v1

--- a/solution.py
+++ b/solution.py
@@ -82,7 +82,8 @@
 
 def key_kernel(pairs, out):
     for q in range(PLANE // 2):
-        out[q] = jnp.concatenate([pairs[2 * q][:, HALF:], pairs[2 * q + 1][:, HALF:]], axis=1)
+        both = jnp.concatenate([pairs[2 * q][:, HALF:], pairs[2 * q + 1][:, HALF:]], axis=1)
+        out[:, q * BLK : (q + 1) * BLK] = both.T
 
 
 def value_kernel(ids, place, message, table, out):
@@ -124,76 +125,90 @@
     lax.fori_loop(0, PLANE // 2, two_blocks, 0)
 
 
-def weight_kernel(place, pairs, k0, k1, k2, k3, k4, k5, k6, k7, probs, sums, scores, tops, totals):
-    block, z = pl.program_id(0), place[2]
-    left = iota((BLK, LANES), 1) < HALF
+def weight_kernel(place, pairs, k0, k1, k2, k3, k4, k5, k6, k7, probs, sums, even, odd, even_top, odd_top, totals):
+    step, z = pl.program_id(0), place[2]
+    block = jnp.minimum(step, PLANE - 1)
     zero = jnp.zeros((BLK, HALF), bf16)
     own = pairs[0][:, :HALF]
     q = jnp.concatenate(
         [jnp.concatenate([own, zero], axis=1), jnp.concatenate([zero, own], axis=1)], axis=0
     )
-    tops[...] = jnp.full(tops.shape, masked_score, f32)
-    totals[...] = jnp.zeros(totals.shape, f32)
-
-    for s, keys in enumerate((k0, k1, k2, k3, k4, k5, k6, k7)):
-
-        @pl.when(s <= z)
-        def _():
-            got = nt_dot(q, keys[...])
-            if s == 0:
-                row, col = iota(got.shape, 0), iota(got.shape, 1)
-                key_pos = (2 * (col >> 7) + (row >> 7)) * BLK + (col & 127)
-                got = jnp.where(key_pos <= block * BLK + (row & 127), got, masked_score)
-            scores[s] = got
-            best = tops[...]
-            for part in range(4):
-                cols = slice(part * LANES, (part + 1) * LANES)
-                best = jnp.maximum(best, jnp.maximum(got[:BLK, cols], got[BLK:, cols]))
-            tops[...] = best
-
-    top = jnp.max(tops[...], axis=1, keepdims=True)
-
-    for s in range(SLABS):
-
-        @pl.when(s <= z)
-        def _():
-            total = totals[...]
-            for bb in range(2):
-                p = jnp.exp(scores[s, bb * BLK : (bb + 1) * BLK, :] - top)
-                for part in range(4):
-                    total = total + p[:, part * LANES : (part + 1) * LANES]
-                probs[s, bb] = p.astype(bf16)
-            totals[...] = total
-
-    sums[...] = jnp.broadcast_to(jnp.sum(totals[...], axis=1, keepdims=True), (BLK, LANES))
-
-
-def attend_kernel(place, probs, sums, v0, v1, v2, v3, v4, v5, v6, v7, out, acc):
+
+    def run(scores, tops, old_scores, old_tops):
+        top = jnp.broadcast_to(jnp.max(old_tops[...], axis=1, keepdims=True), (BLK, LANES))
+        tops[...] = jnp.full((BLK, LANES), masked_score, f32)
+        totals[...] = jnp.zeros(totals.shape, f32)
+        for s, keys in enumerate((k0, k1, k2, k3, k4, k5, k6, k7)):
+
+            @pl.when(s <= z)
+            def _():
+                for c in range(2):
+                    wide = slice(c * 256, (c + 1) * 256)
+                    got = dot(q, keys[:, wide])
+                    if s == 0:
+                        row, col = iota(got.shape, 0), iota(got.shape, 1) + c * 256
+                        key_pos = (2 * (col >> 7) + (row >> 7)) * BLK + (col & 127)
+                        got = jnp.where(key_pos <= block * BLK + (row & 127), got, masked_score)
+                    scores[s, :, wide] = got
+                    tops[...] = jnp.maximum(
+                        tops[...],
+                        jnp.maximum(
+                            jnp.maximum(got[:BLK, :LANES], got[:BLK, LANES:]),
+                            jnp.maximum(got[BLK:, :LANES], got[BLK:, LANES:]),
+                        ),
+                    )
+                    total = totals[...]
+                    for bb in range(2):
+                        for part in range(2 * c, 2 * c + 2):
+                            cols = slice(part * LANES, (part + 1) * LANES)
+                            p = jnp.exp(old_scores[s, bb * BLK : (bb + 1) * BLK, cols] - top)
+                            total = total + p
+                            probs[s, bb, :, cols] = p.astype(bf16)
+                    totals[...] = total
+
+        sums[...] = jnp.broadcast_to(jnp.sum(totals[...], axis=1, keepdims=True), (BLK, LANES))
+
+    @pl.when(step % 2 == 0)
+    def _():
+        run(even, even_top, odd, odd_top)
+
+    @pl.when(step % 2 == 1)
+    def _():
+        run(odd, odd_top, even, even_top)
+
+
+def attend_kernel(near, carried, last, place, probs, *refs):
+    values, refs = refs[: len(near)], refs[len(near) :]
+    acc_in, out, acc = refs[:carried], refs[carried], refs[carried + 1]
     step, z = pl.program_id(0), place[2]
+    left = iota((PLANE * BLK, LANES), 1) < HALF
 
     @pl.when(step == 0)
     def _():
-        acc[...] = jnp.zeros(acc.shape, f32)
-
-    for s, values in enumerate((v0, v1, v2, v3, v4, v5, v6, v7)):
-
-        @pl.when((step == s) & (s <= z))
+        acc[...] = acc_in[0][...] if carried else jnp.zeros(acc.shape, f32)
+
+    for k, s in enumerate(near):
+
+        @pl.when((step == k) & (s <= z))
         def _():
-            for bb in range(2):
-                acc[bb] += dot(probs[0, bb], values[...])
-
-    @pl.when(step == SLABS - 1)
+            got = [dot(probs[0, bb], values[k][...]) for bb in range(2)]
+            acc[...] += jnp.where(left, got[0], got[1])
+
+    @pl.when(step == len(near) - 1)
     def _():
-        left = iota((BLK, LANES), 1) < HALF
-        for q in range(PLANE // 2):
-            pair = []
-            for bb in range(2):
-                rows = slice((2 * q + bb) * BLK, (2 * q + bb + 1) * BLK)
-                o = jnp.where(left, acc[0, rows], acc[1, rows])
-                pair.append((o + pltpu.roll(o, HALF, 1)) / sums[rows])
-            packed = jnp.where(left, pair[0], pair[1]).astype(bf16)
-            for pi in range(PLANE):
-                out[pi, q] = packed
+        if not last:
+            out[...] = acc[...]
+        else:
+            left = iota((BLK, LANES), 1) < HALF
+            for q in range(PLANE // 2):
+                pair = []
+                for bb in range(2):
+                    rows = slice((2 * q + bb) * BLK, (2 * q + bb + 1) * BLK)
+                    o = acc[rows]
+                    pair.append((o + pltpu.roll(o, HALF, 1)) / acc_in[1][rows])
+                packed = jnp.where(left, pair[0], pair[1]).astype(bf16)
+                for pi in range(PLANE):
+                    out[pi, q] = packed
 
 
 def mix_kernel(ids, place, attended, gates_in, table, near, far, lhs, rhs, natural):
@@ -224,10 +239,10 @@
             flat = dot(flat, order).astype(bf16)
             for g in range(4):
                 natural[g] = flat[:, g * LANES : (g + 1) * LANES]
-            near[0, b] = natural[group]
-            far[0, b] = natural[group ^ 1]
-            near[1, b] = natural[group ^ 2]
-            far[1, b] = natural[group ^ 3]
+            core = group & 1
+            for y in range(2):
+                near[y, b] = natural[2 * y + core]
+                far[y, b] = natural[2 * y + (1 - core)]
         return carry
 
     lax.fori_loop(0, PLANE // 2, two_blocks, 0)
@@ -235,11 +250,12 @@
 
 def place_kernel(pieces, out):
     width = out.shape[1] // 2
+    summed = [(pieces[i].astype(f32) + pieces[PLANE + i].astype(f32)).astype(bf16) for i in range(PLANE)]
     for low in range(2):
         own = slice(low * HALF, (low + 1) * HALF)
         for m in range(PLANE // 2):
             out[:, low * width + m * LANES : low * width + (m + 1) * LANES] = jnp.concatenate(
-                [pieces[2 * m][:, own], pieces[2 * m + 1][:, own]], axis=1
+                [summed[2 * m][:, own], summed[2 * m + 1][:, own]], axis=1
             )
 
 
@@ -251,10 +267,15 @@
     return lax.all_to_all(x, PLANE_AXES, split_axis=0, concat_axis=0, tiled=True)
 
 
-def later_slabs(x):
-    return [x] + [
-        lax.ppermute(x, "z", [(i, i + s) for i in range(SLABS - s)]) for s in range(1, SLABS)
-    ]
+def ring(x):
+    up = [(i, (i + 1) % SLABS) for i in range(SLABS)]
+    down = [(i, (i - 1) % SLABS) for i in range(SLABS)]
+    parts = [x] * SLABS
+    for k in range(1, SLABS // 2):
+        parts[k] = lax.ppermute(parts[k - 1], "z", up)
+        parts[SLABS - k] = lax.ppermute(parts[(SLABS - k + 1) % SLABS], "z", down)
+    parts[SLABS // 2] = lax.ppermute(parts[SLABS // 2 - 1], "z", up)
+    return parts
 
 
 def add(a, b):
@@ -278,11 +299,13 @@
         out_specs=vmem,
         cost_estimate=cost(0, 500_000),
     )(queries, keys)
-    pairs = plane_exchange(pairs)
+    features, sent = lax.optimization_barrier((features, pairs))
+    pairs = plane_exchange(sent)
 
     over_y = swap(features, "yh")
     over_c = swap(features, "c")
     over_yc = swap(over_y, "c")
+    over_yc, pairs = lax.optimization_barrier((over_yc, pairs))
     message = pl.pallas_call(
         message_kernel,
         out_shape=jax.ShapeDtypeStruct((PLANE, BLK, 5 * LANES), bf16),
@@ -295,35 +318,15 @@
 
     own_keys = pl.pallas_call(
         key_kernel,
-        out_shape=jax.ShapeDtypeStruct((PLANE // 2, BLK, LANES), bf16),
+        out_shape=jax.ShapeDtypeStruct((LANES, PLANE // 2 * BLK), bf16),
         in_specs=[vmem],
         out_specs=vmem,
         cost_estimate=cost(0, 400_000),
-    )(pairs).reshape(PLANE // 2 * BLK, LANES)
-    key_parts = later_slabs(own_keys)
+    )(pairs)
+    key_parts = ring(own_keys)
+    message, key_parts = lax.optimization_barrier((message, key_parts))
 
     slab = PLANE * BLK
-    probs, sums = pl.pallas_call(
-        weight_kernel,
-        grid=(PLANE,),
-        out_shape=(
-            jax.ShapeDtypeStruct((SLABS, 2, slab, slab // 2), bf16),
-            jax.ShapeDtypeStruct((slab, LANES), f32),
-        ),
-        in_specs=[smem, pl.BlockSpec((1, BLK, LANES), lambda i: (i, 0, 0))] + [vmem] * SLABS,
-        out_specs=(
-            pl.BlockSpec((SLABS, 2, BLK, slab // 2), lambda i: (0, 0, i, 0)),
-            pl.BlockSpec((BLK, LANES), lambda i: (i, 0)),
-        ),
-        scratch_shapes=[
-            pltpu.VMEM((SLABS, 2 * BLK, slab // 2), f32),
-            pltpu.VMEM((BLK, LANES), f32),
-            pltpu.VMEM((BLK, LANES), f32),
-        ],
-        compiler_params=params,
-        cost_estimate=cost(2 * slab * SLABS * slab * 128, 18_000_000, slab * slab * SLABS),
-    )(place, pairs, *key_parts)
-
     partial = pl.pallas_call(
         value_kernel,
         out_shape=jax.ShapeDtypeStruct((PLANE, PLANE // 2, BLK, LANES), bf16),
@@ -332,28 +335,72 @@
         compiler_params=params,
         cost_estimate=cost(2 * 48 * 256 * 256 * 256, 6_000_000),
     )(ids, place, message, value_table)
+    _, pairs = lax.optimization_barrier((partial, pairs))
+    probs, sums = pl.pallas_call(
+        weight_kernel,
+        grid=(PLANE + 1,),
+        out_shape=(
+            jax.ShapeDtypeStruct((SLABS, 2, slab, slab // 2), bf16),
+            jax.ShapeDtypeStruct((slab, LANES), f32),
+        ),
+        in_specs=[smem, pl.BlockSpec((1, BLK, LANES), lambda i: (jnp.minimum(i, PLANE - 1), 0, 0))] + [vmem] * SLABS,
+        out_specs=(
+            pl.BlockSpec((SLABS, 2, BLK, slab // 2), lambda i: (0, 0, jnp.maximum(i - 1, 0), 0)),
+            pl.BlockSpec((BLK, LANES), lambda i: (jnp.maximum(i - 1, 0), 0)),
+        ),
+        scratch_shapes=[
+            pltpu.VMEM((SLABS, 2 * BLK, slab // 2), f32),
+            pltpu.VMEM((SLABS, 2 * BLK, slab // 2), f32),
+            pltpu.VMEM((BLK, LANES), f32),
+            pltpu.VMEM((BLK, LANES), f32),
+            pltpu.VMEM((BLK, LANES), f32),
+        ],
+        compiler_params=params,
+        cost_estimate=cost(2 * slab * SLABS * slab * 128, 18_000_000, slab * slab * SLABS),
+    )(place, pairs, *key_parts)
+
     partial = plane_exchange(partial)
     own_values = jnp.sum(partial.astype(f32), axis=0).astype(bf16).reshape(slab // 2, LANES)
-    value_parts = later_slabs(own_values)
+    own_values, sums = lax.optimization_barrier((own_values, sums))
+    values = ring(own_values)
     output_table = lax.all_gather(output_experts, "z", axis=0, tiled=False)
 
-    attended = pl.pallas_call(
-        attend_kernel,
-        grid_spec=pltpu.PrefetchScalarGridSpec(
-            num_scalar_prefetch=1,
-            grid=(SLABS,),
-            in_specs=[
-                pl.BlockSpec((1, 2, slab, slab // 2), lambda s, at: (jnp.minimum(s, at[2]), 0, 0, 0)),
-                pl.BlockSpec((slab, LANES), lambda s, at: (0, 0)),
-            ]
-            + [pl.BlockSpec((slab // 2, LANES), lambda s, at: (0, 0))] * SLABS,
-            out_specs=pl.BlockSpec((PLANE, PLANE // 2, BLK, LANES), lambda s, at: (0, 0, 0, 0)),
-            scratch_shapes=[pltpu.VMEM((2, slab, LANES), f32)],
-        ),
-        out_shape=jax.ShapeDtypeStruct((PLANE, PLANE // 2, BLK, LANES), bf16),
-        compiler_params=params,
-        cost_estimate=cost(2 * slab * SLABS * slab * 128, 18_000_000),
-    )(place, probs, sums, *value_parts)
+    def weighted(near, carried, last):
+        steps = len(near)
+        full = pl.BlockSpec((slab, LANES), lambda i, at: (0, 0))
+        one = pl.BlockSpec((slab // 2, LANES), lambda i, at: (0, 0))
+
+        def pick(i, at):
+            s = jnp.int32(near[-1])
+            for k in range(steps - 1):
+                s = jnp.where(i == k, near[k], s)
+            return (jnp.where(s <= at[2], s, 0), 0, 0, 0)
+
+        if last:
+            out_shape = jax.ShapeDtypeStruct((PLANE, PLANE // 2, BLK, LANES), bf16)
+            out_spec = pl.BlockSpec(out_shape.shape, lambda i, at: (0, 0, 0, 0))
+        else:
+            out_shape = jax.ShapeDtypeStruct((slab, LANES), f32)
+            out_spec = full
+        return pl.pallas_call(
+            lambda *refs: attend_kernel(near, len(carried), last, *refs),
+            grid_spec=pltpu.PrefetchScalarGridSpec(
+                num_scalar_prefetch=1,
+                grid=(steps,),
+                in_specs=[pl.BlockSpec((1, 2, slab, slab // 2), pick)]
+                + [one] * steps
+                + [full] * len(carried),
+                out_specs=out_spec,
+                scratch_shapes=[pltpu.VMEM((slab, LANES), f32)],
+            ),
+            out_shape=out_shape,
+            compiler_params=params,
+            cost_estimate=cost(steps * 2 * slab * slab * 128, steps * 2_000_000),
+        )(place, probs, *[values[s] for s in near], *carried)
+
+    acc = weighted((0, 1, 7), (), False)
+    acc = weighted((2, 6, 3, 5), (acc,), False)
+    attended = weighted((4,), (acc, sums), True)
     attended = plane_exchange(attended)
 
     half_out = jax.ShapeDtypeStruct((2, PLANE, BLK, LANES), bf16)
@@ -371,8 +418,9 @@
         cost_estimate=cost(2 * 48 * 256 * 256 * 256, 6_000_000),
     )(ids, place, attended, message[:, :, 4 * LANES :], output_table)
     near = add(near, swap(far, "c"))
-    mixed = add(near[0], swap(near[1], "yh"))
-    mixed = plane_exchange(mixed)
+    mixed = lax.all_to_all(
+        near.reshape(2 * PLANE, BLK, LANES), ("yh",) + PLANE_AXES, split_axis=0, concat_axis=0, tiled=True
+    )
     return pl.pallas_call(
         place_kernel,
         out_shape=jax.ShapeDtypeStruct(features.shape, bf16),

time: 225 us -> 204 us (0.907)
  the two profiles are of different devices: /device:TPU:192 before, /device:TPU:224 now
where the time goes in v2:
time: 204 us; the launch traced here: 203 us
  Pallas kernels  68.8 us (34%)
  waiting for transfers between devices  50.7 us (25%)
  starting transfers between devices  43.4 us (21%)
  blocking collectives  16.2 us (8%)
  between operations  13.6 us (7%)
  local copies, waits for them, and re-layouts  8.13 us (4%)
    pallas_call x1, Pallas kernels, body(): pl.pallas_call(weight_kernel, grid=(PLANE + 1,), out_shape=(jax.ShapeDtyp...  23.3 us
    ppermute x6, waiting for transfers between devices, ring(): parts[k] = lax.ppermute(parts[k - 1], 'z', up)  22.5 us
    all_to_all x4, starting transfers between devices, plane_exchange(): lax.all_to_all(x, PLANE_AXES, split_axis=0, concat_axis=0, tiled=True)  19.6 us
    pallas_call x3, Pallas kernels, weighted(): pl.pallas_call(lambda *refs: attend_kernel(near, len(carried), last, *ref...  18.3 us
    all_to_all x1, blocking collectives, body(): lax.all_to_all(near.reshape(2 * PLANE, BLK, LANES), ('yh',) + PLANE_AXES,...  16.2 us
    all_to_all x4, waiting for transfers between devices, plane_exchange(): lax.all_to_all(x, PLANE_AXES, split_axis=0, concat_axis=0, tiled=True)  15 us
    pallas_call x1, Pallas kernels, body(): pl.pallas_call(mix_kernel, out_shape=(half_out, half_out), in_specs=[smem...  10.3 us
    ppermute x4, waiting for transfers between devices, swap(): return lax.ppermute(x, axis, [(0, 1), (1, 0)])  8.69 us
  transfers between devices with their start and end apart: 24, of which 13 were waited for; matrix products, arithmetic and copies ran while one was open for 2% of the time, Pallas kernels for 28%

profile of v2, /device:TPU:224, one launch (start us, length us, event | category | flops | bytes accessed | tf_op | source)
XLA Modules:
  0.0 202.8 jit_solution(14019814815978336164)
XLA Ops:
  6.5 0.7 all-gather.5.cloned.1.call-update
  7.3 0.0 all-gather.7.cloned.1.call-start
  7.3 0.7 all-gather.7.cloned.1.call-update
  8.0 1.8 shard_map.73
  9.8 3.2 %collective-permute-start.1 = (bf16[128,1024]{1,0:T(8,128)(2,1)}, bf16[128,1024]{1,0:T(8,128)(2,1)S(1)}, u32[]{:S(2)}, u32[]{:S(2)}) collective-permute-start(bf16[128,1024]{1,0:T(8,128)(2,1)} %f0), channel_id=1, source_target_pairs={{0,2},{2,0},{1,3},{3,1},{4,6},{6,4},{5,7},{7,5},{8,10},{10,8},{9,1... | collective-permute-start | bytes 786440 | tf_op jit(solution)/shard_map/ppermute | solution.py:263
  13.0 6.6 %collective-permute-done.1.f2 = bf16[128,1024]{1,0:T(8,128)(2,1)S(1)} collective-permute-done((bf16[128,1024]{1,0:T(8,128)(2,1)}, bf16[128,1024]{1,0:T(8,128)(2,1)S(1)}, u32[]{:S(2)}, u32[]{:S(2)}) %collective-permute-start.1) | collective-permute-done | bytes 262176 | tf_op jit(solution)/shard_map/ppermute | solution.py:263
  19.5 0.0 collective-permute-start.2
  19.5 0.5 collective-permute-start
  20.0 5.3 %all-to-all-start = ((bf16[8,128,128]{2,1,0:T(8,128)(2,1)}), bf16[8,128,128]{2,1,0:T(8,128)(2,1)S(1)}, u32[]{:S(2)}, u32[]{:S(2)}) async-start(bf16[8,128,128]{2,1,0:T(8,128)(2,1)} %shard_map.73), calls=%async_computation | async-start | bytes 524288 | tf_op jit(solution)/shard_map/all_to_all | solution.py:267
  25.4 0.9 copy.9
  26.2 0.7 reshape.9.ids
  26.9 0.7 pad_add_fusion.place.refs_0_
  27.6 5.2 %all-to-all-done.pairs = bf16[8,128,128]{2,1,0:T(8,128)(2,1)S(1)} async-done(((bf16[8,128,128]{2,1,0:T(8,128)(2,1)}), bf16[8,128,128]{2,1,0:T(8,128)(2,1)S(1)}, u32[]{:S(2)}, u32[]{:S(2)}) %all-to-all-start) | async-done | bytes 262176 | tf_op jit(solution)/shard_map/all_to_all | solution.py:267
  32.8 0.0 collective-permute-done.2.f3
  32.8 0.0 collective-permute-done.f1
  32.8 0.7 copy-done.5
  33.5 0.7 copy-done.6
  34.2 3.4 %shard_map.74 = bf16[8,128,640]{2,1,0:T(8,128)(2,1)} custom-call(s32[768]{0:T(1024)} %reshape.9.ids, s32[3]{0:T(128)} %pad_add_fusion.place.refs_0_, bf16[128,1024]{1,0:T(8,128)(2,1)} %f0, bf16[128,1024]{1,0:T(8,128)(2,1)} %copy-done.6, bf16[128,1024]{1,0:T(8,128)(2,1)} %copy-done.4, bf16[128,1024]{1,0:T(8,128)(2,1)} %copy-done.5, bf16[48,4096]{1,0:T(8,128)(2,1)} %router.1), custom_call_target="tpu_custom_call" | custom-call | flops 268435456 | bytes 3000000 | tf_op jit(solution)/shard_map/pallas_call | solution.py:309
  37.7 3.6 %all-to-all-start.1 = ((bf16[8,128,640]{2,1,0:T(8,128)(2,1)}), bf16[8,128,640]{2,1,0:T(8,128)(2,1)S(1)}, u32[]{:S(2)}, u32[]{:S(2)}) async-start(bf16[8,128,640]{2,1,0:T(8,128)(2,1)} %shard_map.74), calls=%async_computation.1 | async-start | bytes 2621440 | tf_op jit(solution)/shard_map/all_to_all | solution.py:267
  41.3 1.8 shard_map.75.k0
  43.0 0.0 collective-permute-start.3
  43.0 2.0 collective-permute-start.7
  45.1 6.4 %collective-permute-done.3.k1 = bf16[128,512]{1,0:T(8,128)(2,1)S(1)} collective-permute-done((bf16[128,512]{1,0:T(8,128)(2,1)}, bf16[128,512]{1,0:T(8,128)(2,1)S(1)}, u32[]{:S(2)}, u32[]{:S(2)}) %collective-permute-start.3) | collective-permute-done | bytes 131104 | tf_op jit(solution)/shard_map/ppermute | solution.py:275
  51.5 1.4 collective-permute-start.4
  52.9 0.6 collective-permute-start.8
  53.5 4.1 %collective-permute-done.4.k2 = bf16[128,512]{1,0:T(8,128)(2,1)S(1)} collective-permute-done((bf16[128,512]{1,0:T(8,128)(2,1)S(1)}, bf16[128,512]{1,0:T(8,128)(2,1)S(1)}, u32[]{:S(2)}, u32[]{:S(2)}) %collective-permute-start.4) | collective-permute-done | bytes 131104 | tf_op jit(solution)/shard_map/ppermute | solution.py:275
  57.6 1.9 collective-permute-start.5
  59.5 0.2 collective-permute-start.9
  59.7 2.9 %collective-permute-done.5.k3 = bf16[128,512]{1,0:T(8,128)(2,1)S(1)} collective-permute-done((bf16[128,512]{1,0:T(8,128)(2,1)S(1)}, bf16[128,512]{1,0:T(8,128)(2,1)S(1)}, u32[]{:S(2)}, u32[]{:S(2)}) %collective-permute-start.5) | collective-permute-done | bytes 131104 | tf_op jit(solution)/shard_map/ppermute | solution.py:275
  62.6 3.1 %collective-permute-start.6 = (bf16[128,512]{1,0:T(8,128)(2,1)S(1)}, bf16[128,512]{1,0:T(8,128)(2,1)S(1)}, u32[]{:S(2)}, u32[]{:S(2)}) collective-permute-start(bf16[128,512]{1,0:T(8,128)(2,1)S(1)} %collective-permute-done.5.k3), channel_id=1, source_target_pairs={{0,32},{32,64},{64,96},{96,128},{128,160},{160,192},{192,224},{224... | collective-permute-start | bytes 393224 | tf_op jit(solution)/shard_map/ppermute | solution.py:277
  65.7 0.0 collective-permute-done.9.k5
  65.7 2.5 %collective-permute-done.6.k4 = bf16[128,512]{1,0:T(8,128)(2,1)S(1)} collective-permute-done((bf16[128,512]{1,0:T(8,128)(2,1)S(1)}, bf16[128,512]{1,0:T(8,128)(2,1)S(1)}, u32[]{:S(2)}, u32[]{:S(2)}) %collective-permute-start.6) | collective-permute-done | bytes 131104 | tf_op jit(solution)/shard_map/ppermute | solution.py:277
  68.2 0.0 all-gather.5.cloned.1.call-done
  68.2 1.1 copy-done
  69.3 8.0 %shard_map.76 = bf16[8,4,128,128]{3,2,1,0:T(8,128)(2,1)} custom-call(s32[768]{0:T(1024)} %reshape.9.ids, s32[3]{0:T(128)} %pad_add_fusion.place.refs_0_, bf16[8,128,640]{2,1,0:T(8,128)(2,1)} %copy-done, bf16[8,6,8,32,128]{4,3,2,1,0:T(8,128)(2,1)} %bitcast.12), custom_call_target="tpu_custom_call" | custom-call | flops 1610612736 | bytes 6000000 | tf_op jit(solution)/shard_map/pallas_call | solution.py:330
  77.3 5.2 %all-to-all-start.2 = ((bf16[8,4,128,128]{3,2,1,0:T(8,128)(2,1)}), bf16[8,4,128,128]{3,2,1,0:T(8,128)(2,1)S(1)}, u32[]{:S(2)}, u32[]{:S(2)}) async-start(bf16[8,4,128,128]{3,2,1,0:T(8,128)(2,1)} %shard_map.76), calls=%async_computation.2 | async-start | bytes 2097152 | tf_op jit(solution)/shard_map/all_to_all | solution.py:267
  82.5 23.3 %shard_map.77 = (bf16[8,2,1024,512]{3,2,1,0:T(8,128)(2,1)}, f32[1024,128]{1,0:T(8,128)}) custom-call(s32[3]{0:T(128)} %pad_add_fusion.place.refs_0_, bf16[8,128,128]{2,1,0:T(8,128)(2,1)} %copy-done.2, bf16[128,512]{1,0:T(8,128)(2,1)} %shard_map.75.k0, bf16[128,512]{1,0:T(8,128)(2,1)} %copy-done.14, bf16[128,512]{1,0:T(8,128)(2,1)} %copy-done.16, ...), custom_call_target="tpu_custom_call" | custom-call | flops 2147483648 | bytes 18000000 | tf_op jit(solution)/shard_map/pallas_call | solution.py:339
  105.9 0.2 reduce_sum.12
  106.1 0.1 collective-permute-start.10
  106.1 2.0 collective-permute-start.14
  108.2 3.6 %collective-permute-done.10.refs_3_ = bf16[512,128]{1,0:T(8,128)(2,1)S(1)} collective-permute-done((bf16[512,128]{1,0:T(8,128)(2,1)S(1)}, bf16[512,128]{1,0:T(8,128)(2,1)S(1)}, u32[]{:S(2)}, u32[]{:S(2)}) %collective-permute-start.10) | collective-permute-done | bytes 131104 | tf_op jit(solution)/shard_map/ppermute | solution.py:275
  111.7 1.3 collective-permute-start.11
  113.1 0.4 collective-permute-done.14.refs_4_
  113.5 0.3 collective-permute-start.15
  113.8 2.9 %collective-permute-done.11.refs_2_ = bf16[512,128]{1,0:T(8,128)(2,1)S(1)} collective-permute-done((bf16[512,128]{1,0:T(8,128)(2,1)S(1)}, bf16[512,128]{1,0:T(8,128)(2,1)S(1)}, u32[]{:S(2)}, u32[]{:S(2)}) %collective-permute-start.11) | collective-permute-done | bytes 131104 | tf_op jit(solution)/shard_map/ppermute | solution.py:275
  116.7 3.5 %collective-permute-start.12 = (bf16[512,128]{1,0:T(8,128)(2,1)S(1)}, bf16[512,128]{1,0:T(8,128)(2,1)S(1)}, u32[]{:S(2)}, u32[]{:S(2)}) collective-permute-start(bf16[512,128]{1,0:T(8,128)(2,1)S(1)} %collective-permute-done.11.refs_2_), channel_id=1, source_target_pairs={{0,32},{32,64},{64,96},{96,128},{128,160},{160,192},{192,224},{224... | collective-permute-start | bytes 393224 | tf_op jit(solution)/shard_map/ppermute | solution.py:275
  120.2 0.1 collective-permute-done.15.refs_3_
  120.2 0.0 collective-permute-start.16
  120.2 2.5 %collective-permute-done.12.refs_4_ = bf16[512,128]{1,0:T(8,128)(2,1)S(1)} collective-permute-done((bf16[512,128]{1,0:T(8,128)(2,1)S(1)}, bf16[512,128]{1,0:T(8,128)(2,1)S(1)}, u32[]{:S(2)}, u32[]{:S(2)}) %collective-permute-start.12) | collective-permute-done | bytes 131104 | tf_op jit(solution)/shard_map/ppermute | solution.py:275
  122.8 3.7 %collective-permute-start.13 = (bf16[512,128]{1,0:T(8,128)(2,1)S(1)}, bf16[512,128]{1,0:T(8,128)(2,1)S(1)}, u32[]{:S(2)}, u32[]{:S(2)}) collective-permute-start(bf16[512,128]{1,0:T(8,128)(2,1)S(1)} %collective-permute-done.12.refs_4_), channel_id=1, source_target_pairs={{0,32},{32,64},{64,96},{96,128},{128,160},{160,192},{192,224},{224... | collective-permute-start | bytes 393224 | tf_op jit(solution)/shard_map/ppermute | solution.py:277
  126.5 6.2 %shard_map.78.refs_6_ = f32[1024,128]{1,0:T(8,128)} custom-call(s32[3]{0:T(128)} %pad_add_fusion.place.refs_0_, bf16[8,2,1024,512]{3,2,1,0:T(8,128)(2,1)} %get-tuple-element.39.refs_1_, bf16[512,128]{1,0:T(8,128)(2,1)} %bitcast.10, bf16[512,128]{1,0:T(8,128)(2,1)} %copy-done.7, bf16[512,128]{1,0:T(8,128)(2,1)} %copy-done.8), custom_call_target="tpu_custom_call" | custom-call | flops 805306368 | bytes 6000000 | tf_op jit(solution)/shard_map/pallas_call | solution.py:385
  132.7 0.7 copy-done.13
  133.4 7.4 %shard_map.79.refs_3_ = f32[1024,128]{1,0:T(8,128)} custom-call(s32[3]{0:T(128)} %pad_add_fusion.place.refs_0_, bf16[8,2,1024,512]{3,2,1,0:T(8,128)(2,1)} %get-tuple-element.39.refs_1_, bf16[512,128]{1,0:T(8,128)(2,1)} %copy-done.9, bf16[512,128]{1,0:T(8,128)(2,1)} %copy-done.10, bf16[512,128]{1,0:T(8,128)(2,1)} %copy-done.11, bf16[512,128]{1,0:T(8,128)(2,1)} %copy-done.13, ...), custom_call_target="tpu_custom_call" | custom-call | flops 1073741824 | bytes 8000000 | tf_op jit(solution)/shard_map/pallas_call | solution.py:385
  140.8 0.7 copy-done.12
  141.4 4.7 %shard_map.80 = bf16[8,4,128,128]{3,2,1,0:T(8,128)(2,1)} custom-call(s32[3]{0:T(128)} %pad_add_fusion.place.refs_0_, bf16[8,2,1024,512]{3,2,1,0:T(8,128)(2,1)} %get-tuple-element.39.refs_1_, bf16[512,128]{1,0:T(8,128)(2,1)} %copy-done.12, f32[1024,128]{1,0:T(8,128)} %shard_map.79.refs_3_, f32[1024,128]{1,0:T(8,128)} %get-tuple-element.42.refs_4_), custom_call_target="tpu_custom_call" | custom-call | flops 268435456 | bytes 2000000 | tf_op jit(solution)/shard_map/pallas_call | solution.py:385
  146.2 5.5 %all-to-all-start.3 = ((bf16[8,4,128,128]{3,2,1,0:T(8,128)(2,1)}), bf16[8,4,128,128]{3,2,1,0:T(8,128)(2,1)S(1)}, u32[]{:S(2)}, u32[]{:S(2)}) async-start(bf16[8,4,128,128]{3,2,1,0:T(8,128)(2,1)} %shard_map.80), calls=%async_computation.3 | async-start | bytes 2097152 | tf_op jit(solution)/shard_map/all_to_all | solution.py:267
  151.7 1.7 slice.3.gates_in
  153.4 9.8 %all-to-all-done.3.attended = bf16[8,4,128,128]{3,2,1,0:T(8,128)(2,1)S(1)} async-done(((bf16[8,4,128,128]{3,2,1,0:T(8,128)(2,1)}), bf16[8,4,128,128]{3,2,1,0:T(8,128)(2,1)S(1)}, u32[]{:S(2)}, u32[]{:S(2)}) %all-to-all-start.3) | async-done | bytes 1048608 | tf_op jit(solution)/shard_map/all_to_all | solution.py:267
  163.2 1.0 copy-done.1
  164.2 10.3 %shard_map.81 = (bf16[2,8,128,128]{3,2,1,0:T(8,128)(2,1)}, bf16[2,8,128,128]{3,2,1,0:T(8,128)(2,1)}) custom-call(s32[768]{0:T(1024)} %reshape.9.ids, s32[3]{0:T(128)} %pad_add_fusion.place.refs_0_, bf16[8,4,128,128]{3,2,1,0:T(8,128)(2,1)} %copy-done.1, bf16[8,128,128]{2,1,0:T(8,128)(2,1)} %slice.3.gates_in, bf16[8,6,8,32,128]{4,3,2,1,0:T(8,128)(2,1)} %bitcast.11), custom_call_target="tpu_custom_call" | custom-call | flops 1610612736 | bytes 6000000 | tf_op jit(solution)/shard_map/pallas_call | solution.py:407
  174.5 2.1 %collective-permute-done.17 = bf16[2,8,128,128]{3,2,1,0:T(8,128)(2,1)S(1)} collective-permute-done((bf16[2,8,128,128]{3,2,1,0:T(8,128)(2,1)}, bf16[2,8,128,128]{3,2,1,0:T(8,128)(2,1)S(1)}, u32[]{:S(2)}, u32[]{:S(2)}) %collective-permute-start.17) | collective-permute-done | bytes 524320 | tf_op jit(solution)/shard_map/ppermute | solution.py:263
  176.6 1.2 add_convert_fusion
  177.8 16.2 %all_to_all.25.pieces = bf16[16,128,128]{2,1,0:T(8,128)(2,1)} all-to-all(bf16[16,128,128]{2,1,0:T(8,128)(2,1)S(1)} %bitcast.7), channel_id=1, replica_groups=mesh['z'=8,'yl'=2,'x'=4,'yh'=2,'c'=2] {'yh','yl','x'}, dimensions={0} | all-to-all | bytes 1048576 | tf_op jit(solution)/shard_map/all_to_all | solution.py:421
  194.0 1.9 shard_map.82
  (45 shorter events, 0.1 us)
Async XLA Ops:
  6.5 61.7 %all-gather.5.cloned.1.call-start = ((), (), s32[]{:S(2)}) async-start(), calls=%async_computation.5 | async-start | bytes 3538944 | tf_op jit(solution)/shard_map/all_gather | solution.py:294
  7.3 146.1 %all-gather.7.cloned.1.call-start = ((), (), s32[]{:S(2)}) async-start(), calls=%async_computation.6 | async-start | bytes 3538944 | tf_op jit(solution)/shard_map/all_gather | solution.py:366
  9.8 9.8 %collective-permute-start.1 = (bf16[128,1024]{1,0:T(8,128)(2,1)}, bf16[128,1024]{1,0:T(8,128)(2,1)S(1)}, u32[]{:S(2)}, u32[]{:S(2)}) collective-permute-start(bf16[128,1024]{1,0:T(8,128)(2,1)} %f0), channel_id=1, source_target_pairs={{0,2},{2,0},{1,3},{3,1},{4,6},{6,4},{5,7},{7,5},{8,10},{10,8},{9,1... | collective-permute-start | bytes 786440 | tf_op jit(solution)/shard_map/ppermute | solution.py:263
  19.5 13.3 %copy-start.4 = (bf16[128,1024]{1,0:T(8,128)(2,1)}, bf16[128,1024]{1,0:T(8,128)(2,1)S(1)}, u32[]{:S(2)}) copy-start(bf16[128,1024]{1,0:T(8,128)(2,1)S(1)} %collective-permute-done.1.f2) | copy-start | bytes 786436
  19.5 13.3 %collective-permute-start.2 = (bf16[128,1024]{1,0:T(8,128)(2,1)S(1)}, bf16[128,1024]{1,0:T(8,128)(2,1)S(1)}, u32[]{:S(2)}, u32[]{:S(2)}) collective-permute-start(bf16[128,1024]{1,0:T(8,128)(2,1)S(1)} %collective-permute-done.1.f2), channel_id=1, source_target_pairs={{0,1},{1,0},{2,3},{3,2},{4,5},{5,4},{6,7},{7,6},{8,9},{9,8},{10,11... | collective-permute-start | bytes 786440 | tf_op jit(solution)/shard_map/ppermute | solution.py:263
  19.5 13.3 %collective-permute-start = (bf16[128,1024]{1,0:T(8,128)(2,1)}, bf16[128,1024]{1,0:T(8,128)(2,1)S(1)}, u32[]{:S(2)}, u32[]{:S(2)}) collective-permute-start(bf16[128,1024]{1,0:T(8,128)(2,1)} %f0), channel_id=1, source_target_pairs={{0,1},{1,0},{2,3},{3,2},{4,5},{5,4},{6,7},{7,6},{8,9},{9,8},{10,11... | collective-permute-start | bytes 786440 | tf_op jit(solution)/shard_map/ppermute | solution.py:263
  20.0 12.8 %all-to-all-start = ((bf16[8,128,128]{2,1,0:T(8,128)(2,1)}), bf16[8,128,128]{2,1,0:T(8,128)(2,1)S(1)}, u32[]{:S(2)}, u32[]{:S(2)}) async-start(bf16[8,128,128]{2,1,0:T(8,128)(2,1)} %shard_map.73), calls=%async_computation | async-start | bytes 524288 | tf_op jit(solution)/shard_map/all_to_all | solution.py:267
  32.8 8.4 %copy-start.2 = (bf16[8,128,128]{2,1,0:T(8,128)(2,1)}, bf16[8,128,128]{2,1,0:T(8,128)(2,1)S(1)}, u32[]{:S(2)}) copy-start(bf16[8,128,128]{2,1,0:T(8,128)(2,1)S(1)} %all-to-all-done.pairs) | copy-start | bytes 786436
  32.8 0.7 copy-start.5
  33.5 0.7 copy-start.6
  37.7 30.6 %all-to-all-start.1 = ((bf16[8,128,640]{2,1,0:T(8,128)(2,1)}), bf16[8,128,640]{2,1,0:T(8,128)(2,1)S(1)}, u32[]{:S(2)}, u32[]{:S(2)}) async-start(bf16[8,128,640]{2,1,0:T(8,128)(2,1)} %shard_map.74), calls=%async_computation.1 | async-start | bytes 2621440 | tf_op jit(solution)/shard_map/all_to_all | solution.py:267
  43.0 8.4 %collective-permute-start.3 = (bf16[128,512]{1,0:T(8,128)(2,1)}, bf16[128,512]{1,0:T(8,128)(2,1)S(1)}, u32[]{:S(2)}, u32[]{:S(2)}) collective-permute-start(bf16[128,512]{1,0:T(8,128)(2,1)} %shard_map.75.k0), channel_id=1, source_target_pairs={{0,32},{32,64},{64,96},{96,128},{128,160},{160,192},{192,224},{224... | collective-permute-start | bytes 393224 | tf_op jit(solution)/shard_map/ppermute | solution.py:275
  43.0 9.9 %collective-permute-start.7 = (bf16[128,512]{1,0:T(8,128)(2,1)}, bf16[128,512]{1,0:T(8,128)(2,1)S(1)}, u32[]{:S(2)}, u32[]{:S(2)}) collective-permute-start(bf16[128,512]{1,0:T(8,128)(2,1)} %shard_map.75.k0), channel_id=1, source_target_pairs={{0,224},{32,0},{64,32},{96,64},{128,96},{160,128},{192,160},{224,1... | collective-permute-start | bytes 393224 | tf_op jit(solution)/shard_map/ppermute | solution.py:276
  51.5 31.0 %copy-start.14 = (bf16[128,512]{1,0:T(8,128)(2,1)}, bf16[128,512]{1,0:T(8,128)(2,1)S(1)}, u32[]{:S(2)}) copy-start(bf16[128,512]{1,0:T(8,128)(2,1)S(1)} %collective-permute-done.3.k1) | copy-start | bytes 393220
  51.5 6.2 %collective-permute-start.4 = (bf16[128,512]{1,0:T(8,128)(2,1)S(1)}, bf16[128,512]{1,0:T(8,128)(2,1)S(1)}, u32[]{:S(2)}, u32[]{:S(2)}) collective-permute-start(bf16[128,512]{1,0:T(8,128)(2,1)S(1)} %collective-permute-done.3.k1), channel_id=1, source_target_pairs={{0,32},{32,64},{64,96},{96,128},{128,160},{160,192},{192,224},{224... | collective-permute-start | bytes 393224 | tf_op jit(solution)/shard_map/ppermute | solution.py:275
  52.9 29.6 %copy-start.15 = (bf16[128,512]{1,0:T(8,128)(2,1)}, bf16[128,512]{1,0:T(8,128)(2,1)S(1)}, u32[]{:S(2)}) copy-start(bf16[128,512]{1,0:T(8,128)(2,1)S(1)} %collective-permute-done.7.k7) | copy-start | bytes 393220
  52.9 6.6 %collective-permute-start.8 = (bf16[128,512]{1,0:T(8,128)(2,1)S(1)}, bf16[128,512]{1,0:T(8,128)(2,1)S(1)}, u32[]{:S(2)}, u32[]{:S(2)}) collective-permute-start(bf16[128,512]{1,0:T(8,128)(2,1)S(1)} %collective-permute-done.7.k7), channel_id=1, source_target_pairs={{0,224},{32,0},{64,32},{96,64},{128,96},{160,128},{192,160},{224,1... | collective-permute-start | bytes 393224 | tf_op jit(solution)/shard_map/ppermute | solution.py:276
  57.6 24.9 %copy-start.16 = (bf16[128,512]{1,0:T(8,128)(2,1)}, bf16[128,512]{1,0:T(8,128)(2,1)S(1)}, u32[]{:S(2)}) copy-start(bf16[128,512]{1,0:T(8,128)(2,1)S(1)} %collective-permute-done.4.k2) | copy-start | bytes 393220
  57.6 5.0 %collective-permute-start.5 = (bf16[128,512]{1,0:T(8,128)(2,1)S(1)}, bf16[128,512]{1,0:T(8,128)(2,1)S(1)}, u32[]{:S(2)}, u32[]{:S(2)}) collective-permute-start(bf16[128,512]{1,0:T(8,128)(2,1)S(1)} %collective-permute-done.4.k2), channel_id=1, source_target_pairs={{0,32},{32,64},{64,96},{96,128},{128,160},{160,192},{192,224},{224... | collective-permute-start | bytes 393224 | tf_op jit(solution)/shard_map/ppermute | solution.py:275
  59.5 23.0 %copy-start.17 = (bf16[128,512]{1,0:T(8,128)(2,1)}, bf16[128,512]{1,0:T(8,128)(2,1)S(1)}, u32[]{:S(2)}) copy-start(bf16[128,512]{1,0:T(8,128)(2,1)S(1)} %collective-permute-done.8.k6) | copy-start | bytes 393220
  59.5 6.2 %collective-permute-start.9 = (bf16[128,512]{1,0:T(8,128)(2,1)S(1)}, bf16[128,512]{1,0:T(8,128)(2,1)S(1)}, u32[]{:S(2)}, u32[]{:S(2)}) collective-permute-start(bf16[128,512]{1,0:T(8,128)(2,1)S(1)} %collective-permute-done.8.k6), channel_id=1, source_target_pairs={{0,224},{32,0},{64,32},{96,64},{128,96},{160,128},{192,160},{224,1... | collective-permute-start | bytes 393224 | tf_op jit(solution)/shard_map/ppermute | solution.py:276
  62.6 19.9 %copy-start.18 = (bf16[128,512]{1,0:T(8,128)(2,1)}, bf16[128,512]{1,0:T(8,128)(2,1)S(1)}, u32[]{:S(2)}) copy-start(bf16[128,512]{1,0:T(8,128)(2,1)S(1)} %collective-permute-done.5.k3) | copy-start | bytes 393220
  62.6 5.6 %collective-permute-start.6 = (bf16[128,512]{1,0:T(8,128)(2,1)S(1)}, bf16[128,512]{1,0:T(8,128)(2,1)S(1)}, u32[]{:S(2)}, u32[]{:S(2)}) collective-permute-start(bf16[128,512]{1,0:T(8,128)(2,1)S(1)} %collective-permute-done.5.k3), channel_id=1, source_target_pairs={{0,32},{32,64},{64,96},{96,128},{128,160},{160,192},{192,224},{224... | collective-permute-start | bytes 393224 | tf_op jit(solution)/shard_map/ppermute | solution.py:277
  65.7 16.8 %copy-start.19 = (bf16[128,512]{1,0:T(8,128)(2,1)}, bf16[128,512]{1,0:T(8,128)(2,1)S(1)}, u32[]{:S(2)}) copy-start(bf16[128,512]{1,0:T(8,128)(2,1)S(1)} %collective-permute-done.9.k5) | copy-start | bytes 393220
  68.2 14.3 %copy-start.20 = (bf16[128,512]{1,0:T(8,128)(2,1)}, bf16[128,512]{1,0:T(8,128)(2,1)S(1)}, u32[]{:S(2)}) copy-start(bf16[128,512]{1,0:T(8,128)(2,1)S(1)} %collective-permute-done.6.k4) | copy-start | bytes 393220
  68.2 1.1 copy-start
  77.3 28.6 %all-to-all-start.2 = ((bf16[8,4,128,128]{3,2,1,0:T(8,128)(2,1)}), bf16[8,4,128,128]{3,2,1,0:T(8,128)(2,1)S(1)}, u32[]{:S(2)}, u32[]{:S(2)}) async-start(bf16[8,4,128,128]{3,2,1,0:T(8,128)(2,1)} %shard_map.76), calls=%async_computation.2 | async-start | bytes 2097152 | tf_op jit(solution)/shard_map/all_to_all | solution.py:267
  106.0 20.4 %copy-start.3 = (bf16[4,128,128]{2,1,0:T(8,128)(2,1)}, bf16[4,128,128]{2,1,0:T(8,128)(2,1)S(1)}, u32[]{:S(2)}) copy-start(bf16[4,128,128]{2,1,0:T(8,128)(2,1)S(1)} %reduce_sum.12) | copy-start | bytes 393220
  106.1 5.7 %collective-permute-start.10 = (bf16[512,128]{1,0:T(8,128)(2,1)S(1)}, bf16[512,128]{1,0:T(8,128)(2,1)S(1)}, u32[]{:S(2)}, u32[]{:S(2)}) collective-permute-start(bf16[512,128]{1,0:T(8,128)(2,1)S(1)} %bitcast.8), channel_id=1, source_target_pairs={{0,32},{32,64},{64,96},{96,128},{128,160},{160,192},{192,224},{224... | collective-permute-start | bytes 393224 | tf_op jit(solution)/shard_map/ppermute | solution.py:275
  106.1 7.3 %collective-permute-start.14 = (bf16[512,128]{1,0:T(8,128)(2,1)S(1)}, bf16[512,128]{1,0:T(8,128)(2,1)S(1)}, u32[]{:S(2)}, u32[]{:S(2)}) collective-permute-start(bf16[512,128]{1,0:T(8,128)(2,1)S(1)} %bitcast.9), channel_id=1, source_target_pairs={{0,224},{32,0},{64,32},{96,64},{128,96},{160,128},{192,160},{224,1... | collective-permute-start | bytes 393224 | tf_op jit(solution)/shard_map/ppermute | solution.py:276
  111.7 14.8 %copy-start.7 = (bf16[512,128]{1,0:T(8,128)(2,1)}, bf16[512,128]{1,0:T(8,128)(2,1)S(1)}, u32[]{:S(2)}) copy-start(bf16[512,128]{1,0:T(8,128)(2,1)S(1)} %collective-permute-done.10.refs_3_) | copy-start | bytes 393220
  111.7 5.0 %collective-permute-start.11 = (bf16[512,128]{1,0:T(8,128)(2,1)S(1)}, bf16[512,128]{1,0:T(8,128)(2,1)S(1)}, u32[]{:S(2)}, u32[]{:S(2)}) collective-permute-start(bf16[512,128]{1,0:T(8,128)(2,1)S(1)} %collective-permute-done.10.refs_3_), channel_id=1, source_target_pairs={{0,32},{32,64},{64,96},{96,128},{128,160},{160,192},{192,224},{224... | collective-permute-start | bytes 393224 | tf_op jit(solution)/shard_map/ppermute | solution.py:275
  113.5 13.0 %copy-start.8 = (bf16[512,128]{1,0:T(8,128)(2,1)}, bf16[512,128]{1,0:T(8,128)(2,1)S(1)}, u32[]{:S(2)}) copy-start(bf16[512,128]{1,0:T(8,128)(2,1)S(1)} %collective-permute-done.14.refs_4_) | copy-start | bytes 393220
  113.5 6.8 %collective-permute-start.15 = (bf16[512,128]{1,0:T(8,128)(2,1)S(1)}, bf16[512,128]{1,0:T(8,128)(2,1)S(1)}, u32[]{:S(2)}, u32[]{:S(2)}) collective-permute-start(bf16[512,128]{1,0:T(8,128)(2,1)S(1)} %collective-permute-done.14.refs_4_), channel_id=1, source_target_pairs={{0,224},{32,0},{64,32},{96,64},{128,96},{160,128},{192,160},{224,1... | collective-permute-start | bytes 393224 | tf_op jit(solution)/shard_map/ppermute | solution.py:276
  116.7 16.0 %copy-start.9 = (bf16[512,128]{1,0:T(8,128)(2,1)}, bf16[512,128]{1,0:T(8,128)(2,1)S(1)}, u32[]{:S(2)}) copy-start(bf16[512,128]{1,0:T(8,128)(2,1)S(1)} %collective-permute-done.11.refs_2_) | copy-start | bytes 393220
  116.7 6.1 %collective-permute-start.12 = (bf16[512,128]{1,0:T(8,128)(2,1)S(1)}, bf16[512,128]{1,0:T(8,128)(2,1)S(1)}, u32[]{:S(2)}, u32[]{:S(2)}) collective-permute-start(bf16[512,128]{1,0:T(8,128)(2,1)S(1)} %collective-permute-done.11.refs_2_), channel_id=1, source_target_pairs={{0,32},{32,64},{64,96},{96,128},{128,160},{160,192},{192,224},{224... | collective-permute-start | bytes 393224 | tf_op jit(solution)/shard_map/ppermute | solution.py:275
  120.2 12.5 %copy-start.10 = (bf16[512,128]{1,0:T(8,128)(2,1)}, bf16[512,128]{1,0:T(8,128)(2,1)S(1)}, u32[]{:S(2)}) copy-start(bf16[512,128]{1,0:T(8,128)(2,1)S(1)} %collective-permute-done.15.refs_3_) | copy-start | bytes 393220
  120.2 12.5 %collective-permute-start.16 = (bf16[512,128]{1,0:T(8,128)(2,1)S(1)}, bf16[512,128]{1,0:T(8,128)(2,1)S(1)}, u32[]{:S(2)}, u32[]{:S(2)}) collective-permute-start(bf16[512,128]{1,0:T(8,128)(2,1)S(1)} %collective-permute-done.15.refs_3_), channel_id=1, source_target_pairs={{0,224},{32,0},{64,32},{96,64},{128,96},{160,128},{192,160},{224,1... | collective-permute-start | bytes 393224 | tf_op jit(solution)/shard_map/ppermute | solution.py:276
  122.8 9.9 %copy-start.11 = (bf16[512,128]{1,0:T(8,128)(2,1)}, bf16[512,128]{1,0:T(8,128)(2,1)S(1)}, u32[]{:S(2)}) copy-start(bf16[512,128]{1,0:T(8,128)(2,1)S(1)} %collective-permute-done.12.refs_4_) | copy-start | bytes 393220
  122.8 18.0 %collective-permute-start.13 = (bf16[512,128]{1,0:T(8,128)(2,1)S(1)}, bf16[512,128]{1,0:T(8,128)(2,1)S(1)}, u32[]{:S(2)}, u32[]{:S(2)}) collective-permute-start(bf16[512,128]{1,0:T(8,128)(2,1)S(1)} %collective-permute-done.12.refs_4_), channel_id=1, source_target_pairs={{0,32},{32,64},{64,96},{96,128},{128,160},{160,192},{192,224},{224... | collective-permute-start | bytes 393224 | tf_op jit(solution)/shard_map/ppermute | solution.py:277
  132.7 0.7 copy-start.13
  140.8 0.7 copy-start.12
  146.2 17.0 %all-to-all-start.3 = ((bf16[8,4,128,128]{3,2,1,0:T(8,128)(2,1)}), bf16[8,4,128,128]{3,2,1,0:T(8,128)(2,1)S(1)}, u32[]{:S(2)}, u32[]{:S(2)}) async-start(bf16[8,4,128,128]{3,2,1,0:T(8,128)(2,1)} %shard_map.80), calls=%async_computation.3 | async-start | bytes 2097152 | tf_op jit(solution)/shard_map/all_to_all | solution.py:267
  163.2 1.0 copy-start.1
  174.5 2.1 %collective-permute-start.17 = (bf16[2,8,128,128]{3,2,1,0:T(8,128)(2,1)}, bf16[2,8,128,128]{3,2,1,0:T(8,128)(2,1)S(1)}, u32[]{:S(2)}, u32[]{:S(2)}) collective-permute-start(bf16[2,8,128,128]{3,2,1,0:T(8,128)(2,1)} %get-tuple-element.44), channel_id=1, source_target_pairs={{0,1},{1,0},{2,3},{3,2},{4,5},{5,4},{6,7},{7,6},{8,9},{9,8},{10,11... | collective-permute-start | bytes 1572872 | tf_op jit(solution)/shard_map/ppermute | solution.py:263
Sparse Core Ops, SparseCore 0:
  9.1 48.3 all-gather.4
  59.3 44.3 all-gather.6

commit v3 on v2

--- a/solution.py
+++ b/solution.py
@@ -114,10 +114,12 @@
                     cols = slice(j * LANES, (j + 1) * LANES)
                     k = h * TOP + j
                     total = total + gates[:, k : k + 1] * jnp.where(left, r[:BLK, cols], r[BLK:, cols])
-                sums.append(total + pltpu.roll(total, HALF, 1))
+                sums.append(total)
             done.append(sums)
         for h in range(heads):
-            out[h, q] = jnp.where(left, done[0][h], done[1][h]).astype(bf16)
+            first, second = done[0][h], done[1][h]
+            crossed = pltpu.roll(jnp.where(left, second, first), HALF, 1)
+            out[h, q] = (jnp.where(left, first, second) + crossed).astype(bf16)
         for h in range(heads, PLANE):
             out[h, q] = jnp.zeros((BLK, LANES), bf16)
         return carry
@@ -138,33 +140,33 @@
         top = jnp.broadcast_to(jnp.max(old_tops[...], axis=1, keepdims=True), (BLK, LANES))
         tops[...] = jnp.full((BLK, LANES), masked_score, f32)
         totals[...] = jnp.zeros(totals.shape, f32)
-        for s, keys in enumerate((k0, k1, k2, k3, k4, k5, k6, k7)):
-
-            @pl.when(s <= z)
+        every = (k0, k1, k2, k3, k4, k5, k6, k7)
+        for first in range(0, SLABS, 2):
+
+            @pl.when(first <= z)
             def _():
-                for c in range(2):
-                    wide = slice(c * 256, (c + 1) * 256)
-                    got = dot(q, keys[:, wide])
-                    if s == 0:
-                        row, col = iota(got.shape, 0), iota(got.shape, 1) + c * 256
-                        key_pos = (2 * (col >> 7) + (row >> 7)) * BLK + (col & 127)
-                        got = jnp.where(key_pos <= block * BLK + (row & 127), got, masked_score)
-                    scores[s, :, wide] = got
-                    tops[...] = jnp.maximum(
-                        tops[...],
-                        jnp.maximum(
-                            jnp.maximum(got[:BLK, :LANES], got[:BLK, LANES:]),
-                            jnp.maximum(got[BLK:, :LANES], got[BLK:, LANES:]),
-                        ),
-                    )
-                    total = totals[...]
-                    for bb in range(2):
-                        for part in range(2 * c, 2 * c + 2):
-                            cols = slice(part * LANES, (part + 1) * LANES)
-                            p = jnp.exp(old_scores[s, bb * BLK : (bb + 1) * BLK, cols] - top)
-                            total = total + p
-                            probs[s, bb, :, cols] = p.astype(bf16)
-                    totals[...] = total
+                best, total = tops[...], totals[...]
+                for s in (first, first + 1):
+                    for c in range(2):
+                        wide = slice(c * 256, (c + 1) * 256)
+                        got = dot(q, every[s][:, wide])
+                        if s == 0:
+                            row, col = iota(got.shape, 0), iota(got.shape, 1) + c * 256
+                            key_pos = (2 * (col >> 7) + (row >> 7)) * BLK + (col & 127)
+                            got = jnp.where(key_pos <= block * BLK + (row & 127), got, masked_score)
+                        if s % 2 == 1:
+                            got = jnp.where(s <= z, got, masked_score)
+                        scores[s, :, wide] = got
+                        for rows in (slice(0, BLK), slice(BLK, 2 * BLK)):
+                            for cols in (slice(0, LANES), slice(LANES, 2 * LANES)):
+                                best = jnp.maximum(best, got[rows, cols])
+                        for bb in range(2):
+                            for part in range(2 * c, 2 * c + 2):
+                                cols = slice(part * LANES, (part + 1) * LANES)
+                                p = jnp.exp(old_scores[s, bb * BLK : (bb + 1) * BLK, cols] - top)
+                                total = total + p
+                                probs[s, bb, :, cols] = p.astype(bf16)
+                tops[...], totals[...] = best, total
 
         sums[...] = jnp.broadcast_to(jnp.sum(totals[...], axis=1, keepdims=True), (BLK, LANES))
 
@@ -211,41 +213,55 @@
                     out[pi, q] = packed
 
 
-def mix_kernel(ids, place, attended, gates_in, table, near, far, lhs, rhs, natural):
-    heads = table.shape[1]
-    z, group = place[2], place[1]
-    src, dst = iota((512, 512), 0), iota((512, 512), 1)
-    order = one_hot(dst == ((src & 255) >> 5) * 64 + 2 * (src & 31) + (src >> 8))
+def chosen_kernel(ids, place, table, out, flipped, ordered):
+    b, z = pl.program_id(0), place[2]
+    heads, experts = table.shape[1], table.shape[2]
+
+    @pl.when(b == 0)
+    def _():
+        src, dst = iota((512, 512), 0), iota((512, 512), 1)
+        order = one_hot(dst == ((src & 255) >> 5) * 64 + 2 * (src & 31) + (src >> 8))
+
+        def one_head(h, carry):
+            for e in range(experts):
+                t = table[:, h, e].reshape(256, LANES).T
+                first = pl.multiple_of(h * experts * HALF, experts * HALF) + e * HALF
+                flipped[pl.ds(first, HALF), :] = jnp.concatenate([t[:HALF], t[HALF:]], axis=1)
+            whole = pl.ds(pl.multiple_of(h * experts * HALF, experts * HALF), experts * HALF)
+            ordered[whole, :] = dot(flipped[whole, :], order).astype(bf16)
+            return carry
+
+        lax.fori_loop(0, heads, one_head, 0)
+
+    for k in range(heads * TOP):
+        e = ids[(z * PLANE + b) * heads * TOP + k]
+        first = pl.multiple_of(((k // TOP) * experts + e) * HALF, HALF)
+        out[0, k * HALF : (k + 1) * HALF, :] = ordered[pl.ds(first, HALF), :]
+
+
+def mix_kernel(place, attended, gates_in, rows, near, far, lhs, natural, spread):
+    q, core = pl.program_id(0), place[1] & 1
+    heads = rows.shape[1] // LANES
     left = iota((BLK, LANES), 1) < HALF
 
-    def two_blocks(q, carry):
-        for bb in range(2):
-            b = 2 * q + bb
-            gates = gates_in[b].astype(f32)
-            for h in range(heads):
-                half = attended[h, q][:, bb * HALF : (bb + 1) * HALF]
-                both = jnp.concatenate([half, half], axis=1).astype(f32)
-                for j in range(TOP):
-                    k = h * TOP + j
-                    cols = slice(k * LANES, (k + 1) * LANES)
-                    gated = both * gates[:, k : k + 1]
-                    lhs[0:BLK, cols] = jnp.where(left, gated, 0.0).astype(bf16)
-                    lhs[BLK:, cols] = jnp.where(left, 0.0, gated).astype(bf16)
-                    rhs[:, cols] = table[
-                        :, h, ids[((z * PLANE + b) * heads + h) * TOP + j]
-                    ].reshape(256, LANES)
-            r = nt_dot(lhs[...], rhs[...])
-            flat = jnp.concatenate([r[:BLK], r[BLK:]], axis=1).astype(bf16)
-            flat = dot(flat, order).astype(bf16)
-            for g in range(4):
-                natural[g] = flat[:, g * LANES : (g + 1) * LANES]
-            core = group & 1
-            for y in range(2):
-                near[y, b] = natural[2 * y + core]
-                far[y, b] = natural[2 * y + (1 - core)]
-        return carry
-
-    lax.fori_loop(0, PLANE // 2, two_blocks, 0)
+    @pl.when(q == 0)
+    def _():
+        spread[...] = one_hot(iota(spread.shape, 0) == (iota(spread.shape, 1) >> 6))
+
+    for bb in range(2):
+        gates = dot(gates_in[bb], spread[...])
+        for h in range(heads):
+            packed = attended[h, q].astype(f32)
+            both = jnp.where(left == (bb == 0), packed, pltpu.roll(packed, HALF, 1))
+            cols = slice(h * LANES, (h + 1) * LANES)
+            lhs[bb, :, cols] = (both * gates[:, cols]).astype(bf16)
+    for bb in range(2):
+        flat = dot(lhs[bb], rows[bb]).astype(bf16)
+        for g in range(4):
+            natural[g, bb] = flat[:, g * LANES : (g + 1) * LANES]
+    for y in range(2):
+        near[y] = natural[2 * y + core]
+        far[y] = natural[2 * y + (1 - core)]
 
 
 def place_kernel(pieces, out):
@@ -267,15 +283,8 @@
     return lax.all_to_all(x, PLANE_AXES, split_axis=0, concat_axis=0, tiled=True)
 
 
-def ring(x):
-    up = [(i, (i + 1) % SLABS) for i in range(SLABS)]
-    down = [(i, (i - 1) % SLABS) for i in range(SLABS)]
-    parts = [x] * SLABS
-    for k in range(1, SLABS // 2):
-        parts[k] = lax.ppermute(parts[k - 1], "z", up)
-        parts[SLABS - k] = lax.ppermute(parts[(SLABS - k + 1) % SLABS], "z", down)
-    parts[SLABS // 2] = lax.ppermute(parts[SLABS // 2 - 1], "z", up)
-    return parts
+def ring_step(x, way):
+    return lax.ppermute(x, "z", [(i, (i + way) % SLABS) for i in range(SLABS)])
 
 
 def add(a, b):
@@ -299,13 +308,21 @@
         out_specs=vmem,
         cost_estimate=cost(0, 500_000),
     )(queries, keys)
-    features, sent = lax.optimization_barrier((features, pairs))
-    pairs = plane_exchange(sent)
-
+    pairs = plane_exchange(pairs)
+
+    own_keys = pl.pallas_call(
+        key_kernel,
+        out_shape=jax.ShapeDtypeStruct((LANES, PLANE // 2 * BLK), bf16),
+        in_specs=[vmem],
+        out_specs=vmem,
+        cost_estimate=cost(0, 400_000),
+    )(pairs)
+    keys = [own_keys] * SLABS
+    keys[1], keys[7] = ring_step(own_keys, 1), ring_step(own_keys, -1)
     over_y = swap(features, "yh")
     over_c = swap(features, "c")
     over_yc = swap(over_y, "c")
-    over_yc, pairs = lax.optimization_barrier((over_yc, pairs))
+    keys[2], keys[6] = ring_step(keys[1], 1), ring_step(keys[7], -1)
     message = pl.pallas_call(
         message_kernel,
         out_shape=jax.ShapeDtypeStruct((PLANE, BLK, 5 * LANES), bf16),
@@ -314,17 +331,11 @@
         compiler_params=params,
         cost_estimate=cost(2 * BLK * LANES * 4096 * 2, 3_000_000),
     )(ids, place, features, over_c, over_y, over_yc, router)
+    keys[3], keys[5] = ring_step(keys[2], 1), ring_step(keys[6], -1)
     message = plane_exchange(message)
 
-    own_keys = pl.pallas_call(
-        key_kernel,
-        out_shape=jax.ShapeDtypeStruct((LANES, PLANE // 2 * BLK), bf16),
-        in_specs=[vmem],
-        out_specs=vmem,
-        cost_estimate=cost(0, 400_000),
-    )(pairs)
-    key_parts = ring(own_keys)
-    message, key_parts = lax.optimization_barrier((message, key_parts))
+    keys[4] = ring_step(keys[3], 1)
+    message, keys = lax.optimization_barrier((message, keys))
 
     slab = PLANE * BLK
     partial = pl.pallas_call(
@@ -357,12 +368,12 @@
         ],
         compiler_params=params,
         cost_estimate=cost(2 * slab * SLABS * slab * 128, 18_000_000, slab * slab * SLABS),
-    )(place, pairs, *key_parts)
+    )(place, pairs, *keys)
 
     partial = plane_exchange(partial)
     own_values = jnp.sum(partial.astype(f32), axis=0).astype(bf16).reshape(slab // 2, LANES)
     own_values, sums = lax.optimization_barrier((own_values, sums))
-    values = ring(own_values)
+    values = [own_values] * SLABS
     output_table = lax.all_gather(output_experts, "z", axis=0, tiled=False)
 
     def weighted(near, carried, last):
@@ -398,25 +409,53 @@
             cost_estimate=cost(steps * 2 * slab * slab * 128, steps * 2_000_000),
         )(place, probs, *[values[s] for s in near], *carried)
 
-    acc = weighted((0, 1, 7), (), False)
-    acc = weighted((2, 6, 3, 5), (acc,), False)
+    values[1], values[7] = ring_step(own_values, 1), ring_step(own_values, -1)
+    acc = weighted((0,), (), False)
+    values[1], values[7], acc = lax.optimization_barrier((values[1], values[7], acc))
+    values[2], values[6] = ring_step(values[1], 1), ring_step(values[7], -1)
+    acc = weighted((1, 7), (acc,), False)
+    values[2], values[6], acc = lax.optimization_barrier((values[2], values[6], acc))
+    values[3], values[5] = ring_step(values[2], 1), ring_step(values[6], -1)
+    acc = weighted((2, 6), (acc,), False)
+    values[3], values[5], acc = lax.optimization_barrier((values[3], values[5], acc))
+    values[4] = ring_step(values[3], 1)
+    acc = weighted((3, 5), (acc,), False)
     attended = weighted((4,), (acc, sums), True)
+    _, output_table = lax.optimization_barrier((attended, output_table))
     attended = plane_exchange(attended)
 
+    width = heads * TOP * HALF
+    rows = pl.pallas_call(
+        chosen_kernel,
+        grid=(PLANE,),
+        out_shape=jax.ShapeDtypeStruct((PLANE, width, 512), bf16),
+        in_specs=[smem, smem, vmem],
+        out_specs=pl.BlockSpec((1, width, 512), lambda b: (b, 0, 0)),
+        scratch_shapes=[pltpu.VMEM((heads * 8 * HALF, 512), bf16)] * 2,
+        compiler_params=params,
+        cost_estimate=cost(0, 20_000_000),
+    )(ids, place, output_table)
     half_out = jax.ShapeDtypeStruct((2, PLANE, BLK, LANES), bf16)
+    half_spec = pl.BlockSpec((2, 2, BLK, LANES), lambda b: (0, b, 0, 0))
     near, far = pl.pallas_call(
         mix_kernel,
+        grid=(PLANE // 2,),
         out_shape=(half_out, half_out),
-        in_specs=[smem, smem, vmem, vmem, vmem],
-        out_specs=(vmem, vmem),
+        in_specs=[
+            smem,
+            vmem,
+            pl.BlockSpec((2, BLK, LANES), lambda b: (b, 0, 4)),
+            pl.BlockSpec((2, width, 512), lambda b: (b, 0, 0)),
+        ],
+        out_specs=(half_spec, half_spec),
         scratch_shapes=[
-            pltpu.VMEM((2 * BLK, heads * TOP * LANES), bf16),
-            pltpu.VMEM((256, heads * TOP * LANES), bf16),
-            pltpu.VMEM((4, BLK, LANES), bf16),
+            pltpu.VMEM((2, BLK, width), bf16),
+            pltpu.VMEM((4, 2, BLK, LANES), bf16),
+            pltpu.VMEM((LANES, width), bf16),
         ],
         compiler_params=params,
-        cost_estimate=cost(2 * 48 * 256 * 256 * 256, 6_000_000),
-    )(ids, place, attended, message[:, :, 4 * LANES :], output_table)
+        cost_estimate=cost(2 * 8 * 128 * 768 * 512, 8_000_000),
+    )(place, attended, message, rows)
     near = add(near, swap(far, "c"))
     mixed = lax.all_to_all(
         near.reshape(2 * PLANE, BLK, LANES), ("yh",) + PLANE_AXES, split_axis=0, concat_axis=0, tiled=True

time: 204 us -> 189 us (0.926)
  the two profiles are of different devices: /device:TPU:224 before, /device:TPU:1 now
where the time goes in v3:
time: 189 us; the launch traced here: 188 us
  Pallas kernels  61.3 us (32%)
  starting transfers between devices  57.6 us (30%)
  waiting for transfers between devices  31.5 us (17%)
  blocking collectives  15.8 us (8%)
  between operations  13.6 us (7%)
  local copies, waits for them, and re-layouts  6.26 us (3%)
  other arithmetic  1.98 us (1%)
    ppermute x14, starting transfers between devices, ring_step(): return lax.ppermute(x, 'z', [(i, (i + way) % SLABS) for i in range(SLABS)])  23.5 us
    ppermute x14, waiting for transfers between devices, ring_step(): return lax.ppermute(x, 'z', [(i, (i + way) % SLABS) for i in range(SLABS)])  22.5 us
    all_to_all x4, starting transfers between devices, plane_exchange(): lax.all_to_all(x, PLANE_AXES, split_axis=0, concat_axis=0, tiled=True)  19.8 us
    pallas_call x5, Pallas kernels, weighted(): pl.pallas_call(lambda *refs: attend_kernel(near, len(carried), last, *ref...  17.9 us
    all_to_all x1, blocking collectives, body(): lax.all_to_all(near.reshape(2 * PLANE, BLK, LANES), ('yh',) + PLANE_AXES,...  15.8 us
    ppermute x4, starting transfers between devices, swap(): return lax.ppermute(x, axis, [(0, 1), (1, 0)])  14.3 us
    pallas_call x1, Pallas kernels, body(): pl.pallas_call(weight_kernel, grid=(PLANE + 1,), out_shape=(jax.ShapeDtyp...  10.7 us
    pallas_call x1, Pallas kernels, body(): pl.pallas_call(chosen_kernel, grid=(PLANE,), out_shape=jax.ShapeDtypeStru...  9.81 us
  transfers between devices with their start and end apart: 24, of which 11 were waited for; matrix products, arithmetic and copies ran while one was open for 1% of the time, Pallas kernels for 28%

profile of v3, /device:TPU:1, one launch (start us, length us, event | category | flops | bytes accessed | tf_op | source)
XLA Modules:
  0.0 188.0 jit_solution(13720307228220897231)
XLA Ops:
  6.5 0.7 all-gather.5.cloned.1.call-update
  7.3 0.0 all-gather.7.cloned.1.call-start
  7.3 0.7 all-gather.7.cloned.1.call-update
  8.0 3.8 %collective-permute-start.1 = (bf16[128,1024]{1,0:T(8,128)(2,1)}, bf16[128,1024]{1,0:T(8,128)(2,1)S(1)}, u32[]{:S(2)}, u32[]{:S(2)}) collective-permute-start(bf16[128,1024]{1,0:T(8,128)(2,1)} %f0.1), channel_id=1, source_target_pairs={{0,2},{2,0},{1,3},{3,1},{4,6},{6,4},{5,7},{7,5},{8,10},{10,8},{9,1... | collective-permute-start | bytes 786440 | tf_op jit(solution)/shard_map/ppermute | solution.py:279
  11.8 1.0 collective-permute-start
  12.8 4.3 %collective-permute-done.1.f2 = bf16[128,1024]{1,0:T(8,128)(2,1)S(1)} collective-permute-done((bf16[128,1024]{1,0:T(8,128)(2,1)}, bf16[128,1024]{1,0:T(8,128)(2,1)S(1)}, u32[]{:S(2)}, u32[]{:S(2)}) %collective-permute-start.1) | collective-permute-done | bytes 262176 | tf_op jit(solution)/shard_map/ppermute | solution.py:279
  17.1 2.3 %collective-permute-start.2 = (bf16[128,1024]{1,0:T(8,128)(2,1)S(1)}, bf16[128,1024]{1,0:T(8,128)(2,1)S(1)}, u32[]{:S(2)}, u32[]{:S(2)}) collective-permute-start(bf16[128,1024]{1,0:T(8,128)(2,1)S(1)} %collective-permute-done.1.f2), channel_id=1, source_target_pairs={{0,1},{1,0},{2,3},{3,2},{4,5},{5,4},{6,7},{7,6},{8,9},{9,8},{10,11... | collective-permute-start | bytes 786440 | tf_op jit(solution)/shard_map/ppermute | solution.py:279
  19.4 1.8 shard_map.74
  21.2 5.0 %all-to-all-start.1 = ((bf16[8,128,128]{2,1,0:T(8,128)(2,1)}), bf16[8,128,128]{2,1,0:T(8,128)(2,1)S(1)}, u32[]{:S(2)}, u32[]{:S(2)}) async-start(bf16[8,128,128]{2,1,0:T(8,128)(2,1)} %shard_map.74), calls=%async_computation.1 | async-start | bytes 524288 | tf_op jit(solution)/shard_map/all_to_all | solution.py:283
  26.2 0.9 copy.9
  27.0 0.7 reshape.9.ids
  27.8 0.7 pad_add_fusion.place.refs_0_
  28.4 0.0 collective-permute-done.f1
  28.4 0.0 collective-permute-done.2.f3
  28.4 0.7 copy-done.5
  29.1 0.7 copy-done.6
  29.8 3.4 %shard_map.73 = bf16[8,128,640]{2,1,0:T(8,128)(2,1)} custom-call(s32[768]{0:T(1024)} %reshape.9.ids, s32[3]{0:T(128)} %pad_add_fusion.place.refs_0_, bf16[128,1024]{1,0:T(8,128)(2,1)} %f0.1, bf16[128,1024]{1,0:T(8,128)(2,1)} %copy-done.5, bf16[128,1024]{1,0:T(8,128)(2,1)} %copy-done.4, bf16[128,1024]{1,0:T(8,128)(2,1)} %copy-done.6, bf16[48,4096]{1,0:T(8,128)(2,1)} %router.1), custom_call_target="tpu_custom_call" | custom-call | flops 268435456 | bytes 3000000 | tf_op jit(solution)/shard_map/pallas_call | solution.py:326
  33.2 0.4 all-to-all-done.1.pairs
  33.6 4.8 %all-to-all-start = ((bf16[8,128,640]{2,1,0:T(8,128)(2,1)}), bf16[8,128,640]{2,1,0:T(8,128)(2,1)S(1)}, u32[]{:S(2)}, u32[]{:S(2)}) async-start(bf16[8,128,640]{2,1,0:T(8,128)(2,1)} %shard_map.73), calls=%async_computation | async-start | bytes 2621440 | tf_op jit(solution)/shard_map/all_to_all | solution.py:283
  38.4 1.8 shard_map.75.k0
  40.2 1.6 collective-permute-start.3
  41.8 4.0 %collective-permute-start.7 = (bf16[128,512]{1,0:T(8,128)(2,1)}, bf16[128,512]{1,0:T(8,128)(2,1)S(1)}, u32[]{:S(2)}, u32[]{:S(2)}) collective-permute-start(bf16[128,512]{1,0:T(8,128)(2,1)} %shard_map.75.k0), channel_id=1, source_target_pairs={{0,224},{32,0},{64,32},{96,64},{128,96},{160,128},{192,160},{224,1... | collective-permute-start | bytes 393224 | tf_op jit(solution)/shard_map/ppermute | solution.py:287
  45.8 6.5 %collective-permute-done.3.k1 = bf16[128,512]{1,0:T(8,128)(2,1)S(1)} collective-permute-done((bf16[128,512]{1,0:T(8,128)(2,1)}, bf16[128,512]{1,0:T(8,128)(2,1)S(1)}, u32[]{:S(2)}, u32[]{:S(2)}) %collective-permute-start.3) | collective-permute-done | bytes 131104 | tf_op jit(solution)/shard_map/ppermute | solution.py:287
  52.3 2.9 %collective-permute-start.8 = (bf16[128,512]{1,0:T(8,128)(2,1)S(1)}, bf16[128,512]{1,0:T(8,128)(2,1)S(1)}, u32[]{:S(2)}, u32[]{:S(2)}) collective-permute-start(bf16[128,512]{1,0:T(8,128)(2,1)S(1)} %collective-permute-done.7.k7), channel_id=1, source_target_pairs={{0,224},{32,0},{64,32},{96,64},{128,96},{160,128},{192,160},{224,1... | collective-permute-start | bytes 393224 | tf_op jit(solution)/shard_map/ppermute | solution.py:287
  55.2 6.0 %collective-permute-done.4.k2 = bf16[128,512]{1,0:T(8,128)(2,1)S(1)} collective-permute-done((bf16[128,512]{1,0:T(8,128)(2,1)S(1)}, bf16[128,512]{1,0:T(8,128)(2,1)S(1)}, u32[]{:S(2)}, u32[]{:S(2)}) %collective-permute-start.4) | collective-permute-done | bytes 131104 | tf_op jit(solution)/shard_map/ppermute | solution.py:287
  61.2 2.7 %collective-permute-start.9 = (bf16[128,512]{1,0:T(8,128)(2,1)S(1)}, bf16[128,512]{1,0:T(8,128)(2,1)S(1)}, u32[]{:S(2)}, u32[]{:S(2)}) collective-permute-start(bf16[128,512]{1,0:T(8,128)(2,1)S(1)} %collective-permute-done.8.k6), channel_id=1, source_target_pairs={{0,224},{32,0},{64,32},{96,64},{128,96},{160,128},{192,160},{224,1... | collective-permute-start | bytes 393224 | tf_op jit(solution)/shard_map/ppermute | solution.py:287
  63.9 2.3 %collective-permute-done.5.k3 = bf16[128,512]{1,0:T(8,128)(2,1)S(1)} collective-permute-done((bf16[128,512]{1,0:T(8,128)(2,1)S(1)}, bf16[128,512]{1,0:T(8,128)(2,1)S(1)}, u32[]{:S(2)}, u32[]{:S(2)}) %collective-permute-start.5) | collective-permute-done | bytes 131104 | tf_op jit(solution)/shard_map/ppermute | solution.py:287
  66.2 5.0 %collective-permute-done.6.k4 = bf16[128,512]{1,0:T(8,128)(2,1)S(1)} collective-permute-done((bf16[128,512]{1,0:T(8,128)(2,1)S(1)}, bf16[128,512]{1,0:T(8,128)(2,1)S(1)}, u32[]{:S(2)}, u32[]{:S(2)}) %collective-permute-start.6) | collective-permute-done | bytes 131104 | tf_op jit(solution)/shard_map/ppermute | solution.py:287
  71.3 0.0 all-gather.5.cloned.1.call-done
  71.3 1.1 copy-done
  72.4 8.0 %shard_map.76 = bf16[8,4,128,128]{3,2,1,0:T(8,128)(2,1)} custom-call(s32[768]{0:T(1024)} %reshape.9.ids, s32[3]{0:T(128)} %pad_add_fusion.place.refs_0_, bf16[8,128,640]{2,1,0:T(8,128)(2,1)} %copy-done, bf16[8,6,8,32,128]{4,3,2,1,0:T(8,128)(2,1)} %bitcast.12), custom_call_target="tpu_custom_call" | custom-call | flops 1610612736 | bytes 6000000 | tf_op jit(solution)/shard_map/pallas_call | solution.py:341
  80.4 5.1 %all-to-all-start.2 = ((bf16[8,4,128,128]{3,2,1,0:T(8,128)(2,1)}), bf16[8,4,128,128]{3,2,1,0:T(8,128)(2,1)S(1)}, u32[]{:S(2)}, u32[]{:S(2)}) async-start(bf16[8,4,128,128]{3,2,1,0:T(8,128)(2,1)} %shard_map.76), calls=%async_computation.2 | async-start | bytes 2097152 | tf_op jit(solution)/shard_map/all_to_all | solution.py:283
  85.5 10.7 %shard_map.77 = (bf16[8,2,1024,512]{3,2,1,0:T(8,128)(2,1)}, f32[1024,128]{1,0:T(8,128)}) custom-call(s32[3]{0:T(128)} %pad_add_fusion.place.refs_0_, bf16[8,128,128]{2,1,0:T(8,128)(2,1)} %copy-done.2, bf16[128,512]{1,0:T(8,128)(2,1)} %shard_map.75.k0, bf16[128,512]{1,0:T(8,128)(2,1)} %copy-done.14, bf16[128,512]{1,0:T(8,128)(2,1)} %copy-done.16, ...), custom_call_target="tpu_custom_call" | custom-call | flops 2147483648 | bytes 18000000 | tf_op jit(solution)/shard_map/pallas_call | solution.py:350
  96.2 0.5 all-to-all-done.2
  96.7 0.1 reduce_sum.12
  96.8 0.0 copy-start.3
  96.8 1.5 collective-permute-start.10
  98.3 5.2 %collective-permute-start.11 = (bf16[512,128]{1,0:T(8,128)(2,1)S(1)}, bf16[512,128]{1,0:T(8,128)(2,1)S(1)}, u32[]{:S(2)}, u32[]{:S(2)}) collective-permute-start(bf16[512,128]{1,0:T(8,128)(2,1)S(1)} %bitcast.10), channel_id=1, source_target_pairs={{0,224},{32,0},{64,32},{96,64},{128,96},{160,128},{192,160},{224,1... | collective-permute-start | bytes 393224 | tf_op jit(solution)/shard_map/ppermute | solution.py:287
  103.5 3.8 %shard_map.78.refs_4_ = f32[1024,128]{1,0:T(8,128)} custom-call(s32[3]{0:T(128)} %pad_add_fusion.place.refs_0_, bf16[8,2,1024,512]{3,2,1,0:T(8,128)(2,1)} %get-tuple-element.41.refs_1_, bf16[512,128]{1,0:T(8,128)(2,1)} %bitcast.11), custom_call_target="tpu_custom_call" | custom-call | flops 268435456 | bytes 2000000 | tf_op jit(solution)/shard_map/pallas_call | solution.py:396
  107.3 1.6 collective-permute-done.10.refs_2_
  108.9 0.1 collective-permute-start.12
  109.0 2.7 %collective-permute-start.13 = (bf16[512,128]{1,0:T(8,128)(2,1)S(1)}, bf16[512,128]{1,0:T(8,128)(2,1)S(1)}, u32[]{:S(2)}, u32[]{:S(2)}) collective-permute-start(bf16[512,128]{1,0:T(8,128)(2,1)S(1)} %collective-permute-done.11.refs_3_), channel_id=1, source_target_pairs={{0,224},{32,0},{64,32},{96,64},{128,96},{160,128},{192,160},{224,1... | collective-permute-start | bytes 393224 | tf_op jit(solution)/shard_map/ppermute | solution.py:287
  111.7 3.4 %shard_map.79.refs_4_ = f32[1024,128]{1,0:T(8,128)} custom-call(s32[3]{0:T(128)} %pad_add_fusion.place.refs_0_, bf16[8,2,1024,512]{3,2,1,0:T(8,128)(2,1)} %get-tuple-element.41.refs_1_, bf16[512,128]{1,0:T(8,128)(2,1)} %copy-done.9, bf16[512,128]{1,0:T(8,128)(2,1)} %copy-done.10, f32[1024,128]{1,0:T(8,128)} %shard_map.78.refs_4_), custom_call_target="tpu_custom_call" | custom-call | flops 536870912 | bytes 4000000 | tf_op jit(solution)/shard_map/pallas_call | solution.py:396
  115.1 0.9 collective-permute-start.14
  116.0 1.8 collective-permute-start.15
  117.8 3.4 %shard_map.80.refs_4_ = f32[1024,128]{1,0:T(8,128)} custom-call(s32[3]{0:T(128)} %pad_add_fusion.place.refs_0_, bf16[8,2,1024,512]{3,2,1,0:T(8,128)(2,1)} %get-tuple-element.41.refs_1_, bf16[512,128]{1,0:T(8,128)(2,1)} %copy-done.7, bf16[512,128]{1,0:T(8,128)(2,1)} %copy-done.8, f32[1024,128]{1,0:T(8,128)} %shard_map.79.refs_4_), custom_call_target="tpu_custom_call" | custom-call | flops 536870912 | bytes 4000000 | tf_op jit(solution)/shard_map/pallas_call | solution.py:396
  121.2 0.2 collective-permute-start.16
  121.4 0.5 copy-done.11
  121.8 0.0 copy-done.12
  121.9 3.4 %shard_map.81.refs_3_ = f32[1024,128]{1,0:T(8,128)} custom-call(s32[3]{0:T(128)} %pad_add_fusion.place.refs_0_, bf16[8,2,1024,512]{3,2,1,0:T(8,128)(2,1)} %get-tuple-element.41.refs_1_, bf16[512,128]{1,0:T(8,128)(2,1)} %copy-done.11, bf16[512,128]{1,0:T(8,128)(2,1)} %copy-done.12, f32[1024,128]{1,0:T(8,128)} %shard_map.80.refs_4_), custom_call_target="tpu_custom_call" | custom-call | flops 536870912 | bytes 4000000 | tf_op jit(solution)/shard_map/pallas_call | solution.py:396
  125.2 1.1 collective-permute-done.16.refs_2_
  126.3 0.7 copy-done.13
  127.0 4.0 %shard_map.82 = bf16[8,4,128,128]{3,2,1,0:T(8,128)(2,1)} custom-call(s32[3]{0:T(128)} %pad_add_fusion.place.refs_0_, bf16[8,2,1024,512]{3,2,1,0:T(8,128)(2,1)} %get-tuple-element.41.refs_1_, bf16[512,128]{1,0:T(8,128)(2,1)} %copy-done.13, f32[1024,128]{1,0:T(8,128)} %shard_map.81.refs_3_, f32[1024,128]{1,0:T(8,128)} %get-tuple-element.53.refs_4_), custom_call_target="tpu_custom_call" | custom-call | flops 268435456 | bytes 2000000 | tf_op jit(solution)/shard_map/pallas_call | solution.py:396
  131.0 5.0 %all-to-all-start.3 = ((bf16[8,4,128,128]{3,2,1,0:T(8,128)(2,1)}), bf16[8,4,128,128]{3,2,1,0:T(8,128)(2,1)S(1)}, u32[]{:S(2)}, u32[]{:S(2)}) async-start(bf16[8,4,128,128]{3,2,1,0:T(8,128)(2,1)} %shard_map.82), calls=%async_computation.3 | async-start | bytes 2097152 | tf_op jit(solution)/shard_map/all_to_all | solution.py:283
  135.9 0.0 all-gather.7.cloned.1.call-done
  136.0 9.8 %shard_map.83.rows = bf16[8,768,512]{2,1,0:T(8,128)(2,1)} custom-call(s32[768]{0:T(1024)} %reshape.9.ids, s32[3]{0:T(128)} %pad_add_fusion.place.refs_0_, bf16[8,6,8,32,128]{4,3,2,1,0:T(8,128)(2,1)} %bitcast.7), custom_call_target="tpu_custom_call" | custom-call | bytes 20000000 | tf_op jit(solution)/shard_map/pallas_call | solution.py:428
  145.8 0.6 all-to-all-done.3.attended
  146.4 1.0 copy-done.1
  147.4 6.0 %shard_map.84 = (bf16[2,8,128,128]{3,2,1,0:T(8,128)(2,1)}, bf16[2,8,128,128]{3,2,1,0:T(8,128)(2,1)}) custom-call(s32[3]{0:T(128)} %pad_add_fusion.place.refs_0_, bf16[8,4,128,128]{3,2,1,0:T(8,128)(2,1)} %copy-done.1, bf16[8,128,640]{2,1,0:T(8,128)(2,1)} %copy-done, bf16[8,768,512]{2,1,0:T(8,128)(2,1)} %shard_map.83.rows), custom_call_target="tpu_custom_call" | custom-call | flops 805306368 | bytes 8000000 | tf_op jit(solution)/shard_map/pallas_call | solution.py:440
  153.4 7.2 %collective-permute-start.17 = (bf16[2,8,128,128]{3,2,1,0:T(8,128)(2,1)}, bf16[2,8,128,128]{3,2,1,0:T(8,128)(2,1)S(1)}, u32[]{:S(2)}, u32[]{:S(2)}) collective-permute-start(bf16[2,8,128,128]{3,2,1,0:T(8,128)(2,1)} %get-tuple-element.56), channel_id=1, source_target_pairs={{0,1},{1,0},{2,3},{3,2},{4,5},{5,4},{6,7},{7,6},{8,9},{9,8},{10,11... | collective-permute-start | bytes 1572872 | tf_op jit(solution)/shard_map/ppermute | solution.py:279
  160.6 1.7 collective-permute-done.17
  162.3 1.2 add_convert_fusion
  163.5 15.8 %all_to_all.25.pieces = bf16[16,128,128]{2,1,0:T(8,128)(2,1)} all-to-all(bf16[16,128,128]{2,1,0:T(8,128)(2,1)S(1)} %bitcast.8), channel_id=1, replica_groups=mesh['z'=8,'yl'=2,'x'=4,'yh'=2,'c'=2] {'yh','yl','x'}, dimensions={0} | all-to-all | bytes 1048576 | tf_op jit(solution)/shard_map/all_to_all | solution.py:460
  179.3 1.9 %shard_map.85 = bf16[128,1024]{1,0:T(8,128)(2,1)} custom-call(bf16[16,128,128]{2,1,0:T(8,128)(2,1)} %all_to_all.25.pieces), custom_call_target="tpu_custom_call" | custom-call | bytes 600000 | tf_op jit(solution)/shard_map/pallas_call | solution.py:463
  (47 shorter events, 0.1 us)
Async XLA Ops:
  6.5 64.7 %all-gather.5.cloned.1.call-start = ((), (), s32[]{:S(2)}) async-start(), calls=%async_computation.5 | async-start | bytes 3538944 | tf_op jit(solution)/shard_map/all_gather | solution.py:303
  7.3 128.7 %all-gather.7.cloned.1.call-start = ((), (), s32[]{:S(2)}) async-start(), calls=%async_computation.6 | async-start | bytes 3538944 | tf_op jit(solution)/shard_map/all_gather | solution.py:377
  8.0 9.1 %collective-permute-start.1 = (bf16[128,1024]{1,0:T(8,128)(2,1)}, bf16[128,1024]{1,0:T(8,128)(2,1)S(1)}, u32[]{:S(2)}, u32[]{:S(2)}) collective-permute-start(bf16[128,1024]{1,0:T(8,128)(2,1)} %f0.1), channel_id=1, source_target_pairs={{0,2},{2,0},{1,3},{3,1},{4,6},{6,4},{5,7},{7,5},{8,10},{10,8},{9,1... | collective-permute-start | bytes 786440 | tf_op jit(solution)/shard_map/ppermute | solution.py:279
  11.8 16.6 %collective-permute-start = (bf16[128,1024]{1,0:T(8,128)(2,1)}, bf16[128,1024]{1,0:T(8,128)(2,1)S(1)}, u32[]{:S(2)}, u32[]{:S(2)}) collective-permute-start(bf16[128,1024]{1,0:T(8,128)(2,1)} %f0.1), channel_id=1, source_target_pairs={{0,1},{1,0},{2,3},{3,2},{4,5},{5,4},{6,7},{7,6},{8,9},{9,8},{10,11... | collective-permute-start | bytes 786440 | tf_op jit(solution)/shard_map/ppermute | solution.py:279
  17.1 11.3 %copy-start.4 = (bf16[128,1024]{1,0:T(8,128)(2,1)}, bf16[128,1024]{1,0:T(8,128)(2,1)S(1)}, u32[]{:S(2)}) copy-start(bf16[128,1024]{1,0:T(8,128)(2,1)S(1)} %collective-permute-done.1.f2) | copy-start | bytes 786436
  17.1 11.3 %collective-permute-start.2 = (bf16[128,1024]{1,0:T(8,128)(2,1)S(1)}, bf16[128,1024]{1,0:T(8,128)(2,1)S(1)}, u32[]{:S(2)}, u32[]{:S(2)}) collective-permute-start(bf16[128,1024]{1,0:T(8,128)(2,1)S(1)} %collective-permute-done.1.f2), channel_id=1, source_target_pairs={{0,1},{1,0},{2,3},{3,2},{4,5},{5,4},{6,7},{7,6},{8,9},{9,8},{10,11... | collective-permute-start | bytes 786440 | tf_op jit(solution)/shard_map/ppermute | solution.py:279
  21.2 12.4 %all-to-all-start.1 = ((bf16[8,128,128]{2,1,0:T(8,128)(2,1)}), bf16[8,128,128]{2,1,0:T(8,128)(2,1)S(1)}, u32[]{:S(2)}, u32[]{:S(2)}) async-start(bf16[8,128,128]{2,1,0:T(8,128)(2,1)} %shard_map.74), calls=%async_computation.1 | async-start | bytes 524288 | tf_op jit(solution)/shard_map/all_to_all | solution.py:283
  28.4 0.7 copy-start.5
  29.1 0.7 copy-start.6
  33.6 4.8 %copy-start.2 = (bf16[8,128,128]{2,1,0:T(8,128)(2,1)}, bf16[8,128,128]{2,1,0:T(8,128)(2,1)S(1)}, u32[]{:S(2)}) copy-start(bf16[8,128,128]{2,1,0:T(8,128)(2,1)S(1)} %all-to-all-done.1.pairs) | copy-start | bytes 786436
  33.6 37.7 %all-to-all-start = ((bf16[8,128,640]{2,1,0:T(8,128)(2,1)}), bf16[8,128,640]{2,1,0:T(8,128)(2,1)S(1)}, u32[]{:S(2)}, u32[]{:S(2)}) async-start(bf16[8,128,640]{2,1,0:T(8,128)(2,1)} %shard_map.73), calls=%async_computation | async-start | bytes 2621440 | tf_op jit(solution)/shard_map/all_to_all | solution.py:283
  40.2 12.1 %collective-permute-start.3 = (bf16[128,512]{1,0:T(8,128)(2,1)}, bf16[128,512]{1,0:T(8,128)(2,1)S(1)}, u32[]{:S(2)}, u32[]{:S(2)}) collective-permute-start(bf16[128,512]{1,0:T(8,128)(2,1)} %shard_map.75.k0), channel_id=1, source_target_pairs={{0,32},{32,64},{64,96},{96,128},{128,160},{160,192},{192,224},{224... | collective-permute-start | bytes 393224 | tf_op jit(solution)/shard_map/ppermute | solution.py:287
  41.8 10.4 %collective-permute-start.7 = (bf16[128,512]{1,0:T(8,128)(2,1)}, bf16[128,512]{1,0:T(8,128)(2,1)S(1)}, u32[]{:S(2)}, u32[]{:S(2)}) collective-permute-start(bf16[128,512]{1,0:T(8,128)(2,1)} %shard_map.75.k0), channel_id=1, source_target_pairs={{0,224},{32,0},{64,32},{96,64},{128,96},{160,128},{192,160},{224,1... | collective-permute-start | bytes 393224 | tf_op jit(solution)/shard_map/ppermute | solution.py:287
  52.3 33.2 %copy-start.14 = (bf16[128,512]{1,0:T(8,128)(2,1)}, bf16[128,512]{1,0:T(8,128)(2,1)S(1)}, u32[]{:S(2)}) copy-start(bf16[128,512]{1,0:T(8,128)(2,1)S(1)} %collective-permute-done.3.k1) | copy-start | bytes 393220
  52.3 8.9 %collective-permute-start.4 = (bf16[128,512]{1,0:T(8,128)(2,1)S(1)}, bf16[128,512]{1,0:T(8,128)(2,1)S(1)}, u32[]{:S(2)}, u32[]{:S(2)}) collective-permute-start(bf16[128,512]{1,0:T(8,128)(2,1)S(1)} %collective-permute-done.3.k1), channel_id=1, source_target_pairs={{0,32},{32,64},{64,96},{96,128},{128,160},{160,192},{192,224},{224... | collective-permute-start | bytes 393224 | tf_op jit(solution)/shard_map/ppermute | solution.py:287
  52.3 33.2 %copy-start.15 = (bf16[128,512]{1,0:T(8,128)(2,1)}, bf16[128,512]{1,0:T(8,128)(2,1)S(1)}, u32[]{:S(2)}) copy-start(bf16[128,512]{1,0:T(8,128)(2,1)S(1)} %collective-permute-done.7.k7) | copy-start | bytes 393220
  52.3 8.9 %collective-permute-start.8 = (bf16[128,512]{1,0:T(8,128)(2,1)S(1)}, bf16[128,512]{1,0:T(8,128)(2,1)S(1)}, u32[]{:S(2)}, u32[]{:S(2)}) collective-permute-start(bf16[128,512]{1,0:T(8,128)(2,1)S(1)} %collective-permute-done.7.k7), channel_id=1, source_target_pairs={{0,224},{32,0},{64,32},{96,64},{128,96},{160,128},{192,160},{224,1... | collective-permute-start | bytes 393224 | tf_op jit(solution)/shard_map/ppermute | solution.py:287
  61.2 24.2 %copy-start.16 = (bf16[128,512]{1,0:T(8,128)(2,1)}, bf16[128,512]{1,0:T(8,128)(2,1)S(1)}, u32[]{:S(2)}) copy-start(bf16[128,512]{1,0:T(8,128)(2,1)S(1)} %collective-permute-done.4.k2) | copy-start | bytes 393220
  61.2 5.0 %collective-permute-start.5 = (bf16[128,512]{1,0:T(8,128)(2,1)S(1)}, bf16[128,512]{1,0:T(8,128)(2,1)S(1)}, u32[]{:S(2)}, u32[]{:S(2)}) collective-permute-start(bf16[128,512]{1,0:T(8,128)(2,1)S(1)} %collective-permute-done.4.k2), channel_id=1, source_target_pairs={{0,32},{32,64},{64,96},{96,128},{128,160},{160,192},{192,224},{224... | collective-permute-start | bytes 393224 | tf_op jit(solution)/shard_map/ppermute | solution.py:287
  61.2 24.2 %copy-start.17 = (bf16[128,512]{1,0:T(8,128)(2,1)}, bf16[128,512]{1,0:T(8,128)(2,1)S(1)}, u32[]{:S(2)}) copy-start(bf16[128,512]{1,0:T(8,128)(2,1)S(1)} %collective-permute-done.8.k6) | copy-start | bytes 393220
  61.2 5.0 %collective-permute-start.9 = (bf16[128,512]{1,0:T(8,128)(2,1)S(1)}, bf16[128,512]{1,0:T(8,128)(2,1)S(1)}, u32[]{:S(2)}, u32[]{:S(2)}) collective-permute-start(bf16[128,512]{1,0:T(8,128)(2,1)S(1)} %collective-permute-done.8.k6), channel_id=1, source_target_pairs={{0,224},{32,0},{64,32},{96,64},{128,96},{160,128},{192,160},{224,1... | collective-permute-start | bytes 393224 | tf_op jit(solution)/shard_map/ppermute | solution.py:287
  66.2 19.2 %copy-start.18 = (bf16[128,512]{1,0:T(8,128)(2,1)}, bf16[128,512]{1,0:T(8,128)(2,1)S(1)}, u32[]{:S(2)}) copy-start(bf16[128,512]{1,0:T(8,128)(2,1)S(1)} %collective-permute-done.5.k3) | copy-start | bytes 393220
  66.2 5.0 %collective-permute-start.6 = (bf16[128,512]{1,0:T(8,128)(2,1)S(1)}, bf16[128,512]{1,0:T(8,128)(2,1)S(1)}, u32[]{:S(2)}, u32[]{:S(2)}) collective-permute-start(bf16[128,512]{1,0:T(8,128)(2,1)S(1)} %collective-permute-done.5.k3), channel_id=1, source_target_pairs={{0,32},{32,64},{64,96},{96,128},{128,160},{160,192},{192,224},{224... | collective-permute-start | bytes 393224 | tf_op jit(solution)/shard_map/ppermute | solution.py:287
  66.2 19.2 %copy-start.19 = (bf16[128,512]{1,0:T(8,128)(2,1)}, bf16[128,512]{1,0:T(8,128)(2,1)S(1)}, u32[]{:S(2)}) copy-start(bf16[128,512]{1,0:T(8,128)(2,1)S(1)} %collective-permute-done.9.k5) | copy-start | bytes 393220
  71.3 14.2 %copy-start.20 = (bf16[128,512]{1,0:T(8,128)(2,1)}, bf16[128,512]{1,0:T(8,128)(2,1)S(1)}, u32[]{:S(2)}) copy-start(bf16[128,512]{1,0:T(8,128)(2,1)S(1)} %collective-permute-done.6.k4) | copy-start | bytes 393220
  71.3 1.1 copy-start
  80.4 16.3 %all-to-all-start.2 = ((bf16[8,4,128,128]{3,2,1,0:T(8,128)(2,1)}), bf16[8,4,128,128]{3,2,1,0:T(8,128)(2,1)S(1)}, u32[]{:S(2)}, u32[]{:S(2)}) async-start(bf16[8,4,128,128]{3,2,1,0:T(8,128)(2,1)} %shard_map.76), calls=%async_computation.2 | async-start | bytes 2097152 | tf_op jit(solution)/shard_map/all_to_all | solution.py:283
  96.8 6.7 %copy-start.3 = (bf16[4,128,128]{2,1,0:T(8,128)(2,1)}, bf16[4,128,128]{2,1,0:T(8,128)(2,1)S(1)}, u32[]{:S(2)}) copy-start(bf16[4,128,128]{2,1,0:T(8,128)(2,1)S(1)} %reduce_sum.12) | copy-start | bytes 393220
  96.8 12.1 %collective-permute-start.10 = (bf16[512,128]{1,0:T(8,128)(2,1)S(1)}, bf16[512,128]{1,0:T(8,128)(2,1)S(1)}, u32[]{:S(2)}, u32[]{:S(2)}) collective-permute-start(bf16[512,128]{1,0:T(8,128)(2,1)S(1)} %bitcast.9), channel_id=1, source_target_pairs={{0,32},{32,64},{64,96},{96,128},{128,160},{160,192},{192,224},{224... | collective-permute-start | bytes 393224 | tf_op jit(solution)/shard_map/ppermute | solution.py:287
  98.3 10.6 %collective-permute-start.11 = (bf16[512,128]{1,0:T(8,128)(2,1)S(1)}, bf16[512,128]{1,0:T(8,128)(2,1)S(1)}, u32[]{:S(2)}, u32[]{:S(2)}) collective-permute-start(bf16[512,128]{1,0:T(8,128)(2,1)S(1)} %bitcast.10), channel_id=1, source_target_pairs={{0,224},{32,0},{64,32},{96,64},{128,96},{160,128},{192,160},{224,1... | collective-permute-start | bytes 393224 | tf_op jit(solution)/shard_map/ppermute | solution.py:287
  108.9 2.8 %copy-start.9 = (bf16[512,128]{1,0:T(8,128)(2,1)}, bf16[512,128]{1,0:T(8,128)(2,1)S(1)}, u32[]{:S(2)}) copy-start(bf16[512,128]{1,0:T(8,128)(2,1)S(1)} %collective-permute-done.10.refs_2_) | copy-start | bytes 393220
  108.9 2.8 %copy-start.10 = (bf16[512,128]{1,0:T(8,128)(2,1)}, bf16[512,128]{1,0:T(8,128)(2,1)S(1)}, u32[]{:S(2)}) copy-start(bf16[512,128]{1,0:T(8,128)(2,1)S(1)} %collective-permute-done.11.refs_3_) | copy-start | bytes 393220
  108.9 6.1 %collective-permute-start.12 = (bf16[512,128]{1,0:T(8,128)(2,1)S(1)}, bf16[512,128]{1,0:T(8,128)(2,1)S(1)}, u32[]{:S(2)}, u32[]{:S(2)}) collective-permute-start(bf16[512,128]{1,0:T(8,128)(2,1)S(1)} %collective-permute-done.10.refs_2_), channel_id=1, source_target_pairs={{0,32},{32,64},{64,96},{96,128},{128,160},{160,192},{192,224},{224... | collective-permute-start | bytes 393224 | tf_op jit(solution)/shard_map/ppermute | solution.py:287
  109.0 6.0 %collective-permute-start.13 = (bf16[512,128]{1,0:T(8,128)(2,1)S(1)}, bf16[512,128]{1,0:T(8,128)(2,1)S(1)}, u32[]{:S(2)}, u32[]{:S(2)}) collective-permute-start(bf16[512,128]{1,0:T(8,128)(2,1)S(1)} %collective-permute-done.11.refs_3_), channel_id=1, source_target_pairs={{0,224},{32,0},{64,32},{96,64},{128,96},{160,128},{192,160},{224,1... | collective-permute-start | bytes 393224 | tf_op jit(solution)/shard_map/ppermute | solution.py:287
  115.0 2.8 %copy-start.7 = (bf16[512,128]{1,0:T(8,128)(2,1)}, bf16[512,128]{1,0:T(8,128)(2,1)S(1)}, u32[]{:S(2)}) copy-start(bf16[512,128]{1,0:T(8,128)(2,1)S(1)} %collective-permute-done.12.refs_2_) | copy-start | bytes 393220
  115.0 2.8 %copy-start.8 = (bf16[512,128]{1,0:T(8,128)(2,1)}, bf16[512,128]{1,0:T(8,128)(2,1)S(1)}, u32[]{:S(2)}) copy-start(bf16[512,128]{1,0:T(8,128)(2,1)S(1)} %collective-permute-done.13.refs_3_) | copy-start | bytes 393220
  115.1 6.1 %collective-permute-start.14 = (bf16[512,128]{1,0:T(8,128)(2,1)S(1)}, bf16[512,128]{1,0:T(8,128)(2,1)S(1)}, u32[]{:S(2)}, u32[]{:S(2)}) collective-permute-start(bf16[512,128]{1,0:T(8,128)(2,1)S(1)} %collective-permute-done.12.refs_2_), channel_id=1, source_target_pairs={{0,32},{32,64},{64,96},{96,128},{128,160},{160,192},{192,224},{224... | collective-permute-start | bytes 393224 | tf_op jit(solution)/shard_map/ppermute | solution.py:287
  116.0 5.2 %collective-permute-start.15 = (bf16[512,128]{1,0:T(8,128)(2,1)S(1)}, bf16[512,128]{1,0:T(8,128)(2,1)S(1)}, u32[]{:S(2)}, u32[]{:S(2)}) collective-permute-start(bf16[512,128]{1,0:T(8,128)(2,1)S(1)} %collective-permute-done.13.refs_3_), channel_id=1, source_target_pairs={{0,224},{32,0},{64,32},{96,64},{128,96},{160,128},{192,160},{224,1... | collective-permute-start | bytes 393224 | tf_op jit(solution)/shard_map/ppermute | solution.py:287
  121.2 0.7 copy-start.11
  121.2 0.7 copy-start.12
  121.2 5.1 %collective-permute-start.16 = (bf16[512,128]{1,0:T(8,128)(2,1)S(1)}, bf16[512,128]{1,0:T(8,128)(2,1)S(1)}, u32[]{:S(2)}, u32[]{:S(2)}) collective-permute-start(bf16[512,128]{1,0:T(8,128)(2,1)S(1)} %collective-permute-done.14.refs_2_), channel_id=1, source_target_pairs={{0,32},{32,64},{64,96},{96,128},{128,160},{160,192},{192,224},{224... | collective-permute-start | bytes 393224 | tf_op jit(solution)/shard_map/ppermute | solution.py:287
  126.3 0.7 copy-start.13
  131.0 15.4 %all-to-all-start.3 = ((bf16[8,4,128,128]{3,2,1,0:T(8,128)(2,1)}), bf16[8,4,128,128]{3,2,1,0:T(8,128)(2,1)S(1)}, u32[]{:S(2)}, u32[]{:S(2)}) async-start(bf16[8,4,128,128]{3,2,1,0:T(8,128)(2,1)} %shard_map.82), calls=%async_computation.3 | async-start | bytes 2097152 | tf_op jit(solution)/shard_map/all_to_all | solution.py:283
  146.4 1.0 copy-start.1
  153.4 8.9 %collective-permute-start.17 = (bf16[2,8,128,128]{3,2,1,0:T(8,128)(2,1)}, bf16[2,8,128,128]{3,2,1,0:T(8,128)(2,1)S(1)}, u32[]{:S(2)}, u32[]{:S(2)}) collective-permute-start(bf16[2,8,128,128]{3,2,1,0:T(8,128)(2,1)} %get-tuple-element.56), channel_id=1, source_target_pairs={{0,1},{1,0},{2,3},{3,2},{4,5},{5,4},{6,7},{7,6},{8,9},{9,8},{10,11... | collective-permute-start | bytes 1572872 | tf_op jit(solution)/shard_map/ppermute | solution.py:279
Sparse Core Ops, SparseCore 0:
  9.1 53.9 all-gather.4
  64.9 45.2 all-gather.6

commit v4 on v3

--- a/solution.py
+++ b/solution.py
@@ -21,11 +21,12 @@
 f32 = jnp.float32
 i32 = jnp.int32
 masked_score = -1e30
-VMEM_BYTES = 56 * 1024 * 1024
+MIB = 1024 * 1024
 
 smem = pl.BlockSpec(memory_space=pltpu.SMEM)
 vmem = pl.BlockSpec(memory_space=pltpu.VMEM)
-params = pltpu.CompilerParams(vmem_limit_bytes=VMEM_BYTES)
+large = pltpu.CompilerParams(vmem_limit_bytes=56 * MIB)
+small = pltpu.CompilerParams(vmem_limit_bytes=20 * MIB)
 
 
 def cost(flops, nbytes, trans=0):
@@ -328,7 +329,7 @@
         out_shape=jax.ShapeDtypeStruct((PLANE, BLK, 5 * LANES), bf16),
         in_specs=[smem, smem] + [vmem] * 5,
         out_specs=vmem,
-        compiler_params=params,
+        compiler_params=small,
         cost_estimate=cost(2 * BLK * LANES * 4096 * 2, 3_000_000),
     )(ids, place, features, over_c, over_y, over_yc, router)
     keys[3], keys[5] = ring_step(keys[2], 1), ring_step(keys[6], -1)
@@ -343,7 +344,7 @@
         out_shape=jax.ShapeDtypeStruct((PLANE, PLANE // 2, BLK, LANES), bf16),
         in_specs=[smem, smem, vmem, vmem],
         out_specs=vmem,
-        compiler_params=params,
+        compiler_params=small,
         cost_estimate=cost(2 * 48 * 256 * 256 * 256, 6_000_000),
     )(ids, place, message, value_table)
     _, pairs = lax.optimization_barrier((partial, pairs))
@@ -366,7 +367,7 @@
             pltpu.VMEM((BLK, LANES), f32),
             pltpu.VMEM((BLK, LANES), f32),
         ],
-        compiler_params=params,
+        compiler_params=large,
         cost_estimate=cost(2 * slab * SLABS * slab * 128, 18_000_000, slab * slab * SLABS),
     )(place, pairs, *keys)
 
@@ -405,7 +406,7 @@
                 scratch_shapes=[pltpu.VMEM((slab, LANES), f32)],
             ),
             out_shape=out_shape,
-            compiler_params=params,
+            compiler_params=large,
             cost_estimate=cost(steps * 2 * slab * slab * 128, steps * 2_000_000),
         )(place, probs, *[values[s] for s in near], *carried)
 
@@ -432,7 +433,7 @@
         in_specs=[smem, smem, vmem],
         out_specs=pl.BlockSpec((1, width, 512), lambda b: (b, 0, 0)),
         scratch_shapes=[pltpu.VMEM((heads * 8 * HALF, 512), bf16)] * 2,
-        compiler_params=params,
+        compiler_params=large,
         cost_estimate=cost(0, 20_000_000),
     )(ids, place, output_table)
     half_out = jax.ShapeDtypeStruct((2, PLANE, BLK, LANES), bf16)
@@ -453,7 +454,7 @@
             pltpu.VMEM((4, 2, BLK, LANES), bf16),
             pltpu.VMEM((LANES, width), bf16),
         ],
-        compiler_params=params,
+        compiler_params=small,
         cost_estimate=cost(2 * 8 * 128 * 768 * 512, 8_000_000),
     )(place, attended, message, rows)
     near = add(near, swap(far, "c"))

time: 189 us -> 188 us (level)
  Pallas kernels: 61.3 us -> 56 us
  waiting for transfers between devices: 31.5 us -> 33.9 us
  local copies, waits for them, and re-layouts: 6.26 us -> 8.37 us
    pallas_call x1, Pallas kernels: 6.02 us -> 3.17 us  [body(): pl.pallas_call(mix_kernel, grid=(PLANE // 2,), out_shape=(half_out, half_...]
    unnamed x43 -> x47, local copies, waits for them, and re-layouts: 5.53 us -> 8.24 us
  transfers between devices with their start and end apart: 24 -> 24, of which waited for: 11 -> 12; matrix products, arithmetic and copies ran while one was open for 1% -> 1% of each run, Pallas kernels for 28% -> 27%
where the time goes in v4:
time: 188 us; the launch traced here: 187 us
  starting transfers between devices  58.8 us (31%)
  Pallas kernels  56 us (30%)
  waiting for transfers between devices  33.9 us (18%)
  blocking collectives  15.8 us (8%)
  between operations  13.7 us (7%)
  local copies, waits for them, and re-layouts  8.37 us (4%)
    ppermute x14, starting transfers between devices, ring_step(): return lax.ppermute(x, 'z', [(i, (i + way) % SLABS) for i in range(SLABS)])  24.4 us
    ppermute x14, waiting for transfers between devices, ring_step(): return lax.ppermute(x, 'z', [(i, (i + way) % SLABS) for i in range(SLABS)])  24.4 us
    all_to_all x4, starting transfers between devices, plane_exchange(): lax.all_to_all(x, PLANE_AXES, split_axis=0, concat_axis=0, tiled=True)  18.2 us
    pallas_call x5, Pallas kernels, weighted(): pl.pallas_call(lambda *refs: attend_kernel(near, len(carried), last, *ref...  17.9 us
    ppermute x4, starting transfers between devices, swap(): return lax.ppermute(x, axis, [(0, 1), (1, 0)])  16.1 us
    all_to_all x1, blocking collectives, body(): lax.all_to_all(near.reshape(2 * PLANE, BLK, LANES), ('yh',) + PLANE_AXES,...  15.8 us
    pallas_call x1, Pallas kernels, body(): pl.pallas_call(weight_kernel, grid=(PLANE + 1,), out_shape=(jax.ShapeDtyp...  10.7 us
    pallas_call x1, Pallas kernels, body(): pl.pallas_call(chosen_kernel, grid=(PLANE,), out_shape=jax.ShapeDtypeStru...  9.81 us
  transfers between devices with their start and end apart: 24, of which 12 were waited for; matrix products, arithmetic and copies ran while one was open for 1% of the time, Pallas kernels for 27%

profile of v4, /device:TPU:1, one launch (start us, length us, event | category | flops | bytes accessed | tf_op | source)
XLA Modules:
  0.0 186.8 jit_solution(6389241798821776024)
XLA Ops:
  6.5 0.7 all-gather.5.cloned.1.call-update
  7.3 0.0 all-gather.7.cloned.1.call-start
  7.3 0.7 all-gather.7.cloned.1.call-update
  8.0 3.8 %collective-permute-start.1 = (bf16[128,1024]{1,0:T(8,128)(2,1)}, bf16[128,1024]{1,0:T(8,128)(2,1)S(1)}, u32[]{:S(2)}, u32[]{:S(2)}) collective-permute-start(bf16[128,1024]{1,0:T(8,128)(2,1)} %f0.1), channel_id=1, source_target_pairs={{0,2},{2,0},{1,3},{3,1},{4,6},{6,4},{5,7},{7,5},{8,10},{10,8},{9,1... | collective-permute-start | bytes 786440 | tf_op jit(solution)/shard_map/ppermute | solution.py:280
  11.8 1.0 collective-permute-start
  12.8 4.3 %collective-permute-done.1.f2 = bf16[128,1024]{1,0:T(8,128)(2,1)S(1)} collective-permute-done((bf16[128,1024]{1,0:T(8,128)(2,1)}, bf16[128,1024]{1,0:T(8,128)(2,1)S(1)}, u32[]{:S(2)}, u32[]{:S(2)}) %collective-permute-start.1) | collective-permute-done | bytes 262176 | tf_op jit(solution)/shard_map/ppermute | solution.py:280
  17.1 2.3 %collective-permute-start.2 = (bf16[128,1024]{1,0:T(8,128)(2,1)S(1)}, bf16[128,1024]{1,0:T(8,128)(2,1)S(1)}, u32[]{:S(2)}, u32[]{:S(2)}) collective-permute-start(bf16[128,1024]{1,0:T(8,128)(2,1)S(1)} %collective-permute-done.1.f2), channel_id=1, source_target_pairs={{0,1},{1,0},{2,3},{3,2},{4,5},{5,4},{6,7},{7,6},{8,9},{9,8},{10,11... | collective-permute-start | bytes 786440 | tf_op jit(solution)/shard_map/ppermute | solution.py:280
  19.4 1.8 shard_map.74
  21.2 5.0 %all-to-all-start.1 = ((bf16[8,128,128]{2,1,0:T(8,128)(2,1)}), bf16[8,128,128]{2,1,0:T(8,128)(2,1)S(1)}, u32[]{:S(2)}, u32[]{:S(2)}) async-start(bf16[8,128,128]{2,1,0:T(8,128)(2,1)} %shard_map.74), calls=%async_computation.1 | async-start | bytes 524288 | tf_op jit(solution)/shard_map/all_to_all | solution.py:284
  26.2 0.9 copy.9
  27.0 0.1 reshape.9.ids
  27.2 0.1 pad_add_fusion.place.refs_0_
  27.3 0.0 collective-permute-done.f1
  27.3 0.0 copy-start.1
  27.3 1.0 copy-done.1
  28.3 0.9 copy-done.2
  29.2 2.7 %shard_map.73 = bf16[8,128,640]{2,1,0:T(8,128)(2,1)} custom-call(s32[768]{0:T(1024)S(1)} %reshape.9.ids, s32[3]{0:T(128)S(1)} %pad_add_fusion.place.refs_0_, bf16[128,1024]{1,0:T(8,128)(2,1)S(1)} %copy-done.2, bf16[128,1024]{1,0:T(8,128)(2,1)S(1)} %collective-permute-done.f1, bf16[128,1024]{1,0:T(8,128)(2,1)S(1)} %collective-permute-done.1.f2, ...), custom_call_target="tpu_custom_call" | custom-call | flops 268435456 | bytes 3000000 | tf_op jit(solution)/shard_map/pallas_call | solution.py:327
  31.9 1.7 all-to-all-done.1.pairs
  33.6 3.6 %all-to-all-start = ((bf16[8,128,640]{2,1,0:T(8,128)(2,1)}), bf16[8,128,640]{2,1,0:T(8,128)(2,1)S(1)}, u32[]{:S(2)}, u32[]{:S(2)}) async-start(bf16[8,128,640]{2,1,0:T(8,128)(2,1)} %shard_map.73), calls=%async_computation | async-start | bytes 2621440 | tf_op jit(solution)/shard_map/all_to_all | solution.py:284
  37.2 1.8 shard_map.75.k0
  39.0 1.6 collective-permute-start.3
  40.6 3.9 %collective-permute-start.7 = (bf16[128,512]{1,0:T(8,128)(2,1)}, bf16[128,512]{1,0:T(8,128)(2,1)S(1)}, u32[]{:S(2)}, u32[]{:S(2)}) collective-permute-start(bf16[128,512]{1,0:T(8,128)(2,1)} %shard_map.75.k0), channel_id=1, source_target_pairs={{0,224},{32,0},{64,32},{96,64},{128,96},{160,128},{192,160},{224,1... | collective-permute-start | bytes 393224 | tf_op jit(solution)/shard_map/ppermute | solution.py:288
  44.6 6.4 %collective-permute-done.3.k1 = bf16[128,512]{1,0:T(8,128)(2,1)S(1)} collective-permute-done((bf16[128,512]{1,0:T(8,128)(2,1)}, bf16[128,512]{1,0:T(8,128)(2,1)S(1)}, u32[]{:S(2)}, u32[]{:S(2)}) %collective-permute-start.3) | collective-permute-done | bytes 131104 | tf_op jit(solution)/shard_map/ppermute | solution.py:288
  51.0 2.7 %collective-permute-start.8 = (bf16[128,512]{1,0:T(8,128)(2,1)S(1)}, bf16[128,512]{1,0:T(8,128)(2,1)S(1)}, u32[]{:S(2)}, u32[]{:S(2)}) collective-permute-start(bf16[128,512]{1,0:T(8,128)(2,1)S(1)} %collective-permute-done.7.k7), channel_id=1, source_target_pairs={{0,224},{32,0},{64,32},{96,64},{128,96},{160,128},{192,160},{224,1... | collective-permute-start | bytes 393224 | tf_op jit(solution)/shard_map/ppermute | solution.py:288
  53.7 6.3 %collective-permute-done.4.k2 = bf16[128,512]{1,0:T(8,128)(2,1)S(1)} collective-permute-done((bf16[128,512]{1,0:T(8,128)(2,1)S(1)}, bf16[128,512]{1,0:T(8,128)(2,1)S(1)}, u32[]{:S(2)}, u32[]{:S(2)}) %collective-permute-start.4) | collective-permute-done | bytes 131104 | tf_op jit(solution)/shard_map/ppermute | solution.py:288
  60.0 2.7 %collective-permute-start.9 = (bf16[128,512]{1,0:T(8,128)(2,1)S(1)}, bf16[128,512]{1,0:T(8,128)(2,1)S(1)}, u32[]{:S(2)}, u32[]{:S(2)}) collective-permute-start(bf16[128,512]{1,0:T(8,128)(2,1)S(1)} %collective-permute-done.8.k6), channel_id=1, source_target_pairs={{0,224},{32,0},{64,32},{96,64},{128,96},{160,128},{192,160},{224,1... | collective-permute-start | bytes 393224 | tf_op jit(solution)/shard_map/ppermute | solution.py:288
  62.6 2.3 %collective-permute-done.5.k3 = bf16[128,512]{1,0:T(8,128)(2,1)S(1)} collective-permute-done((bf16[128,512]{1,0:T(8,128)(2,1)S(1)}, bf16[128,512]{1,0:T(8,128)(2,1)S(1)}, u32[]{:S(2)}, u32[]{:S(2)}) %collective-permute-start.5) | collective-permute-done | bytes 131104 | tf_op jit(solution)/shard_map/ppermute | solution.py:288
  65.0 0.0 collective-permute-done.9.k5
  65.0 5.0 %collective-permute-done.6.k4 = bf16[128,512]{1,0:T(8,128)(2,1)S(1)} collective-permute-done((bf16[128,512]{1,0:T(8,128)(2,1)S(1)}, bf16[128,512]{1,0:T(8,128)(2,1)S(1)}, u32[]{:S(2)}, u32[]{:S(2)}) %collective-permute-start.6) | collective-permute-done | bytes 131104 | tf_op jit(solution)/shard_map/ppermute | solution.py:288
  70.0 1.9 %copy-done.6 = bf16[48,8,32,128]{3,2,1,0:T(8,128)(2,1)S(1)} copy-done((bf16[48,8,32,128]{3,2,1,0:T(8,128)(2,1)S(1)}, bf16[48,8,32,128]{3,2,1,0:T(8,128)(2,1)}, u32[]{:S(2)}) %copy-start.6) | copy-done | bytes 3145752
  71.9 6.3 %shard_map.76 = bf16[8,4,128,128]{3,2,1,0:T(8,128)(2,1)} custom-call(s32[768]{0:T(1024)S(1)} %reshape.9.ids, s32[3]{0:T(128)S(1)} %pad_add_fusion.place.refs_0_, bf16[8,128,640]{2,1,0:T(8,128)(2,1)S(1)} %all-to-all-done.message.gates_in, bf16[8,6,8,32,128]{4,3,2,1,0:T(8,128)(2,1)S(1)} %bitcast.7), custom_call_target="tpu_custom_call" | custom-call | flops 1610612736 | bytes 6000000 | tf_op jit(solution)/shard_map/pallas_call | solution.py:342
  78.3 5.0 %all-to-all-start.2 = ((bf16[8,4,128,128]{3,2,1,0:T(8,128)(2,1)}), bf16[8,4,128,128]{3,2,1,0:T(8,128)(2,1)S(1)}, u32[]{:S(2)}, u32[]{:S(2)}) async-start(bf16[8,4,128,128]{3,2,1,0:T(8,128)(2,1)} %shard_map.76), calls=%async_computation.2 | async-start | bytes 2097152 | tf_op jit(solution)/shard_map/all_to_all | solution.py:284
  83.2 10.7 %shard_map.77 = (bf16[8,2,1024,512]{3,2,1,0:T(8,128)(2,1)}, f32[1024,128]{1,0:T(8,128)}) custom-call(s32[3]{0:T(128)} %copy-done.3, bf16[8,128,128]{2,1,0:T(8,128)(2,1)} %copy-done.7, bf16[128,512]{1,0:T(8,128)(2,1)} %shard_map.75.k0, bf16[128,512]{1,0:T(8,128)(2,1)} %copy-done.16, bf16[128,512]{1,0:T(8,128)(2,1)} %copy-done.18, ...), custom_call_target="tpu_custom_call" | custom-call | flops 2147483648 | bytes 18000000 | tf_op jit(solution)/shard_map/pallas_call | solution.py:351
  94.0 0.2 reduce_sum.12
  94.1 0.0 copy-start.8
  94.1 0.1 collective-permute-start.10
  94.2 7.0 %collective-permute-start.11 = (bf16[512,128]{1,0:T(8,128)(2,1)S(1)}, bf16[512,128]{1,0:T(8,128)(2,1)S(1)}, u32[]{:S(2)}, u32[]{:S(2)}) collective-permute-start(bf16[512,128]{1,0:T(8,128)(2,1)S(1)} %bitcast.11), channel_id=1, source_target_pairs={{0,224},{32,0},{64,32},{96,64},{128,96},{160,128},{192,160},{224,1... | collective-permute-start | bytes 393224 | tf_op jit(solution)/shard_map/ppermute | solution.py:288
  101.2 3.8 %shard_map.78.refs_4_ = f32[1024,128]{1,0:T(8,128)} custom-call(s32[3]{0:T(128)} %copy-done.3, bf16[8,2,1024,512]{3,2,1,0:T(8,128)(2,1)} %get-tuple-element.41.refs_1_, bf16[512,128]{1,0:T(8,128)(2,1)} %bitcast.12), custom_call_target="tpu_custom_call" | custom-call | flops 268435456 | bytes 2000000 | tf_op jit(solution)/shard_map/pallas_call | solution.py:397
  105.0 1.5 collective-permute-done.10.refs_2_
  106.5 0.1 collective-permute-start.12
  106.6 2.8 %collective-permute-start.13 = (bf16[512,128]{1,0:T(8,128)(2,1)S(1)}, bf16[512,128]{1,0:T(8,128)(2,1)S(1)}, u32[]{:S(2)}, u32[]{:S(2)}) collective-permute-start(bf16[512,128]{1,0:T(8,128)(2,1)S(1)} %collective-permute-done.11.refs_3_), channel_id=1, source_target_pairs={{0,224},{32,0},{64,32},{96,64},{128,96},{160,128},{192,160},{224,1... | collective-permute-start | bytes 393224 | tf_op jit(solution)/shard_map/ppermute | solution.py:288
  109.4 3.3 %shard_map.79.refs_4_ = f32[1024,128]{1,0:T(8,128)} custom-call(s32[3]{0:T(128)} %copy-done.3, bf16[8,2,1024,512]{3,2,1,0:T(8,128)(2,1)} %get-tuple-element.41.refs_1_, bf16[512,128]{1,0:T(8,128)(2,1)} %copy-done.11, bf16[512,128]{1,0:T(8,128)(2,1)} %copy-done.12, f32[1024,128]{1,0:T(8,128)} %shard_map.78.refs_4_), custom_call_target="tpu_custom_call" | custom-call | flops 536870912 | bytes 4000000 | tf_op jit(solution)/shard_map/pallas_call | solution.py:397
  112.7 0.3 collective-permute-done.12.refs_2_
  113.0 0.0 collective-permute-done.13.refs_3_
  113.0 0.7 collective-permute-start.14
  113.7 2.1 %collective-permute-start.15 = (bf16[512,128]{1,0:T(8,128)(2,1)S(1)}, bf16[512,128]{1,0:T(8,128)(2,1)S(1)}, u32[]{:S(2)}, u32[]{:S(2)}) collective-permute-start(bf16[512,128]{1,0:T(8,128)(2,1)S(1)} %collective-permute-done.13.refs_3_), channel_id=1, source_target_pairs={{0,224},{32,0},{64,32},{96,64},{128,96},{160,128},{192,160},{224,1... | collective-permute-start | bytes 393224 | tf_op jit(solution)/shard_map/ppermute | solution.py:288
  115.8 3.4 %shard_map.80.refs_4_ = f32[1024,128]{1,0:T(8,128)} custom-call(s32[3]{0:T(128)} %copy-done.3, bf16[8,2,1024,512]{3,2,1,0:T(8,128)(2,1)} %get-tuple-element.41.refs_1_, bf16[512,128]{1,0:T(8,128)(2,1)} %copy-done.9, bf16[512,128]{1,0:T(8,128)(2,1)} %copy-done.10, f32[1024,128]{1,0:T(8,128)} %shard_map.79.refs_4_), custom_call_target="tpu_custom_call" | custom-call | flops 536870912 | bytes 4000000 | tf_op jit(solution)/shard_map/pallas_call | solution.py:397
  119.1 0.1 collective-permute-done.14.refs_2_
  119.2 0.9 collective-permute-start.16
  120.1 3.4 %shard_map.81.refs_3_ = f32[1024,128]{1,0:T(8,128)} custom-call(s32[3]{0:T(128)} %copy-done.3, bf16[8,2,1024,512]{3,2,1,0:T(8,128)(2,1)} %get-tuple-element.41.refs_1_, bf16[512,128]{1,0:T(8,128)(2,1)} %copy-done.13, bf16[512,128]{1,0:T(8,128)(2,1)} %copy-done.14, f32[1024,128]{1,0:T(8,128)} %shard_map.80.refs_4_), custom_call_target="tpu_custom_call" | custom-call | flops 536870912 | bytes 4000000 | tf_op jit(solution)/shard_map/pallas_call | solution.py:397
  123.4 2.5 %collective-permute-done.16.refs_2_ = bf16[512,128]{1,0:T(8,128)(2,1)S(1)} collective-permute-done((bf16[512,128]{1,0:T(8,128)(2,1)S(1)}, bf16[512,128]{1,0:T(8,128)(2,1)S(1)}, u32[]{:S(2)}, u32[]{:S(2)}) %collective-permute-start.16) | collective-permute-done | bytes 131104 | tf_op jit(solution)/shard_map/ppermute | solution.py:288
  125.9 0.7 copy-done.15
  126.5 4.0 %shard_map.82 = bf16[8,4,128,128]{3,2,1,0:T(8,128)(2,1)} custom-call(s32[3]{0:T(128)} %copy-done.3, bf16[8,2,1024,512]{3,2,1,0:T(8,128)(2,1)} %get-tuple-element.41.refs_1_, bf16[512,128]{1,0:T(8,128)(2,1)} %copy-done.15, f32[1024,128]{1,0:T(8,128)} %shard_map.81.refs_3_, f32[1024,128]{1,0:T(8,128)} %get-tuple-element.53.refs_4_), custom_call_target="tpu_custom_call" | custom-call | flops 268435456 | bytes 2000000 | tf_op jit(solution)/shard_map/pallas_call | solution.py:397
  130.5 4.7 %all-to-all-start.3 = ((bf16[8,4,128,128]{3,2,1,0:T(8,128)(2,1)}), bf16[8,4,128,128]{3,2,1,0:T(8,128)(2,1)S(1)}, u32[]{:S(2)}, u32[]{:S(2)}) async-start(bf16[8,4,128,128]{3,2,1,0:T(8,128)(2,1)} %shard_map.82), calls=%async_computation.3 | async-start | bytes 2097152 | tf_op jit(solution)/shard_map/all_to_all | solution.py:284
  135.3 0.0 all-gather.7.cloned.1.call-done
  135.3 9.8 %shard_map.83.rows = bf16[8,768,512]{2,1,0:T(8,128)(2,1)} custom-call(s32[768]{0:T(1024)} %copy-done.5, s32[3]{0:T(128)} %copy-done.3, bf16[8,6,8,32,128]{4,3,2,1,0:T(8,128)(2,1)} %bitcast.8), custom_call_target="tpu_custom_call" | custom-call | bytes 20000000 | tf_op jit(solution)/shard_map/pallas_call | solution.py:429
  145.1 0.5 all-to-all-done.3.attended
  145.6 2.8 %copy-done = bf16[8,768,512]{2,1,0:T(8,128)(2,1)S(1)} copy-done((bf16[8,768,512]{2,1,0:T(8,128)(2,1)S(1)}, bf16[8,768,512]{2,1,0:T(8,128)(2,1)}, u32[]{:S(2)}) %copy-start) | copy-done | bytes 6291480
  148.4 3.2 %shard_map.84 = (bf16[2,8,128,128]{3,2,1,0:T(8,128)(2,1)S(1)}, bf16[2,8,128,128]{3,2,1,0:T(8,128)(2,1)S(1)}) custom-call(s32[3]{0:T(128)S(1)} %copy-done.4, bf16[8,4,128,128]{3,2,1,0:T(8,128)(2,1)S(1)} %all-to-all-done.3.attended, bf16[8,128,640]{2,1,0:T(8,128)(2,1)S(1)} %all-to-all-done.message.gates_in, bf16[8,768,512]{2,1,0:T(8,128)(2,1)S(1)} %copy-done), custom_call_target="tpu_custom_call" | custom-call | flops 805306368 | bytes 8000000 | tf_op jit(solution)/shard_map/pallas_call | solution.py:441
  151.6 9.0 %collective-permute-start.17 = (bf16[2,8,128,128]{3,2,1,0:T(8,128)(2,1)S(1)}, bf16[2,8,128,128]{3,2,1,0:T(8,128)(2,1)S(1)}, u32[]{:S(2)}, u32[]{:S(2)}) collective-permute-start(bf16[2,8,128,128]{3,2,1,0:T(8,128)(2,1)S(1)} %get-tuple-element.56), channel_id=1, source_target_pairs={{0,1},{1,0},{2,3},{3,2},{4,5},{5,4},{6,7},{7,6},{8,9},{9,8},{10,11... | collective-permute-start | bytes 1572872 | tf_op jit(solution)/shard_map/ppermute | solution.py:280
  160.6 1.5 collective-permute-done.17
  162.1 0.1 add_convert_fusion
  162.3 15.8 %all_to_all.25.pieces = bf16[16,128,128]{2,1,0:T(8,128)(2,1)} all-to-all(bf16[16,128,128]{2,1,0:T(8,128)(2,1)S(1)} %bitcast.9), channel_id=1, replica_groups=mesh['z'=8,'yl'=2,'x'=4,'yh'=2,'c'=2] {'yh','yl','x'}, dimensions={0} | all-to-all | bytes 1048576 | tf_op jit(solution)/shard_map/all_to_all | solution.py:461
  178.1 1.9 %shard_map.85 = bf16[128,1024]{1,0:T(8,128)(2,1)} custom-call(bf16[16,128,128]{2,1,0:T(8,128)(2,1)} %all_to_all.25.pieces), custom_call_target="tpu_custom_call" | custom-call | bytes 600000 | tf_op jit(solution)/shard_map/pallas_call | solution.py:464
  (51 shorter events, 0.1 us)
Async XLA Ops:
  6.5 63.5 %all-gather.5.cloned.1.call-start = ((), (), s32[]{:S(2)}) async-start(), calls=%async_computation.5 | async-start | bytes 3538944 | tf_op jit(solution)/shard_map/all_gather | solution.py:304
  7.3 128.0 %all-gather.7.cloned.1.call-start = ((), (), s32[]{:S(2)}) async-start(), calls=%async_computation.6 | async-start | bytes 3538944 | tf_op jit(solution)/shard_map/all_gather | solution.py:378
  8.0 9.1 %collective-permute-start.1 = (bf16[128,1024]{1,0:T(8,128)(2,1)}, bf16[128,1024]{1,0:T(8,128)(2,1)S(1)}, u32[]{:S(2)}, u32[]{:S(2)}) collective-permute-start(bf16[128,1024]{1,0:T(8,128)(2,1)} %f0.1), channel_id=1, source_target_pairs={{0,2},{2,0},{1,3},{3,1},{4,6},{6,4},{5,7},{7,5},{8,10},{10,8},{9,1... | collective-permute-start | bytes 786440 | tf_op jit(solution)/shard_map/ppermute | solution.py:280
  11.8 15.4 %collective-permute-start = (bf16[128,1024]{1,0:T(8,128)(2,1)}, bf16[128,1024]{1,0:T(8,128)(2,1)S(1)}, u32[]{:S(2)}, u32[]{:S(2)}) collective-permute-start(bf16[128,1024]{1,0:T(8,128)(2,1)} %f0.1), channel_id=1, source_target_pairs={{0,1},{1,0},{2,3},{3,2},{4,5},{5,4},{6,7},{7,6},{8,9},{9,8},{10,11... | collective-permute-start | bytes 786440 | tf_op jit(solution)/shard_map/ppermute | solution.py:280
  17.1 10.1 %collective-permute-start.2 = (bf16[128,1024]{1,0:T(8,128)(2,1)S(1)}, bf16[128,1024]{1,0:T(8,128)(2,1)S(1)}, u32[]{:S(2)}, u32[]{:S(2)}) collective-permute-start(bf16[128,1024]{1,0:T(8,128)(2,1)S(1)} %collective-permute-done.1.f2), channel_id=1, source_target_pairs={{0,1},{1,0},{2,3},{3,2},{4,5},{5,4},{6,7},{7,6},{8,9},{9,8},{10,11... | collective-permute-start | bytes 786440 | tf_op jit(solution)/shard_map/ppermute | solution.py:280
  21.2 12.4 %all-to-all-start.1 = ((bf16[8,128,128]{2,1,0:T(8,128)(2,1)}), bf16[8,128,128]{2,1,0:T(8,128)(2,1)S(1)}, u32[]{:S(2)}, u32[]{:S(2)}) async-start(bf16[8,128,128]{2,1,0:T(8,128)(2,1)} %shard_map.74), calls=%async_computation.1 | async-start | bytes 524288 | tf_op jit(solution)/shard_map/all_to_all | solution.py:284
  27.2 51.1 %copy-start.5 = (s32[768]{0:T(1024)}, s32[768]{0:T(1024)S(1)}, u32[]{:S(2)}) copy-start(s32[768]{0:T(1024)S(1)} %reshape.9.ids) | copy-start | bytes 9220
  27.3 51.0 %copy-start.3 = (s32[3]{0:T(128)}, s32[3]{0:T(128)S(1)}, u32[]{:S(2)}) copy-start(s32[3]{0:T(128)S(1)} %pad_add_fusion.place.refs_0_) | copy-start | bytes 40
  27.3 1.0 copy-start.1
  28.3 0.9 copy-start.2
  33.6 3.6 %copy-start.7 = (bf16[8,128,128]{2,1,0:T(8,128)(2,1)}, bf16[8,128,128]{2,1,0:T(8,128)(2,1)S(1)}, u32[]{:S(2)}) copy-start(bf16[8,128,128]{2,1,0:T(8,128)(2,1)S(1)} %all-to-all-done.1.pairs) | copy-start | bytes 786436
  33.6 36.4 %all-to-all-start = ((bf16[8,128,640]{2,1,0:T(8,128)(2,1)}), bf16[8,128,640]{2,1,0:T(8,128)(2,1)S(1)}, u32[]{:S(2)}, u32[]{:S(2)}) async-start(bf16[8,128,640]{2,1,0:T(8,128)(2,1)} %shard_map.73), calls=%async_computation | async-start | bytes 2621440 | tf_op jit(solution)/shard_map/all_to_all | solution.py:284
  39.0 12.0 %collective-permute-start.3 = (bf16[128,512]{1,0:T(8,128)(2,1)}, bf16[128,512]{1,0:T(8,128)(2,1)S(1)}, u32[]{:S(2)}, u32[]{:S(2)}) collective-permute-start(bf16[128,512]{1,0:T(8,128)(2,1)} %shard_map.75.k0), channel_id=1, source_target_pairs={{0,32},{32,64},{64,96},{96,128},{128,160},{160,192},{192,224},{224... | collective-permute-start | bytes 393224 | tf_op jit(solution)/shard_map/ppermute | solution.py:288
  40.6 10.4 %collective-permute-start.7 = (bf16[128,512]{1,0:T(8,128)(2,1)}, bf16[128,512]{1,0:T(8,128)(2,1)S(1)}, u32[]{:S(2)}, u32[]{:S(2)}) collective-permute-start(bf16[128,512]{1,0:T(8,128)(2,1)} %shard_map.75.k0), channel_id=1, source_target_pairs={{0,224},{32,0},{64,32},{96,64},{128,96},{160,128},{192,160},{224,1... | collective-permute-start | bytes 393224 | tf_op jit(solution)/shard_map/ppermute | solution.py:288
  51.0 27.2 %copy-start.16 = (bf16[128,512]{1,0:T(8,128)(2,1)}, bf16[128,512]{1,0:T(8,128)(2,1)S(1)}, u32[]{:S(2)}) copy-start(bf16[128,512]{1,0:T(8,128)(2,1)S(1)} %collective-permute-done.3.k1) | copy-start | bytes 393220
  51.0 9.0 %collective-permute-start.4 = (bf16[128,512]{1,0:T(8,128)(2,1)S(1)}, bf16[128,512]{1,0:T(8,128)(2,1)S(1)}, u32[]{:S(2)}, u32[]{:S(2)}) collective-permute-start(bf16[128,512]{1,0:T(8,128)(2,1)S(1)} %collective-permute-done.3.k1), channel_id=1, source_target_pairs={{0,32},{32,64},{64,96},{96,128},{128,160},{160,192},{192,224},{224... | collective-permute-start | bytes 393224 | tf_op jit(solution)/shard_map/ppermute | solution.py:288
  51.0 27.2 %copy-start.17 = (bf16[128,512]{1,0:T(8,128)(2,1)}, bf16[128,512]{1,0:T(8,128)(2,1)S(1)}, u32[]{:S(2)}) copy-start(bf16[128,512]{1,0:T(8,128)(2,1)S(1)} %collective-permute-done.7.k7) | copy-start | bytes 393220
  51.0 8.9 %collective-permute-start.8 = (bf16[128,512]{1,0:T(8,128)(2,1)S(1)}, bf16[128,512]{1,0:T(8,128)(2,1)S(1)}, u32[]{:S(2)}, u32[]{:S(2)}) collective-permute-start(bf16[128,512]{1,0:T(8,128)(2,1)S(1)} %collective-permute-done.7.k7), channel_id=1, source_target_pairs={{0,224},{32,0},{64,32},{96,64},{128,96},{160,128},{192,160},{224,1... | collective-permute-start | bytes 393224 | tf_op jit(solution)/shard_map/ppermute | solution.py:288
  59.9 18.3 %copy-start.18 = (bf16[128,512]{1,0:T(8,128)(2,1)}, bf16[128,512]{1,0:T(8,128)(2,1)S(1)}, u32[]{:S(2)}) copy-start(bf16[128,512]{1,0:T(8,128)(2,1)S(1)} %collective-permute-done.4.k2) | copy-start | bytes 393220
  59.9 5.0 %collective-permute-start.5 = (bf16[128,512]{1,0:T(8,128)(2,1)S(1)}, bf16[128,512]{1,0:T(8,128)(2,1)S(1)}, u32[]{:S(2)}, u32[]{:S(2)}) collective-permute-start(bf16[128,512]{1,0:T(8,128)(2,1)S(1)} %collective-permute-done.4.k2), channel_id=1, source_target_pairs={{0,32},{32,64},{64,96},{96,128},{128,160},{160,192},{192,224},{224... | collective-permute-start | bytes 393224 | tf_op jit(solution)/shard_map/ppermute | solution.py:288
  59.9 18.3 %copy-start.19 = (bf16[128,512]{1,0:T(8,128)(2,1)}, bf16[128,512]{1,0:T(8,128)(2,1)S(1)}, u32[]{:S(2)}) copy-start(bf16[128,512]{1,0:T(8,128)(2,1)S(1)} %collective-permute-done.8.k6) | copy-start | bytes 393220
  60.0 5.0 %collective-permute-start.9 = (bf16[128,512]{1,0:T(8,128)(2,1)S(1)}, bf16[128,512]{1,0:T(8,128)(2,1)S(1)}, u32[]{:S(2)}, u32[]{:S(2)}) collective-permute-start(bf16[128,512]{1,0:T(8,128)(2,1)S(1)} %collective-permute-done.8.k6), channel_id=1, source_target_pairs={{0,224},{32,0},{64,32},{96,64},{128,96},{160,128},{192,160},{224,1... | collective-permute-start | bytes 393224 | tf_op jit(solution)/shard_map/ppermute | solution.py:288
  65.0 13.3 %copy-start.20 = (bf16[128,512]{1,0:T(8,128)(2,1)}, bf16[128,512]{1,0:T(8,128)(2,1)S(1)}, u32[]{:S(2)}) copy-start(bf16[128,512]{1,0:T(8,128)(2,1)S(1)} %collective-permute-done.5.k3) | copy-start | bytes 393220
  65.0 5.0 %collective-permute-start.6 = (bf16[128,512]{1,0:T(8,128)(2,1)S(1)}, bf16[128,512]{1,0:T(8,128)(2,1)S(1)}, u32[]{:S(2)}, u32[]{:S(2)}) collective-permute-start(bf16[128,512]{1,0:T(8,128)(2,1)S(1)} %collective-permute-done.5.k3), channel_id=1, source_target_pairs={{0,32},{32,64},{64,96},{96,128},{128,160},{160,192},{192,224},{224... | collective-permute-start | bytes 393224 | tf_op jit(solution)/shard_map/ppermute | solution.py:288
  65.0 13.3 %copy-start.21 = (bf16[128,512]{1,0:T(8,128)(2,1)}, bf16[128,512]{1,0:T(8,128)(2,1)S(1)}, u32[]{:S(2)}) copy-start(bf16[128,512]{1,0:T(8,128)(2,1)S(1)} %collective-permute-done.9.k5) | copy-start | bytes 393220
  70.0 8.3 %copy-start.22 = (bf16[128,512]{1,0:T(8,128)(2,1)}, bf16[128,512]{1,0:T(8,128)(2,1)S(1)}, u32[]{:S(2)}) copy-start(bf16[128,512]{1,0:T(8,128)(2,1)S(1)} %collective-permute-done.6.k4) | copy-start | bytes 393220
  70.0 1.9 %copy-start.6 = (bf16[48,8,32,128]{3,2,1,0:T(8,128)(2,1)S(1)}, bf16[48,8,32,128]{3,2,1,0:T(8,128)(2,1)}, u32[]{:S(2)}) copy-start(bf16[48,8,32,128]{3,2,1,0:T(8,128)(2,1)} %all-gather.5.cloned.1.call-done) | copy-start | bytes 9437188
  78.3 15.7 %all-to-all-start.2 = ((bf16[8,4,128,128]{3,2,1,0:T(8,128)(2,1)}), bf16[8,4,128,128]{3,2,1,0:T(8,128)(2,1)S(1)}, u32[]{:S(2)}, u32[]{:S(2)}) async-start(bf16[8,4,128,128]{3,2,1,0:T(8,128)(2,1)} %shard_map.76), calls=%async_computation.2 | async-start | bytes 2097152 | tf_op jit(solution)/shard_map/all_to_all | solution.py:284
  94.1 7.1 %copy-start.8 = (bf16[4,128,128]{2,1,0:T(8,128)(2,1)}, bf16[4,128,128]{2,1,0:T(8,128)(2,1)S(1)}, u32[]{:S(2)}) copy-start(bf16[4,128,128]{2,1,0:T(8,128)(2,1)S(1)} %reduce_sum.12) | copy-start | bytes 393220
  94.1 12.4 %collective-permute-start.10 = (bf16[512,128]{1,0:T(8,128)(2,1)S(1)}, bf16[512,128]{1,0:T(8,128)(2,1)S(1)}, u32[]{:S(2)}, u32[]{:S(2)}) collective-permute-start(bf16[512,128]{1,0:T(8,128)(2,1)S(1)} %bitcast.10), channel_id=1, source_target_pairs={{0,32},{32,64},{64,96},{96,128},{128,160},{160,192},{192,224},{224... | collective-permute-start | bytes 393224 | tf_op jit(solution)/shard_map/ppermute | solution.py:288
  94.2 12.3 %collective-permute-start.11 = (bf16[512,128]{1,0:T(8,128)(2,1)S(1)}, bf16[512,128]{1,0:T(8,128)(2,1)S(1)}, u32[]{:S(2)}, u32[]{:S(2)}) collective-permute-start(bf16[512,128]{1,0:T(8,128)(2,1)S(1)} %bitcast.11), channel_id=1, source_target_pairs={{0,224},{32,0},{64,32},{96,64},{128,96},{160,128},{192,160},{224,1... | collective-permute-start | bytes 393224 | tf_op jit(solution)/shard_map/ppermute | solution.py:288
  106.5 2.9 %copy-start.11 = (bf16[512,128]{1,0:T(8,128)(2,1)}, bf16[512,128]{1,0:T(8,128)(2,1)S(1)}, u32[]{:S(2)}) copy-start(bf16[512,128]{1,0:T(8,128)(2,1)S(1)} %collective-permute-done.10.refs_2_) | copy-start | bytes 393220
  106.5 2.8 %copy-start.12 = (bf16[512,128]{1,0:T(8,128)(2,1)}, bf16[512,128]{1,0:T(8,128)(2,1)S(1)}, u32[]{:S(2)}) copy-start(bf16[512,128]{1,0:T(8,128)(2,1)S(1)} %collective-permute-done.11.refs_3_) | copy-start | bytes 393220
  106.5 6.5 %collective-permute-start.12 = (bf16[512,128]{1,0:T(8,128)(2,1)S(1)}, bf16[512,128]{1,0:T(8,128)(2,1)S(1)}, u32[]{:S(2)}, u32[]{:S(2)}) collective-permute-start(bf16[512,128]{1,0:T(8,128)(2,1)S(1)} %collective-permute-done.10.refs_2_), channel_id=1, source_target_pairs={{0,32},{32,64},{64,96},{96,128},{128,160},{160,192},{192,224},{224... | collective-permute-start | bytes 393224 | tf_op jit(solution)/shard_map/ppermute | solution.py:288
  106.6 6.4 %collective-permute-start.13 = (bf16[512,128]{1,0:T(8,128)(2,1)S(1)}, bf16[512,128]{1,0:T(8,128)(2,1)S(1)}, u32[]{:S(2)}, u32[]{:S(2)}) collective-permute-start(bf16[512,128]{1,0:T(8,128)(2,1)S(1)} %collective-permute-done.11.refs_3_), channel_id=1, source_target_pairs={{0,224},{32,0},{64,32},{96,64},{128,96},{160,128},{192,160},{224,1... | collective-permute-start | bytes 393224 | tf_op jit(solution)/shard_map/ppermute | solution.py:288
  113.0 2.8 %copy-start.9 = (bf16[512,128]{1,0:T(8,128)(2,1)}, bf16[512,128]{1,0:T(8,128)(2,1)S(1)}, u32[]{:S(2)}) copy-start(bf16[512,128]{1,0:T(8,128)(2,1)S(1)} %collective-permute-done.12.refs_2_) | copy-start | bytes 393220
  113.0 2.8 %copy-start.10 = (bf16[512,128]{1,0:T(8,128)(2,1)}, bf16[512,128]{1,0:T(8,128)(2,1)S(1)}, u32[]{:S(2)}) copy-start(bf16[512,128]{1,0:T(8,128)(2,1)S(1)} %collective-permute-done.13.refs_3_) | copy-start | bytes 393220
  113.0 6.2 %collective-permute-start.14 = (bf16[512,128]{1,0:T(8,128)(2,1)S(1)}, bf16[512,128]{1,0:T(8,128)(2,1)S(1)}, u32[]{:S(2)}, u32[]{:S(2)}) collective-permute-start(bf16[512,128]{1,0:T(8,128)(2,1)S(1)} %collective-permute-done.12.refs_2_), channel_id=1, source_target_pairs={{0,32},{32,64},{64,96},{96,128},{128,160},{160,192},{192,224},{224... | collective-permute-start | bytes 393224 | tf_op jit(solution)/shard_map/ppermute | solution.py:288
  113.7 5.5 %collective-permute-start.15 = (bf16[512,128]{1,0:T(8,128)(2,1)S(1)}, bf16[512,128]{1,0:T(8,128)(2,1)S(1)}, u32[]{:S(2)}, u32[]{:S(2)}) collective-permute-start(bf16[512,128]{1,0:T(8,128)(2,1)S(1)} %collective-permute-done.13.refs_3_), channel_id=1, source_target_pairs={{0,224},{32,0},{64,32},{96,64},{128,96},{160,128},{192,160},{224,1... | collective-permute-start | bytes 393224 | tf_op jit(solution)/shard_map/ppermute | solution.py:288
  119.2 0.9 copy-start.13
  119.2 0.9 copy-start.14
  119.2 6.7 %collective-permute-start.16 = (bf16[512,128]{1,0:T(8,128)(2,1)S(1)}, bf16[512,128]{1,0:T(8,128)(2,1)S(1)}, u32[]{:S(2)}, u32[]{:S(2)}) collective-permute-start(bf16[512,128]{1,0:T(8,128)(2,1)S(1)} %collective-permute-done.14.refs_2_), channel_id=1, source_target_pairs={{0,32},{32,64},{64,96},{96,128},{128,160},{160,192},{192,224},{224... | collective-permute-start | bytes 393224 | tf_op jit(solution)/shard_map/ppermute | solution.py:288
  125.9 0.7 copy-start.15
  130.5 15.1 %all-to-all-start.3 = ((bf16[8,4,128,128]{3,2,1,0:T(8,128)(2,1)}), bf16[8,4,128,128]{3,2,1,0:T(8,128)(2,1)S(1)}, u32[]{:S(2)}, u32[]{:S(2)}) async-start(bf16[8,4,128,128]{3,2,1,0:T(8,128)(2,1)} %shard_map.82), calls=%async_computation.3 | async-start | bytes 2097152 | tf_op jit(solution)/shard_map/all_to_all | solution.py:284
  135.3 10.3 %copy-start.4 = (s32[3]{0:T(128)S(1)}, s32[3]{0:T(128)}, u32[]{:S(2)}) copy-start(s32[3]{0:T(128)} %copy-done.3) | copy-start | bytes 40
  145.6 2.8 %copy-start = (bf16[8,768,512]{2,1,0:T(8,128)(2,1)S(1)}, bf16[8,768,512]{2,1,0:T(8,128)(2,1)}, u32[]{:S(2)}) copy-start(bf16[8,768,512]{2,1,0:T(8,128)(2,1)} %shard_map.83.rows) | copy-start | bytes 18874372
  151.6 10.5 %collective-permute-start.17 = (bf16[2,8,128,128]{3,2,1,0:T(8,128)(2,1)S(1)}, bf16[2,8,128,128]{3,2,1,0:T(8,128)(2,1)S(1)}, u32[]{:S(2)}, u32[]{:S(2)}) collective-permute-start(bf16[2,8,128,128]{3,2,1,0:T(8,128)(2,1)S(1)} %get-tuple-element.56), channel_id=1, source_target_pairs={{0,1},{1,0},{2,3},{3,2},{4,5},{5,4},{6,7},{7,6},{8,9},{9,8},{10,11... | collective-permute-start | bytes 1572872 | tf_op jit(solution)/shard_map/ppermute | solution.py:280
Sparse Core Ops, SparseCore 0:
  9.1 54.1 all-gather.4
  65.1 47.0 all-gather.6

commit v5 on v4

--- a/solution.py
+++ b/solution.py
@@ -406,15 +406,13 @@
                 scratch_shapes=[pltpu.VMEM((slab, LANES), f32)],
             ),
             out_shape=out_shape,
-            compiler_params=large,
+            compiler_params=small,
             cost_estimate=cost(steps * 2 * slab * slab * 128, steps * 2_000_000),
         )(place, probs, *[values[s] for s in near], *carried)
 
     values[1], values[7] = ring_step(own_values, 1), ring_step(own_values, -1)
-    acc = weighted((0,), (), False)
-    values[1], values[7], acc = lax.optimization_barrier((values[1], values[7], acc))
     values[2], values[6] = ring_step(values[1], 1), ring_step(values[7], -1)
-    acc = weighted((1, 7), (acc,), False)
+    acc = weighted((0, 1, 7), (), False)
     values[2], values[6], acc = lax.optimization_barrier((values[2], values[6], acc))
     values[3], values[5] = ring_step(values[2], 1), ring_step(values[6], -1)
     acc = weighted((2, 6), (acc,), False)

time: 188 us -> 187 us (level)
  Pallas kernels: 56 us -> 42.5 us
  waiting for transfers between devices: 33.9 us -> 41 us
  local copies, waits for them, and re-layouts: 8.37 us -> 13.5 us
    pallas_call x5 -> x4, Pallas kernels: 17.9 us -> 4.55 us  [weighted(): pl.pallas_call(lambda *refs: attend_kernel(near, len(carried), last, *ref...]
    ppermute x14, waiting for transfers between devices: 24.4 us -> 31.4 us  [ring_step(): return lax.ppermute(x, 'z', [(i, (i + way) % SLABS) for i in range(SLABS)])]
    unnamed x47 -> x37, local copies, waits for them, and re-layouts: 8.24 us -> 13.3 us
  transfers between devices with their start and end apart: 24 -> 24, of which waited for: 12 -> 11; matrix products, arithmetic and copies ran while one was open for 1% -> 1% of each run, Pallas kernels for 27% -> 20%
where the time goes in v5:
time: 187 us; the launch traced here: 186 us
  starting transfers between devices  59.5 us (32%)
  Pallas kernels  42.5 us (23%)
  waiting for transfers between devices  41 us (22%)
  blocking collectives  15.8 us (8%)
  between operations  13.7 us (7%)
  local copies, waits for them, and re-layouts  13.5 us (7%)
    ppermute x14, waiting for transfers between devices, ring_step(): return lax.ppermute(x, 'z', [(i, (i + way) % SLABS) for i in range(SLABS)])  31.4 us
    ppermute x14, starting transfers between devices, ring_step(): return lax.ppermute(x, 'z', [(i, (i + way) % SLABS) for i in range(SLABS)])  23.6 us
    all_to_all x4, starting transfers between devices, plane_exchange(): lax.all_to_all(x, PLANE_AXES, split_axis=0, concat_axis=0, tiled=True)  18.7 us
    ppermute x4, starting transfers between devices, swap(): return lax.ppermute(x, axis, [(0, 1), (1, 0)])  17.2 us
    all_to_all x1, blocking collectives, body(): lax.all_to_all(near.reshape(2 * PLANE, BLK, LANES), ('yh',) + PLANE_AXES,...  15.8 us
    unnamed x37, local copies, waits for them, and re-layouts  13.3 us
    pallas_call x1, Pallas kernels, body(): pl.pallas_call(weight_kernel, grid=(PLANE + 1,), out_shape=(jax.ShapeDtyp...  10.6 us
    pallas_call x1, Pallas kernels, body(): pl.pallas_call(chosen_kernel, grid=(PLANE,), out_shape=jax.ShapeDtypeStru...  9.79 us
  transfers between devices with their start and end apart: 24, of which 11 were waited for; matrix products, arithmetic and copies ran while one was open for 1% of the time, Pallas kernels for 20%

profile of v5, /device:TPU:1, one launch (start us, length us, event | category | flops | bytes accessed | tf_op | source)
XLA Modules:
  0.0 186.3 jit_solution(4577589874072977282)
XLA Ops:
  6.5 0.7 all-gather.5.cloned.1.call-update
  7.3 0.0 all-gather.7.cloned.1.call-start
  7.3 0.7 all-gather.7.cloned.1.call-update
  8.0 3.8 %collective-permute-start.1 = (bf16[128,1024]{1,0:T(8,128)(2,1)}, bf16[128,1024]{1,0:T(8,128)(2,1)S(1)}, u32[]{:S(2)}, u32[]{:S(2)}) collective-permute-start(bf16[128,1024]{1,0:T(8,128)(2,1)} %f0.1), channel_id=1, source_target_pairs={{0,2},{2,0},{1,3},{3,1},{4,6},{6,4},{5,7},{7,5},{8,10},{10,8},{9,1... | collective-permute-start | bytes 786440 | tf_op jit(solution)/shard_map/ppermute | solution.py:280
  11.8 1.0 collective-permute-start
  12.8 4.3 %collective-permute-done.1.f2 = bf16[128,1024]{1,0:T(8,128)(2,1)S(1)} collective-permute-done((bf16[128,1024]{1,0:T(8,128)(2,1)}, bf16[128,1024]{1,0:T(8,128)(2,1)S(1)}, u32[]{:S(2)}, u32[]{:S(2)}) %collective-permute-start.1) | collective-permute-done | bytes 262176 | tf_op jit(solution)/shard_map/ppermute | solution.py:280
  17.1 2.3 %collective-permute-start.2 = (bf16[128,1024]{1,0:T(8,128)(2,1)S(1)}, bf16[128,1024]{1,0:T(8,128)(2,1)S(1)}, u32[]{:S(2)}, u32[]{:S(2)}) collective-permute-start(bf16[128,1024]{1,0:T(8,128)(2,1)S(1)} %collective-permute-done.1.f2), channel_id=1, source_target_pairs={{0,1},{1,0},{2,3},{3,2},{4,5},{5,4},{6,7},{7,6},{8,9},{9,8},{10,11... | collective-permute-start | bytes 786440 | tf_op jit(solution)/shard_map/ppermute | solution.py:280
  19.4 1.8 shard_map.74
  21.2 5.0 %all-to-all-start.1 = ((bf16[8,128,128]{2,1,0:T(8,128)(2,1)}), bf16[8,128,128]{2,1,0:T(8,128)(2,1)S(1)}, u32[]{:S(2)}, u32[]{:S(2)}) async-start(bf16[8,128,128]{2,1,0:T(8,128)(2,1)} %shard_map.74), calls=%async_computation.1 | async-start | bytes 524288 | tf_op jit(solution)/shard_map/all_to_all | solution.py:284
  26.2 0.9 copy.9
  27.0 0.1 reshape.9.ids
  27.2 0.1 pad_add_fusion.place.refs_0_
  27.3 0.0 collective-permute-done.f1
  27.3 0.0 collective-permute-done.2.f3
  27.3 0.0 copy-start.3
  27.3 1.0 copy-done.3
  28.3 0.9 copy-done.4
  29.2 2.7 %shard_map.73 = bf16[8,128,640]{2,1,0:T(8,128)(2,1)} custom-call(s32[768]{0:T(1024)S(1)} %reshape.9.ids, s32[3]{0:T(128)S(1)} %pad_add_fusion.place.refs_0_, bf16[128,1024]{1,0:T(8,128)(2,1)S(1)} %copy-done.4, bf16[128,1024]{1,0:T(8,128)(2,1)S(1)} %collective-permute-done.f1, bf16[128,1024]{1,0:T(8,128)(2,1)S(1)} %collective-permute-done.1.f2, ...), custom_call_target="tpu_custom_call" | custom-call | flops 268435456 | bytes 3000000 | tf_op jit(solution)/shard_map/pallas_call | solution.py:327
  31.9 1.7 all-to-all-done.1.pairs
  33.6 3.6 %all-to-all-start = ((bf16[8,128,640]{2,1,0:T(8,128)(2,1)}), bf16[8,128,640]{2,1,0:T(8,128)(2,1)S(1)}, u32[]{:S(2)}, u32[]{:S(2)}) async-start(bf16[8,128,640]{2,1,0:T(8,128)(2,1)} %shard_map.73), calls=%async_computation | async-start | bytes 2621440 | tf_op jit(solution)/shard_map/all_to_all | solution.py:284
  37.2 1.8 shard_map.75.k0
  39.0 1.6 collective-permute-start.3
  40.6 3.9 %collective-permute-start.7 = (bf16[128,512]{1,0:T(8,128)(2,1)}, bf16[128,512]{1,0:T(8,128)(2,1)S(1)}, u32[]{:S(2)}, u32[]{:S(2)}) collective-permute-start(bf16[128,512]{1,0:T(8,128)(2,1)} %shard_map.75.k0), channel_id=1, source_target_pairs={{0,224},{32,0},{64,32},{96,64},{128,96},{160,128},{192,160},{224,1... | collective-permute-start | bytes 393224 | tf_op jit(solution)/shard_map/ppermute | solution.py:288
  44.6 6.4 %collective-permute-done.3.k1 = bf16[128,512]{1,0:T(8,128)(2,1)S(1)} collective-permute-done((bf16[128,512]{1,0:T(8,128)(2,1)}, bf16[128,512]{1,0:T(8,128)(2,1)S(1)}, u32[]{:S(2)}, u32[]{:S(2)}) %collective-permute-start.3) | collective-permute-done | bytes 131104 | tf_op jit(solution)/shard_map/ppermute | solution.py:288
  51.0 0.0 collective-permute-start.4
  51.0 2.7 %collective-permute-start.8 = (bf16[128,512]{1,0:T(8,128)(2,1)S(1)}, bf16[128,512]{1,0:T(8,128)(2,1)S(1)}, u32[]{:S(2)}, u32[]{:S(2)}) collective-permute-start(bf16[128,512]{1,0:T(8,128)(2,1)S(1)} %collective-permute-done.7.k7), channel_id=1, source_target_pairs={{0,224},{32,0},{64,32},{96,64},{128,96},{160,128},{192,160},{224,1... | collective-permute-start | bytes 393224 | tf_op jit(solution)/shard_map/ppermute | solution.py:288
  53.7 6.3 %collective-permute-done.4.k2 = bf16[128,512]{1,0:T(8,128)(2,1)S(1)} collective-permute-done((bf16[128,512]{1,0:T(8,128)(2,1)S(1)}, bf16[128,512]{1,0:T(8,128)(2,1)S(1)}, u32[]{:S(2)}, u32[]{:S(2)}) %collective-permute-start.4) | collective-permute-done | bytes 131104 | tf_op jit(solution)/shard_map/ppermute | solution.py:288
  60.0 2.7 %collective-permute-start.9 = (bf16[128,512]{1,0:T(8,128)(2,1)S(1)}, bf16[128,512]{1,0:T(8,128)(2,1)S(1)}, u32[]{:S(2)}, u32[]{:S(2)}) collective-permute-start(bf16[128,512]{1,0:T(8,128)(2,1)S(1)} %collective-permute-done.8.k6), channel_id=1, source_target_pairs={{0,224},{32,0},{64,32},{96,64},{128,96},{160,128},{192,160},{224,1... | collective-permute-start | bytes 393224 | tf_op jit(solution)/shard_map/ppermute | solution.py:288
  62.6 2.3 %collective-permute-done.5.k3 = bf16[128,512]{1,0:T(8,128)(2,1)S(1)} collective-permute-done((bf16[128,512]{1,0:T(8,128)(2,1)S(1)}, bf16[128,512]{1,0:T(8,128)(2,1)S(1)}, u32[]{:S(2)}, u32[]{:S(2)}) %collective-permute-start.5) | collective-permute-done | bytes 131104 | tf_op jit(solution)/shard_map/ppermute | solution.py:288
  65.0 5.0 %collective-permute-done.6.k4 = bf16[128,512]{1,0:T(8,128)(2,1)S(1)} collective-permute-done((bf16[128,512]{1,0:T(8,128)(2,1)S(1)}, bf16[128,512]{1,0:T(8,128)(2,1)S(1)}, u32[]{:S(2)}, u32[]{:S(2)}) %collective-permute-start.6) | collective-permute-done | bytes 131104 | tf_op jit(solution)/shard_map/ppermute | solution.py:288
  70.0 1.9 %copy-done.9 = bf16[48,8,32,128]{3,2,1,0:T(8,128)(2,1)S(1)} copy-done((bf16[48,8,32,128]{3,2,1,0:T(8,128)(2,1)S(1)}, bf16[48,8,32,128]{3,2,1,0:T(8,128)(2,1)}, u32[]{:S(2)}) %copy-start.9) | copy-done | bytes 3145752
  72.0 6.3 %shard_map.76 = bf16[8,4,128,128]{3,2,1,0:T(8,128)(2,1)} custom-call(s32[768]{0:T(1024)S(1)} %reshape.9.ids, s32[3]{0:T(128)S(1)} %pad_add_fusion.place.refs_0_, bf16[8,128,640]{2,1,0:T(8,128)(2,1)S(1)} %all-to-all-done.message.gates_in, bf16[8,6,8,32,128]{4,3,2,1,0:T(8,128)(2,1)S(1)} %bitcast.10), custom_call_target="tpu_custom_call" | custom-call | flops 1610612736 | bytes 6000000 | tf_op jit(solution)/shard_map/pallas_call | solution.py:342
  78.3 4.9 %all-to-all-start.2 = ((bf16[8,4,128,128]{3,2,1,0:T(8,128)(2,1)}), bf16[8,4,128,128]{3,2,1,0:T(8,128)(2,1)S(1)}, u32[]{:S(2)}, u32[]{:S(2)}) async-start(bf16[8,4,128,128]{3,2,1,0:T(8,128)(2,1)} %shard_map.76), calls=%async_computation.2 | async-start | bytes 2097152 | tf_op jit(solution)/shard_map/all_to_all | solution.py:284
  83.2 10.6 %shard_map.77 = (bf16[8,2,1024,512]{3,2,1,0:T(8,128)(2,1)}, f32[1024,128]{1,0:T(8,128)}) custom-call(s32[3]{0:T(128)} %copy-done.6, bf16[8,128,128]{2,1,0:T(8,128)(2,1)} %copy-done.10, bf16[128,512]{1,0:T(8,128)(2,1)} %shard_map.75.k0, bf16[128,512]{1,0:T(8,128)(2,1)} %copy-done.11, bf16[128,512]{1,0:T(8,128)(2,1)} %copy-done.13, ...), custom_call_target="tpu_custom_call" | custom-call | flops 2147483648 | bytes 18000000 | tf_op jit(solution)/shard_map/pallas_call | solution.py:351
  93.9 0.0 all-to-all-done.2
  93.9 0.1 reduce_sum.12
  94.0 0.1 collective-permute-start.10
  94.1 7.0 %collective-permute-start.12 = (bf16[512,128]{1,0:T(8,128)(2,1)S(1)}, bf16[512,128]{1,0:T(8,128)(2,1)S(1)}, u32[]{:S(2)}, u32[]{:S(2)}) collective-permute-start(bf16[512,128]{1,0:T(8,128)(2,1)S(1)} %bitcast.8), channel_id=1, source_target_pairs={{0,224},{32,0},{64,32},{96,64},{128,96},{160,128},{192,160},{224,1... | collective-permute-start | bytes 393224 | tf_op jit(solution)/shard_map/ppermute | solution.py:288
  101.2 5.4 %collective-permute-done.10.refs_3_ = bf16[512,128]{1,0:T(8,128)(2,1)S(1)} collective-permute-done((bf16[512,128]{1,0:T(8,128)(2,1)S(1)}, bf16[512,128]{1,0:T(8,128)(2,1)S(1)}, u32[]{:S(2)}, u32[]{:S(2)}) %collective-permute-start.10) | collective-permute-done | bytes 131104 | tf_op jit(solution)/shard_map/ppermute | solution.py:288
  106.6 0.0 collective-permute-start.11
  106.6 0.0 collective-permute-done.12.refs_4_
  106.6 2.8 %collective-permute-start.13 = (bf16[512,128]{1,0:T(8,128)(2,1)S(1)}, bf16[512,128]{1,0:T(8,128)(2,1)S(1)}, u32[]{:S(2)}, u32[]{:S(2)}) collective-permute-start(bf16[512,128]{1,0:T(8,128)(2,1)S(1)} %collective-permute-done.12.refs_4_), channel_id=1, source_target_pairs={{0,224},{32,0},{64,32},{96,64},{128,96},{160,128},{192,160},{224,1... | collective-permute-start | bytes 393224 | tf_op jit(solution)/shard_map/ppermute | solution.py:288
  109.3 5.8 %copy-done = bf16[8,2,1024,512]{3,2,1,0:T(8,128)(2,1)S(1)} copy-done((bf16[8,2,1024,512]{3,2,1,0:T(8,128)(2,1)S(1)}, bf16[8,2,1024,512]{3,2,1,0:T(8,128)(2,1)}, u32[]{:S(2)}) %copy-start) | copy-done | bytes 16777240
  115.1 1.4 shard_map.78.refs_4_
  116.5 0.0 collective-permute-done.11.refs_2_
  116.6 0.1 collective-permute-start.14
  116.7 2.7 %collective-permute-start.15 = (bf16[512,128]{1,0:T(8,128)(2,1)S(1)}, bf16[512,128]{1,0:T(8,128)(2,1)S(1)}, u32[]{:S(2)}, u32[]{:S(2)}) collective-permute-start(bf16[512,128]{1,0:T(8,128)(2,1)S(1)} %collective-permute-done.13.refs_3_), channel_id=1, source_target_pairs={{0,224},{32,0},{64,32},{96,64},{128,96},{160,128},{192,160},{224,1... | collective-permute-start | bytes 393224 | tf_op jit(solution)/shard_map/ppermute | solution.py:288
  119.3 0.7 shard_map.79.refs_4_
  120.0 1.7 collective-permute-done.14.refs_2_
  121.7 0.0 collective-permute-done.15.refs_3_
  121.7 0.7 shard_map.80.refs_3_
  122.4 4.3 %collective-permute-done.16.refs_2_ = bf16[512,128]{1,0:T(8,128)(2,1)S(1)} collective-permute-done((bf16[512,128]{1,0:T(8,128)(2,1)S(1)}, bf16[512,128]{1,0:T(8,128)(2,1)S(1)}, u32[]{:S(2)}, u32[]{:S(2)}) %collective-permute-start.16) | collective-permute-done | bytes 131104 | tf_op jit(solution)/shard_map/ppermute | solution.py:288
  126.7 1.8 shard_map.81
  128.5 5.2 %all-to-all-start.3 = ((bf16[8,4,128,128]{3,2,1,0:T(8,128)(2,1)}), bf16[8,4,128,128]{3,2,1,0:T(8,128)(2,1)S(1)}, u32[]{:S(2)}, u32[]{:S(2)}) async-start(bf16[8,4,128,128]{3,2,1,0:T(8,128)(2,1)} %shard_map.81), calls=%async_computation.3 | async-start | bytes 2097152 | tf_op jit(solution)/shard_map/all_to_all | solution.py:284
  133.7 0.0 all-gather.7.cloned.1.call-done
  133.7 9.8 %shard_map.82.rows = bf16[8,768,512]{2,1,0:T(8,128)(2,1)} custom-call(s32[768]{0:T(1024)} %copy-done.5, s32[3]{0:T(128)} %copy-done.6, bf16[8,6,8,32,128]{4,3,2,1,0:T(8,128)(2,1)} %bitcast.11), custom_call_target="tpu_custom_call" | custom-call | bytes 20000000 | tf_op jit(solution)/shard_map/pallas_call | solution.py:427
  143.5 0.5 all-to-all-done.3.attended
  144.0 2.8 %copy-done.1 = bf16[8,768,512]{2,1,0:T(8,128)(2,1)S(1)} copy-done((bf16[8,768,512]{2,1,0:T(8,128)(2,1)S(1)}, bf16[8,768,512]{2,1,0:T(8,128)(2,1)}, u32[]{:S(2)}) %copy-start.1) | copy-done | bytes 6291480
  146.8 3.2 %shard_map.83 = (bf16[2,8,128,128]{3,2,1,0:T(8,128)(2,1)S(1)}, bf16[2,8,128,128]{3,2,1,0:T(8,128)(2,1)S(1)}) custom-call(s32[3]{0:T(128)S(1)} %copy-done.8, bf16[8,4,128,128]{3,2,1,0:T(8,128)(2,1)S(1)} %all-to-all-done.3.attended, bf16[8,128,640]{2,1,0:T(8,128)(2,1)S(1)} %all-to-all-done.message.gates_in, bf16[8,768,512]{2,1,0:T(8,128)(2,1)S(1)} %copy-done.1), custom_call_target="tpu_custom_call" | custom-call | flops 805306368 | bytes 8000000 | tf_op jit(solution)/shard_map/pallas_call | solution.py:439
  150.0 10.1 %collective-permute-start.17 = (bf16[2,8,128,128]{3,2,1,0:T(8,128)(2,1)S(1)}, bf16[2,8,128,128]{3,2,1,0:T(8,128)(2,1)S(1)}, u32[]{:S(2)}, u32[]{:S(2)}) collective-permute-start(bf16[2,8,128,128]{3,2,1,0:T(8,128)(2,1)S(1)} %get-tuple-element.50), channel_id=1, source_target_pairs={{0,1},{1,0},{2,3},{3,2},{4,5},{5,4},{6,7},{7,6},{8,9},{9,8},{10,11... | collective-permute-start | bytes 1572872 | tf_op jit(solution)/shard_map/ppermute | solution.py:280
  160.1 1.5 collective-permute-done.17
  161.7 0.1 add_convert_fusion
  161.8 15.8 %all_to_all.25.pieces = bf16[16,128,128]{2,1,0:T(8,128)(2,1)} all-to-all(bf16[16,128,128]{2,1,0:T(8,128)(2,1)S(1)} %bitcast.12), channel_id=1, replica_groups=mesh['z'=8,'yl'=2,'x'=4,'yh'=2,'c'=2] {'yh','yl','x'}, dimensions={0} | all-to-all | bytes 1048576 | tf_op jit(solution)/shard_map/all_to_all | solution.py:459
  177.6 1.9 %shard_map.84 = bf16[128,1024]{1,0:T(8,128)(2,1)} custom-call(bf16[16,128,128]{2,1,0:T(8,128)(2,1)} %all_to_all.25.pieces), custom_call_target="tpu_custom_call" | custom-call | bytes 600000 | tf_op jit(solution)/shard_map/pallas_call | solution.py:462
  (40 shorter events, 0.1 us)
Async XLA Ops:
  6.5 63.5 %all-gather.5.cloned.1.call-start = ((), (), s32[]{:S(2)}) async-start(), calls=%async_computation.5 | async-start | bytes 3538944 | tf_op jit(solution)/shard_map/all_gather | solution.py:304
  7.3 126.5 %all-gather.7.cloned.1.call-start = ((), (), s32[]{:S(2)}) async-start(), calls=%async_computation.6 | async-start | bytes 3538944 | tf_op jit(solution)/shard_map/all_gather | solution.py:378
  8.0 9.1 %collective-permute-start.1 = (bf16[128,1024]{1,0:T(8,128)(2,1)}, bf16[128,1024]{1,0:T(8,128)(2,1)S(1)}, u32[]{:S(2)}, u32[]{:S(2)}) collective-permute-start(bf16[128,1024]{1,0:T(8,128)(2,1)} %f0.1), channel_id=1, source_target_pairs={{0,2},{2,0},{1,3},{3,1},{4,6},{6,4},{5,7},{7,5},{8,10},{10,8},{9,1... | collective-permute-start | bytes 786440 | tf_op jit(solution)/shard_map/ppermute | solution.py:280
  11.8 15.4 %collective-permute-start = (bf16[128,1024]{1,0:T(8,128)(2,1)}, bf16[128,1024]{1,0:T(8,128)(2,1)S(1)}, u32[]{:S(2)}, u32[]{:S(2)}) collective-permute-start(bf16[128,1024]{1,0:T(8,128)(2,1)} %f0.1), channel_id=1, source_target_pairs={{0,1},{1,0},{2,3},{3,2},{4,5},{5,4},{6,7},{7,6},{8,9},{9,8},{10,11... | collective-permute-start | bytes 786440 | tf_op jit(solution)/shard_map/ppermute | solution.py:280
  17.1 10.1 %collective-permute-start.2 = (bf16[128,1024]{1,0:T(8,128)(2,1)S(1)}, bf16[128,1024]{1,0:T(8,128)(2,1)S(1)}, u32[]{:S(2)}, u32[]{:S(2)}) collective-permute-start(bf16[128,1024]{1,0:T(8,128)(2,1)S(1)} %collective-permute-done.1.f2), channel_id=1, source_target_pairs={{0,1},{1,0},{2,3},{3,2},{4,5},{5,4},{6,7},{7,6},{8,9},{9,8},{10,11... | collective-permute-start | bytes 786440 | tf_op jit(solution)/shard_map/ppermute | solution.py:280
  21.2 12.4 %all-to-all-start.1 = ((bf16[8,128,128]{2,1,0:T(8,128)(2,1)}), bf16[8,128,128]{2,1,0:T(8,128)(2,1)S(1)}, u32[]{:S(2)}, u32[]{:S(2)}) async-start(bf16[8,128,128]{2,1,0:T(8,128)(2,1)} %shard_map.74), calls=%async_computation.1 | async-start | bytes 524288 | tf_op jit(solution)/shard_map/all_to_all | solution.py:284
  27.2 51.1 %copy-start.5 = (s32[768]{0:T(1024)}, s32[768]{0:T(1024)S(1)}, u32[]{:S(2)}) copy-start(s32[768]{0:T(1024)S(1)} %reshape.9.ids) | copy-start | bytes 9220
  27.3 51.0 %copy-start.6 = (s32[3]{0:T(128)}, s32[3]{0:T(128)S(1)}, u32[]{:S(2)}) copy-start(s32[3]{0:T(128)S(1)} %pad_add_fusion.place.refs_0_) | copy-start | bytes 40
  27.3 1.0 copy-start.3
  28.3 0.9 copy-start.4
  33.6 3.6 %copy-start.10 = (bf16[8,128,128]{2,1,0:T(8,128)(2,1)}, bf16[8,128,128]{2,1,0:T(8,128)(2,1)S(1)}, u32[]{:S(2)}) copy-start(bf16[8,128,128]{2,1,0:T(8,128)(2,1)S(1)} %all-to-all-done.1.pairs) | copy-start | bytes 786436
  33.6 36.4 %all-to-all-start = ((bf16[8,128,640]{2,1,0:T(8,128)(2,1)}), bf16[8,128,640]{2,1,0:T(8,128)(2,1)S(1)}, u32[]{:S(2)}, u32[]{:S(2)}) async-start(bf16[8,128,640]{2,1,0:T(8,128)(2,1)} %shard_map.73), calls=%async_computation | async-start | bytes 2621440 | tf_op jit(solution)/shard_map/all_to_all | solution.py:284
  39.0 12.0 %collective-permute-start.3 = (bf16[128,512]{1,0:T(8,128)(2,1)}, bf16[128,512]{1,0:T(8,128)(2,1)S(1)}, u32[]{:S(2)}, u32[]{:S(2)}) collective-permute-start(bf16[128,512]{1,0:T(8,128)(2,1)} %shard_map.75.k0), channel_id=1, source_target_pairs={{0,32},{32,64},{64,96},{96,128},{128,160},{160,192},{192,224},{224... | collective-permute-start | bytes 393224 | tf_op jit(solution)/shard_map/ppermute | solution.py:288
  40.6 10.4 %collective-permute-start.7 = (bf16[128,512]{1,0:T(8,128)(2,1)}, bf16[128,512]{1,0:T(8,128)(2,1)S(1)}, u32[]{:S(2)}, u32[]{:S(2)}) collective-permute-start(bf16[128,512]{1,0:T(8,128)(2,1)} %shard_map.75.k0), channel_id=1, source_target_pairs={{0,224},{32,0},{64,32},{96,64},{128,96},{160,128},{192,160},{224,1... | collective-permute-start | bytes 393224 | tf_op jit(solution)/shard_map/ppermute | solution.py:288
  51.0 27.2 %copy-start.11 = (bf16[128,512]{1,0:T(8,128)(2,1)}, bf16[128,512]{1,0:T(8,128)(2,1)S(1)}, u32[]{:S(2)}) copy-start(bf16[128,512]{1,0:T(8,128)(2,1)S(1)} %collective-permute-done.3.k1) | copy-start | bytes 393220
  51.0 9.0 %collective-permute-start.4 = (bf16[128,512]{1,0:T(8,128)(2,1)S(1)}, bf16[128,512]{1,0:T(8,128)(2,1)S(1)}, u32[]{:S(2)}, u32[]{:S(2)}) collective-permute-start(bf16[128,512]{1,0:T(8,128)(2,1)S(1)} %collective-permute-done.3.k1), channel_id=1, source_target_pairs={{0,32},{32,64},{64,96},{96,128},{128,160},{160,192},{192,224},{224... | collective-permute-start | bytes 393224 | tf_op jit(solution)/shard_map/ppermute | solution.py:288
  51.0 27.2 %copy-start.12 = (bf16[128,512]{1,0:T(8,128)(2,1)}, bf16[128,512]{1,0:T(8,128)(2,1)S(1)}, u32[]{:S(2)}) copy-start(bf16[128,512]{1,0:T(8,128)(2,1)S(1)} %collective-permute-done.7.k7) | copy-start | bytes 393220
  51.0 8.9 %collective-permute-start.8 = (bf16[128,512]{1,0:T(8,128)(2,1)S(1)}, bf16[128,512]{1,0:T(8,128)(2,1)S(1)}, u32[]{:S(2)}, u32[]{:S(2)}) collective-permute-start(bf16[128,512]{1,0:T(8,128)(2,1)S(1)} %collective-permute-done.7.k7), channel_id=1, source_target_pairs={{0,224},{32,0},{64,32},{96,64},{128,96},{160,128},{192,160},{224,1... | collective-permute-start | bytes 393224 | tf_op jit(solution)/shard_map/ppermute | solution.py:288
  59.9 18.3 %copy-start.13 = (bf16[128,512]{1,0:T(8,128)(2,1)}, bf16[128,512]{1,0:T(8,128)(2,1)S(1)}, u32[]{:S(2)}) copy-start(bf16[128,512]{1,0:T(8,128)(2,1)S(1)} %collective-permute-done.4.k2) | copy-start | bytes 393220
  60.0 5.0 %collective-permute-start.5 = (bf16[128,512]{1,0:T(8,128)(2,1)S(1)}, bf16[128,512]{1,0:T(8,128)(2,1)S(1)}, u32[]{:S(2)}, u32[]{:S(2)}) collective-permute-start(bf16[128,512]{1,0:T(8,128)(2,1)S(1)} %collective-permute-done.4.k2), channel_id=1, source_target_pairs={{0,32},{32,64},{64,96},{96,128},{128,160},{160,192},{192,224},{224... | collective-permute-start | bytes 393224 | tf_op jit(solution)/shard_map/ppermute | solution.py:288
  60.0 18.3 %copy-start.14 = (bf16[128,512]{1,0:T(8,128)(2,1)}, bf16[128,512]{1,0:T(8,128)(2,1)S(1)}, u32[]{:S(2)}) copy-start(bf16[128,512]{1,0:T(8,128)(2,1)S(1)} %collective-permute-done.8.k6) | copy-start | bytes 393220
  60.0 5.0 %collective-permute-start.9 = (bf16[128,512]{1,0:T(8,128)(2,1)S(1)}, bf16[128,512]{1,0:T(8,128)(2,1)S(1)}, u32[]{:S(2)}, u32[]{:S(2)}) collective-permute-start(bf16[128,512]{1,0:T(8,128)(2,1)S(1)} %collective-permute-done.8.k6), channel_id=1, source_target_pairs={{0,224},{32,0},{64,32},{96,64},{128,96},{160,128},{192,160},{224,1... | collective-permute-start | bytes 393224 | tf_op jit(solution)/shard_map/ppermute | solution.py:288
  65.0 13.3 %copy-start.15 = (bf16[128,512]{1,0:T(8,128)(2,1)}, bf16[128,512]{1,0:T(8,128)(2,1)S(1)}, u32[]{:S(2)}) copy-start(bf16[128,512]{1,0:T(8,128)(2,1)S(1)} %collective-permute-done.5.k3) | copy-start | bytes 393220
  65.0 5.0 %collective-permute-start.6 = (bf16[128,512]{1,0:T(8,128)(2,1)S(1)}, bf16[128,512]{1,0:T(8,128)(2,1)S(1)}, u32[]{:S(2)}, u32[]{:S(2)}) collective-permute-start(bf16[128,512]{1,0:T(8,128)(2,1)S(1)} %collective-permute-done.5.k3), channel_id=1, source_target_pairs={{0,32},{32,64},{64,96},{96,128},{128,160},{160,192},{192,224},{224... | collective-permute-start | bytes 393224 | tf_op jit(solution)/shard_map/ppermute | solution.py:288
  65.0 13.3 %copy-start.16 = (bf16[128,512]{1,0:T(8,128)(2,1)}, bf16[128,512]{1,0:T(8,128)(2,1)S(1)}, u32[]{:S(2)}) copy-start(bf16[128,512]{1,0:T(8,128)(2,1)S(1)} %collective-permute-done.9.k5) | copy-start | bytes 393220
  70.0 8.3 %copy-start.17 = (bf16[128,512]{1,0:T(8,128)(2,1)}, bf16[128,512]{1,0:T(8,128)(2,1)S(1)}, u32[]{:S(2)}) copy-start(bf16[128,512]{1,0:T(8,128)(2,1)S(1)} %collective-permute-done.6.k4) | copy-start | bytes 393220
  70.0 1.9 %copy-start.9 = (bf16[48,8,32,128]{3,2,1,0:T(8,128)(2,1)S(1)}, bf16[48,8,32,128]{3,2,1,0:T(8,128)(2,1)}, u32[]{:S(2)}) copy-start(bf16[48,8,32,128]{3,2,1,0:T(8,128)(2,1)} %all-gather.5.cloned.1.call-done) | copy-start | bytes 9437188
  78.3 15.6 %all-to-all-start.2 = ((bf16[8,4,128,128]{3,2,1,0:T(8,128)(2,1)}), bf16[8,4,128,128]{3,2,1,0:T(8,128)(2,1)S(1)}, u32[]{:S(2)}, u32[]{:S(2)}) async-start(bf16[8,4,128,128]{3,2,1,0:T(8,128)(2,1)} %shard_map.76), calls=%async_computation.2 | async-start | bytes 2097152 | tf_op jit(solution)/shard_map/all_to_all | solution.py:284
  83.2 26.1 %copy-start.7 = (s32[3]{0:T(128)S(1)}, s32[3]{0:T(128)}, u32[]{:S(2)}) copy-start(s32[3]{0:T(128)} %copy-done.6) | copy-start | bytes 40
  94.0 12.5 %collective-permute-start.10 = (bf16[512,128]{1,0:T(8,128)(2,1)S(1)}, bf16[512,128]{1,0:T(8,128)(2,1)S(1)}, u32[]{:S(2)}, u32[]{:S(2)}) collective-permute-start(bf16[512,128]{1,0:T(8,128)(2,1)S(1)} %bitcast.7), channel_id=1, source_target_pairs={{0,32},{32,64},{64,96},{96,128},{128,160},{160,192},{192,224},{224... | collective-permute-start | bytes 393224 | tf_op jit(solution)/shard_map/ppermute | solution.py:288
  94.1 12.4 %collective-permute-start.12 = (bf16[512,128]{1,0:T(8,128)(2,1)S(1)}, bf16[512,128]{1,0:T(8,128)(2,1)S(1)}, u32[]{:S(2)}, u32[]{:S(2)}) collective-permute-start(bf16[512,128]{1,0:T(8,128)(2,1)S(1)} %bitcast.8), channel_id=1, source_target_pairs={{0,224},{32,0},{64,32},{96,64},{128,96},{160,128},{192,160},{224,1... | collective-permute-start | bytes 393224 | tf_op jit(solution)/shard_map/ppermute | solution.py:288
  106.6 10.0 %collective-permute-start.11 = (bf16[512,128]{1,0:T(8,128)(2,1)S(1)}, bf16[512,128]{1,0:T(8,128)(2,1)S(1)}, u32[]{:S(2)}, u32[]{:S(2)}) collective-permute-start(bf16[512,128]{1,0:T(8,128)(2,1)S(1)} %collective-permute-done.10.refs_3_), channel_id=1, source_target_pairs={{0,32},{32,64},{64,96},{96,128},{128,160},{160,192},{192,224},{224... | collective-permute-start | bytes 393224 | tf_op jit(solution)/shard_map/ppermute | solution.py:288
  106.6 10.0 %collective-permute-start.13 = (bf16[512,128]{1,0:T(8,128)(2,1)S(1)}, bf16[512,128]{1,0:T(8,128)(2,1)S(1)}, u32[]{:S(2)}, u32[]{:S(2)}) collective-permute-start(bf16[512,128]{1,0:T(8,128)(2,1)S(1)} %collective-permute-done.12.refs_4_), channel_id=1, source_target_pairs={{0,224},{32,0},{64,32},{96,64},{128,96},{160,128},{192,160},{224,1... | collective-permute-start | bytes 393224 | tf_op jit(solution)/shard_map/ppermute | solution.py:288
  109.3 5.8 %copy-start = (bf16[8,2,1024,512]{3,2,1,0:T(8,128)(2,1)S(1)}, bf16[8,2,1024,512]{3,2,1,0:T(8,128)(2,1)}, u32[]{:S(2)}) copy-start(bf16[8,2,1024,512]{3,2,1,0:T(8,128)(2,1)} %get-tuple-element.38.refs_1_) | copy-start | bytes 50331652
  116.6 5.1 %collective-permute-start.14 = (bf16[512,128]{1,0:T(8,128)(2,1)S(1)}, bf16[512,128]{1,0:T(8,128)(2,1)S(1)}, u32[]{:S(2)}, u32[]{:S(2)}) collective-permute-start(bf16[512,128]{1,0:T(8,128)(2,1)S(1)} %collective-permute-done.11.refs_2_), channel_id=1, source_target_pairs={{0,32},{32,64},{64,96},{96,128},{128,160},{160,192},{192,224},{224... | collective-permute-start | bytes 393224 | tf_op jit(solution)/shard_map/ppermute | solution.py:288
  116.7 5.0 %collective-permute-start.15 = (bf16[512,128]{1,0:T(8,128)(2,1)S(1)}, bf16[512,128]{1,0:T(8,128)(2,1)S(1)}, u32[]{:S(2)}, u32[]{:S(2)}) collective-permute-start(bf16[512,128]{1,0:T(8,128)(2,1)S(1)} %collective-permute-done.13.refs_3_), channel_id=1, source_target_pairs={{0,224},{32,0},{64,32},{96,64},{128,96},{160,128},{192,160},{224,1... | collective-permute-start | bytes 393224 | tf_op jit(solution)/shard_map/ppermute | solution.py:288
  120.0 6.7 %copy-start.2 = (f32[1024,128]{1,0:T(8,128)S(1)}, f32[1024,128]{1,0:T(8,128)}, u32[]{:S(2)}) copy-start(f32[1024,128]{1,0:T(8,128)} %get-tuple-element.47.refs_4_) | copy-start | bytes 1572868
  121.7 5.0 %collective-permute-start.16 = (bf16[512,128]{1,0:T(8,128)(2,1)S(1)}, bf16[512,128]{1,0:T(8,128)(2,1)S(1)}, u32[]{:S(2)}, u32[]{:S(2)}) collective-permute-start(bf16[512,128]{1,0:T(8,128)(2,1)S(1)} %collective-permute-done.14.refs_2_), channel_id=1, source_target_pairs={{0,32},{32,64},{64,96},{96,128},{128,160},{160,192},{192,224},{224... | collective-permute-start | bytes 393224 | tf_op jit(solution)/shard_map/ppermute | solution.py:288
  128.5 15.6 %all-to-all-start.3 = ((bf16[8,4,128,128]{3,2,1,0:T(8,128)(2,1)}), bf16[8,4,128,128]{3,2,1,0:T(8,128)(2,1)S(1)}, u32[]{:S(2)}, u32[]{:S(2)}) async-start(bf16[8,4,128,128]{3,2,1,0:T(8,128)(2,1)} %shard_map.81), calls=%async_computation.3 | async-start | bytes 2097152 | tf_op jit(solution)/shard_map/all_to_all | solution.py:284
  133.7 10.3 %copy-start.8 = (s32[3]{0:T(128)S(1)}, s32[3]{0:T(128)}, u32[]{:S(2)}) copy-start(s32[3]{0:T(128)} %copy-done.6) | copy-start | bytes 40
  144.0 2.8 %copy-start.1 = (bf16[8,768,512]{2,1,0:T(8,128)(2,1)S(1)}, bf16[8,768,512]{2,1,0:T(8,128)(2,1)}, u32[]{:S(2)}) copy-start(bf16[8,768,512]{2,1,0:T(8,128)(2,1)} %shard_map.82.rows) | copy-start | bytes 18874372
  150.0 11.7 %collective-permute-start.17 = (bf16[2,8,128,128]{3,2,1,0:T(8,128)(2,1)S(1)}, bf16[2,8,128,128]{3,2,1,0:T(8,128)(2,1)S(1)}, u32[]{:S(2)}, u32[]{:S(2)}) collective-permute-start(bf16[2,8,128,128]{3,2,1,0:T(8,128)(2,1)S(1)} %get-tuple-element.50), channel_id=1, source_target_pairs={{0,1},{1,0},{2,3},{3,2},{4,5},{5,4},{6,7},{7,6},{8,9},{9,8},{10,11... | collective-permute-start | bytes 1572872 | tf_op jit(solution)/shard_map/ppermute | solution.py:280
Sparse Core Ops, SparseCore 0:
  9.1 54.1 all-gather.4
  65.1 47.0 all-gather.6
